TPU v7x, 32 devices: a whole 2x2x4 slice. The times are simulated.
32 devices in a mesh: seq: 4 (over z), exp: 4 (over x, core), dp: 2 (over y).
Axes of the slice: x: 2, y: 2, z: 4, core: 2. Of those that a mesh axis runs over, the one named last changes fastest.
Arguments:
- queries: bfloat16 [768, 24, 128], P(('dp', 'seq'), 'exp'), parts along dimension 0, may hold values from -4.5 to 4.5
- keys: bfloat16 [768, 4, 128], P(('dp', 'seq'), 'exp'), parts along dimension 0, may hold values from -4.5 to 4.5
- values: bfloat16 [768, 4, 128], P(('dp', 'seq'), 'exp'), parts along dimension 0, may hold values from -16 to 16
- doc_ids: int32 [768], P('dp'), parts along dimension 0, may hold values from 0 to 2, never falling along the last dimension, each value on 1 to 320 neighbouring positions
- norm_gain: float32 [3072], replicated, may hold values from 0.1 to 1.9
- expert_ids: int32 [768, 2], P(('dp', 'seq', 'exp')), parts along dimension 0, may hold values from 0 to 3, all different within a row; in each aligned block of 24 rows (0 to 23, 24 to 47, ...) at most 12 rows name the same one
- route_weights: float32 [768, 2], P(('dp', 'seq', 'exp')), parts along dimension 0, may hold values from 0.2 to 1
- w_in: bfloat16 [4, 3072, 2048], P('exp', None, 'seq'), may hold values from -0.109375 to 0.109375
- w_out: bfloat16 [4, 2048, 3072], P('exp', 'seq'), may hold values from -0.125 to 0.125
Outputs:
- mixed: bfloat16 [768, 3072], P(('dp', 'seq', 'exp')), parts along dimension 0
There are 2 independent parts, one for each index of `dp`. A program takes and returns all parts, laid end to end along the dimension named above; an argument that names none is the same for every part. Nothing has to cross between parts.
Inputs may be any that keep to these rules, and one draw needn't show every extreme that they name: `doc_ids`: never falling along the sequence. `expert_ids`: within the 24 tokens of one device no expert is named by more than 12 tokens, and in every draw some expert of some device is named by exactly 12; the two experts of a token differ.
All inputs are finite; a program needn't handle non-finite values.
Results may differ from a plain program's by a relative error of at most 0.015.
Values may be sent and summed in bfloat16 or wider, within the bound.
No kernel may reach another device: no remote copies, remote signals or barrier semaphores. Data moves between devices by JAX's collectives and lax.ppermute only.
A program may use at most 128 MiB of HBM per device.

v0:
```python
import jax
import jax.numpy as jnp
from jax import lax
from jax.sharding import PartitionSpec as P

WINDOW = 2048


epsilon = 1e-05


def shifted(x, axis, by):
    size = lax.axis_size(axis)
    pairs = [(i, i + by) for i in range(size) if 0 <= i + by < size]
    return lax.ppermute(x, axis, pairs)


def shards(queries, keys, values, doc_ids, norm_gain, expert_ids, route_weights, w_in, w_out):
    block_len, heads_dev, head_dim = queries.shape
    seq_count = lax.axis_size("seq")
    exp_count = lax.axis_size("exp")
    seq_index = lax.axis_index("seq")
    reach_blocks = min(-(-WINDOW // block_len), seq_count - 1)
    own_keys = keys[:, 0, :]
    own_values = values[:, 0, :]
    key_list = [own_keys]
    value_list = [own_values]
    for distance in range(1, reach_blocks + 1):
        far_keys, far_values = shifted((own_keys, own_values), "seq", distance)
        key_list.insert(0, far_keys)
        value_list.insert(0, far_values)
    near_keys = jnp.concatenate(key_list, axis=0)
    near_values = jnp.concatenate(value_list, axis=0)
    key_count = near_keys.shape[0]
    query_rows = jnp.transpose(queries, (1, 0, 2)).reshape(heads_dev * block_len, head_dim)
    score = lax.dot_general(
        query_rows, near_keys, (((1,), (1,)), ((), ())), preferred_element_type=jnp.float32
    )
    score = score * (1.0 / head_dim**0.5)
    query_pos = seq_index * block_len + jnp.arange(block_len, dtype=jnp.int32)
    key_pos = (seq_index - reach_blocks) * block_len + jnp.arange(key_count, dtype=jnp.int32)
    padded_docs = jnp.concatenate(
        [jnp.full((reach_blocks * block_len,), -1, jnp.int32), doc_ids], axis=0
    )
    key_docs = lax.dynamic_slice_in_dim(padded_docs, seq_index * block_len, key_count, 0)
    query_docs = lax.dynamic_slice_in_dim(doc_ids, seq_index * block_len, block_len, 0)
    allowed = (key_pos[None, :] <= query_pos[:, None]) & (
        query_pos[:, None] - key_pos[None, :] < WINDOW
    )
    allowed = allowed & (key_pos[None, :] >= 0) & (query_docs[:, None] == key_docs[None, :])
    allowed = jnp.tile(allowed, (heads_dev, 1))
    score = jnp.where(allowed, score, -jnp.inf)
    top_score = jnp.max(score, axis=1, keepdims=True)
    weights = jnp.where(allowed, jnp.exp(score - top_score), 0.0)
    probs = (weights / jnp.sum(weights, axis=1, keepdims=True)).astype(jnp.bfloat16)
    attended = jnp.dot(probs, near_values, preferred_element_type=jnp.float32).astype(jnp.bfloat16)
    attended = jnp.transpose(attended.reshape(heads_dev, block_len, head_dim), (1, 0, 2)).reshape(
        block_len, heads_dev * head_dim
    )
    attn = lax.all_to_all(attended, "exp", split_axis=0, concat_axis=1, tiled=True)
    token_count = attn.shape[0]
    width = attn.shape[1]
    attn_float = attn.astype(jnp.float32)
    mean_square = jnp.mean(attn_float * attn_float, axis=1, keepdims=True)
    normed = (attn_float * lax.rsqrt(mean_square + epsilon) * norm_gain[None, :]).astype(
        jnp.bfloat16
    )
    capacity = max((token_count + 2) // 3, 2 * token_count // exp_count)
    flat_ids = expert_ids.reshape(token_count * 2)
    onehot = (flat_ids[:, None] == jnp.arange(exp_count, dtype=jnp.int32)[None, :]).astype(
        jnp.int32
    )
    earlier = jnp.cumsum(onehot, axis=0) - onehot
    slot = jnp.sum(earlier * onehot, axis=1)
    local_code = (flat_ids * capacity + slot).reshape(token_count, 2)
    slot_range = jnp.arange(exp_count * capacity, dtype=jnp.int32)
    first_hit = local_code[:, 0:1] == slot_range[None, :]
    second_hit = local_code[:, 1:2] == slot_range[None, :]
    placing = jnp.transpose((first_hit | second_hit).astype(jnp.bfloat16))
    outgoing = jnp.dot(placing, normed, preferred_element_type=jnp.float32).astype(jnp.bfloat16)
    arrived = lax.all_to_all(
        outgoing.reshape(exp_count, capacity, width), "exp", split_axis=0, concat_axis=0, tiled=True
    )
    row_count = exp_count * capacity
    arrived = arrived.reshape(row_count, width)
    weight_in = w_in[0]
    weight_out = w_out[0]
    hidden = jax.nn.silu(
        jnp.dot(
            lax.all_gather(arrived, "seq", axis=0, tiled=True),
            weight_in,
            preferred_element_type=jnp.float32,
        )
    ).astype(jnp.bfloat16)
    summed = lax.psum_scatter(
        jnp.dot(hidden, weight_out, preferred_element_type=jnp.float32).astype(jnp.bfloat16),
        "seq",
        scatter_dimension=0,
        tiled=True,
    )
    expert_out = summed.reshape(exp_count, capacity, width)
    returned = lax.all_to_all(expert_out, "exp", split_axis=0, concat_axis=0, tiled=True).reshape(
        row_count, width
    )
    combine = route_weights[:, 0:1] * first_hit.astype(jnp.float32) + route_weights[
        :, 1:2
    ] * second_hit.astype(jnp.float32)
    moe_part = jnp.dot(
        combine,
        returned.astype(jnp.float32),
        precision=lax.Precision.HIGHEST,
        preferred_element_type=jnp.float32,
    )
    return (attn_float + moe_part).astype(jnp.bfloat16)


def solution(mesh):
    placed = (
        P(("dp", "seq"), "exp", None),
        P(("dp", "seq"), "exp", None),
        P(("dp", "seq"), "exp", None),
        P("dp"),
        P(),
        P(("dp", "seq", "exp"), None),
        P(("dp", "seq", "exp"), None),
        P("exp", None, "seq"),
        P("exp", "seq", None),
    )
    return jax.shard_map(
        shards, mesh=mesh, in_specs=placed, out_specs=P(("dp", "seq", "exp"), None), check_vma=False
    )
```

profile of v0, /device:TPU:0, one launch (start us, length us, event | category | flops | bytes accessed | tf_op | source)
XLA Modules:
  0.0 141.2 jit_solution(12314320888660095931)
XLA Ops:
  6.5 7.2 %collective-permute-start = (bf16[96,128]{1,0:T(8,128)(2,1)}, bf16[96,128]{1,0:T(8,128)(2,1)S(1)}, u32[]{:S(2)}, u32[]{:S(2)}) collective-permute-start(bf16[96,128]{1,0:T(8,128)(2,1)} %bitcast.48), channel_id=1, source_target_pairs={{0,24},{1,25},{2,26},{3,27},{4,28},{5,29},{6,30},{7,31}} | collective-permute-start | bytes 73736 | tf_op jit(solution)/shard_map/ppermute | solution.py:15
  13.8 1.3 collective-permute-start.1
  15.1 2.5 %collective-permute-start.2 = (bf16[96,128]{1,0:T(8,128)(2,1)}, bf16[96,128]{1,0:T(8,128)(2,1)S(1)}, u32[]{:S(2)}, u32[]{:S(2)}) collective-permute-start(bf16[96,128]{1,0:T(8,128)(2,1)} %bitcast.50), channel_id=1, source_target_pairs={{0,8},{8,16},{16,24},{1,9},{9,17},{17,25},{2,10},{10,18},{18,26},{... | collective-permute-start | bytes 73736 | tf_op jit(solution)/shard_map/ppermute | solution.py:15
  17.5 1.3 collective-permute-start.3
  18.8 1.3 collective-permute-start.4
  20.2 0.8 pad_dynamic-slice_fusion
  23.9 1.3 collective-permute-start.5
  25.3 1.3 fusion.49
  27.7 0.8 all_to_all.16
  28.5 3.3 %all-to-all-start = ((bf16[4,24,768]{2,1,0:T(8,128)(2,1)}), bf16[4,24,768]{2,1,0:T(8,128)(2,1)S(1)}, u32[]{:S(2)}, u32[]{:S(2)}) async-start(bf16[4,24,768]{2,1,0:T(8,128)(2,1)} %all_to_all.16), calls=%async_computation | async-start | bytes 294912 | tf_op jit(solution)/shard_map/all_to_all | solution.py:60
  31.9 4.7 %all-to-all-done = bf16[4,24,768]{2,1,0:T(8,128)(2,1)S(1)} async-done(((bf16[4,24,768]{2,1,0:T(8,128)(2,1)}), bf16[4,24,768]{2,1,0:T(8,128)(2,1)S(1)}, u32[]{:S(2)}, u32[]{:S(2)}) %all-to-all-start) | async-done | bytes 147488 | tf_op jit(solution)/shard_map/all_to_all | solution.py:60
  37.3 1.1 fusion.11
  38.4 1.1 convolution_convert_fusion.1
  39.5 1.8 %reshape.153 = bf16[4,12,3072]{2,1,0:T(8,128)(2,1)} reshape(bf16[48,3072]{1,0:T(8,128)(2,1)} %convolution_convert_fusion.1) | data formatting | bytes 589824 | tf_op jit(solution)/shard_map/reshape | solution.py:82
  41.2 11.6 %all_to_all.23 = bf16[4,12,3072]{2,1,0:T(8,128)(2,1)} all-to-all(bf16[4,12,3072]{2,1,0:T(8,128)(2,1)} %reshape.153), channel_id=1, replica_groups=mesh['seq'=4,'exp'=4,'dp'=2] {'exp'}, dimensions={0} | all-to-all | bytes 589824 | tf_op jit(solution)/shard_map/all_to_all | solution.py:81
  52.9 1.8 %reshape.154 = bf16[48,3072]{1,0:T(8,128)(2,1)} reshape(bf16[4,12,3072]{2,1,0:T(8,128)(2,1)} %all_to_all.23) | data formatting | bytes 589824 | tf_op jit(solution)/shard_map/reshape | solution.py:85
  54.7 29.2 %all-gather.2.cloned.1.call-done = bf16[192,3072]{1,0:T(8,128)(2,1)} async-done(((bf16[48,3072]{1,0:T(8,128)(2,1)}), bf16[192,3072]{1,0:T(8,128)(2,1)}) %all-gather.2.cloned.1.call-update) | async-done | bytes 1179664 | tf_op jit(solution)/shard_map/all_gather | solution.py:90
  83.9 4.8 %convolution_convert_fusion = bf16[192,3072]{1,0:T(8,128)(2,1)} fusion(bf16[1,512,3072]{2,1,0:T(8,128)(2,1)S(1)} %copy-done, bf16[192,3072]{1,0:T(8,128)(2,1)} %all-gather.2.cloned.1.call-done, bf16[1,3072,512]{2,1,0:T(8,128)(2,1)} %param.16), kind=kOutput, calls=%fused_computation | convolution fusion | flops 1209040896 | bytes 8650752 | tf_op jit(solution)/shard_map/dot_general | solution.py:96
  88.8 28.4 %reduce-scatter.2.cloned.1.call-done = bf16[48,3072]{1,0:T(8,128)(2,1)} async-done(((bf16[192,3072]{1,0:T(8,128)(2,1)}), bf16[48,3072]{1,0:T(8,128)(2,1)}) %reduce-scatter.2.cloned.1.call-update) | async-done | bytes 294928 | tf_op jit(solution)/shard_map/reduce_scatter | solution.py:95
  117.2 1.8 %reshape.155 = bf16[4,12,3072]{2,1,0:T(8,128)(2,1)} reshape(bf16[48,3072]{1,0:T(8,128)(2,1)} %reduce-scatter.2.cloned.1.call-done) | data formatting | bytes 589824 | tf_op jit(solution)/shard_map/reshape | solution.py:101
  119.0 4.1 %all-to-all-start.2 = ((bf16[4,12,3072]{2,1,0:T(8,128)(2,1)}), bf16[4,12,3072]{2,1,0:T(8,128)(2,1)}, u32[]{:S(2)}, u32[]{:S(2)}) async-start(bf16[4,12,3072]{2,1,0:T(8,128)(2,1)} %reshape.155), calls=%async_computation.3 | async-start | bytes 786432 | tf_op jit(solution)/shard_map/all_to_all | solution.py:102
  123.1 7.5 %all-to-all-done.2 = bf16[4,12,3072]{2,1,0:T(8,128)(2,1)} async-done(((bf16[4,12,3072]{2,1,0:T(8,128)(2,1)}), bf16[4,12,3072]{2,1,0:T(8,128)(2,1)}, u32[]{:S(2)}, u32[]{:S(2)}) %all-to-all-start.2) | async-done | bytes 294944 | tf_op jit(solution)/shard_map/all_to_all | solution.py:102
  130.6 1.8 %reshape.156 = bf16[48,3072]{1,0:T(8,128)(2,1)} reshape(bf16[4,12,3072]{2,1,0:T(8,128)(2,1)} %all-to-all-done.2) | data formatting | bytes 589824 | tf_op jit(solution)/shard_map/reshape | solution.py:102
  132.4 2.0 %fusion = bf16[24,3072]{1,0:T(8,128)(2,1)} fusion(f32[24,3072]{1,0:T(8,128)S(1)} %bitcast.42, bf16[48,3072]{1,0:T(8,128)(2,1)} %reshape.156, f32[24]{0:T(128)S(1)} %get-tuple-element.6, s32[24]{0:T(128)S(1)} %get-tuple-element.8, f32[24]{0:T(128)S(1)} %get-tuple-element.5, s32[24]{0:T(128)S(1)} %get-tuple-element.7), kind=kOutput, calls=%fused_computation.3 | convolution fusion | flops 42620544 | bytes 737664 | tf_op jit(solution)/shard_map/dot_general | solution.py:108
  (42 shorter events, 4.9 us)
Async XLA Ops:
  6.5 77.4 %copy-start = (bf16[1,512,3072]{2,1,0:T(8,128)(2,1)S(1)}, bf16[1,512,3072]{2,1,0:T(8,128)(2,1)}, u32[]{:S(2)}) copy-start(bf16[1,512,3072]{2,1,0:T(8,128)(2,1)} %param.17) | copy-start | bytes 9437188
  6.5 20.8 %copy-start.4 = (bf16[96,1,128]{2,0,1:T(8,128)(2,1)S(1)}, bf16[96,1,128]{2,0,1:T(8,128)(2,1)}, u32[]{:S(2)}) copy-start(bf16[96,1,128]{2,0,1:T(8,128)(2,1)} %param.11) | copy-start | bytes 73732
  6.5 17.4 %collective-permute-start = (bf16[96,128]{1,0:T(8,128)(2,1)}, bf16[96,128]{1,0:T(8,128)(2,1)S(1)}, u32[]{:S(2)}, u32[]{:S(2)}) collective-permute-start(bf16[96,128]{1,0:T(8,128)(2,1)} %bitcast.48), channel_id=1, source_target_pairs={{0,24},{1,25},{2,26},{3,27},{4,28},{5,29},{6,30},{7,31}} | collective-permute-start | bytes 73736 | tf_op jit(solution)/shard_map/ppermute | solution.py:15
  13.8 11.4 %collective-permute-start.1 = (bf16[96,128]{1,0:T(8,128)(2,1)}, bf16[96,128]{1,0:T(8,128)(2,1)S(1)}, u32[]{:S(2)}, u32[]{:S(2)}) collective-permute-start(bf16[96,128]{1,0:T(8,128)(2,1)} %bitcast.49), channel_id=1, source_target_pairs={{0,16},{8,24},{1,17},{9,25},{2,18},{10,26},{3,19},{11,27},{4,20},{... | collective-permute-start | bytes 73736 | tf_op jit(solution)/shard_map/ppermute | solution.py:15
  15.1 10.1 %collective-permute-start.2 = (bf16[96,128]{1,0:T(8,128)(2,1)}, bf16[96,128]{1,0:T(8,128)(2,1)S(1)}, u32[]{:S(2)}, u32[]{:S(2)}) collective-permute-start(bf16[96,128]{1,0:T(8,128)(2,1)} %bitcast.50), channel_id=1, source_target_pairs={{0,8},{8,16},{16,24},{1,9},{9,17},{17,25},{2,10},{10,18},{18,26},{... | collective-permute-start | bytes 73736 | tf_op jit(solution)/shard_map/ppermute | solution.py:15
  17.5 9.7 %collective-permute-start.3 = (bf16[96,128]{1,0:T(8,128)(2,1)}, bf16[96,128]{1,0:T(8,128)(2,1)S(1)}, u32[]{:S(2)}, u32[]{:S(2)}) collective-permute-start(bf16[96,128]{1,0:T(8,128)(2,1)} %bitcast.52), channel_id=1, source_target_pairs={{0,24},{1,25},{2,26},{3,27},{4,28},{5,29},{6,30},{7,31}} | collective-permute-start | bytes 73736 | tf_op jit(solution)/shard_map/ppermute | solution.py:15
  18.8 8.4 %collective-permute-start.4 = (bf16[96,128]{1,0:T(8,128)(2,1)}, bf16[96,128]{1,0:T(8,128)(2,1)S(1)}, u32[]{:S(2)}, u32[]{:S(2)}) collective-permute-start(bf16[96,128]{1,0:T(8,128)(2,1)} %bitcast.53), channel_id=1, source_target_pairs={{0,16},{8,24},{1,17},{9,25},{2,18},{10,26},{3,19},{11,27},{4,20},{... | collective-permute-start | bytes 73736 | tf_op jit(solution)/shard_map/ppermute | solution.py:15
  23.9 3.4 %collective-permute-start.5 = (bf16[96,128]{1,0:T(8,128)(2,1)}, bf16[96,128]{1,0:T(8,128)(2,1)S(1)}, u32[]{:S(2)}, u32[]{:S(2)}) collective-permute-start(bf16[96,128]{1,0:T(8,128)(2,1)} %bitcast.54), channel_id=1, source_target_pairs={{0,8},{8,16},{16,24},{1,9},{9,17},{17,25},{2,10},{10,18},{18,26},{... | collective-permute-start | bytes 73736 | tf_op jit(solution)/shard_map/ppermute | solution.py:15
  25.3 13.1 %copy-start.2 = (f32[3072]{0:T(1024)S(1)}, f32[3072]{0:T(1024)}, u32[]{:S(2)}) copy-start(f32[3072]{0:T(1024)} %param.13) | copy-start | bytes 36868
  28.5 8.1 %all-to-all-start = ((bf16[4,24,768]{2,1,0:T(8,128)(2,1)}), bf16[4,24,768]{2,1,0:T(8,128)(2,1)S(1)}, u32[]{:S(2)}, u32[]{:S(2)}) async-start(bf16[4,24,768]{2,1,0:T(8,128)(2,1)} %all_to_all.16), calls=%async_computation | async-start | bytes 294912 | tf_op jit(solution)/shard_map/all_to_all | solution.py:60
  31.9 52.0 %all-gather.2.cloned.1.call-start = ((), (), s32[]{:S(2)}) async-start(), calls=%async_computation.4 | async-start | bytes 1474560 | tf_op jit(solution)/shard_map/all_gather | solution.py:90
  36.6 0.7 copy-start.1
  54.7 68.4 %copy-start.3 = (f32[24,2]{0,1:T(2,128)S(1)}, f32[24,2]{0,1:T(2,128)}, u32[]{:S(2)}) copy-start(f32[24,2]{0,1:T(2,128)} %param.15) | copy-start | bytes 580
  54.7 62.5 %reduce-scatter.2.cloned.1.call-start = ((), (), s32[]{:S(2)}) async-start(), calls=%async_computation.5 | async-start | bytes 1474560 | tf_op jit(solution)/shard_map/reduce_scatter | solution.py:95
  119.0 11.6 %all-to-all-start.2 = ((bf16[4,12,3072]{2,1,0:T(8,128)(2,1)}), bf16[4,12,3072]{2,1,0:T(8,128)(2,1)}, u32[]{:S(2)}, u32[]{:S(2)}) async-start(bf16[4,12,3072]{2,1,0:T(8,128)(2,1)} %reshape.155), calls=%async_computation.3 | async-start | bytes 786432 | tf_op jit(solution)/shard_map/all_to_all | solution.py:102
Sparse Core Ops, SparseCore 0:
  54.8 29.0 all-gather.1
  88.9 28.2 reduce-scatter.1
where the time goes:
time: 142 us; the launch traced here: 141 us
  waiting for transfers between devices  69.8 us (49%)
  starting transfers between devices  22.4 us (16%)
  between operations  13.7 us (10%)
  blocking collectives  11.6 us (8%)
  local copies, waits for them, and re-layouts  10.6 us (7%)
  matrix products  9.44 us (7%)
  other arithmetic  3.65 us (3%)
    all_gather x1, waiting for transfers between devices, shards(): lax.all_gather(arrived, 'seq', axis=0, tiled=True)  29.2 us
    reduce_scatter x1, waiting for transfers between devices, shards(): lax.psum_scatter(jnp.dot(hidden, weight_out, preferred_element_type=jnp.f...  28.4 us
    ppermute x6, starting transfers between devices, shifted(): return lax.ppermute(x, axis, pairs)  14.8 us
    all_to_all x1, blocking collectives, shards(): lax.all_to_all(outgoing.reshape(exp_count, capacity, width), 'exp', split...  11.6 us
    all_to_all x1, waiting for transfers between devices, shards(): lax.all_to_all(expert_out, 'exp', split_axis=0, concat_axis=0, tiled=True)  7.48 us
    dot_general x1, matrix products, shards(): jnp.dot(hidden, weight_out, preferred_element_type=jnp.float32)  4.83 us
    all_to_all x1, waiting for transfers between devices, shards(): lax.all_to_all(attended, 'exp', split_axis=0, concat_axis=1, tiled=True)  4.71 us
    all_to_all x1, starting transfers between devices, shards(): lax.all_to_all(expert_out, 'exp', split_axis=0, concat_axis=0, tiled=True)  4.11 us
  transfers between devices with their start and end apart: 10, of which 4 were waited for; matrix products, arithmetic and copies ran while one was open for 4% of the time, Pallas kernels for 0%

commit v1 on v0

--- a/solution.py
+++ b/solution.py
@@ -1,6 +1,10 @@
+import functools
+
 import jax
 import jax.numpy as jnp
 from jax import lax
+from jax.experimental import pallas as pl
+from jax.experimental.pallas import tpu as pltpu
 from jax.sharding import PartitionSpec as P
 
 WINDOW = 2048
@@ -15,7 +19,13 @@
     return lax.ppermute(x, axis, pairs)
 
 
-def shards(queries, keys, values, doc_ids, norm_gain, expert_ids, route_weights, w_in, w_out):
+def flipped(x, axis, by):
+    return lax.ppermute(x, axis, [(i, i ^ by) for i in range(lax.axis_size(axis))])
+
+
+def routed_shards(
+    queries, keys, values, doc_ids, norm_gain, expert_ids, route_weights, w_in, w_out
+):
     block_len, heads_dev, head_dim = queries.shape
     seq_count = lax.axis_size("seq")
     exp_count = lax.axis_size("exp")
@@ -114,6 +124,196 @@
     return (attn_float + moe_part).astype(jnp.bfloat16)
 
 
+def attend_kernel(block_len, scale, *refs):
+    count = len(refs) - 6
+    query_ref, packs = refs[0], refs[1 : 1 + count]
+    query_info, key_info, out_ref, keys_ref, values_ref = refs[1 + count :]
+    for i, pack in enumerate(packs):
+        rows = slice(i * block_len, (i + 1) * block_len)
+        keys_ref[rows] = pack[0:block_len]
+        values_ref[rows] = pack[block_len : 2 * block_len]
+    query_pos, query_doc = query_info[:, 0:1], query_info[:, 1:2]
+    key_pos, key_doc = key_info[0:1, :], key_info[1:2, :]
+    allowed = (key_pos <= query_pos) & (query_pos - key_pos < WINDOW) & (query_doc == key_doc)
+    head_dim = query_ref.shape[2]
+    for head in range(query_ref.shape[0]):
+        score = lax.dot_general(
+            query_ref[head],
+            keys_ref[...],
+            (((1,), (1,)), ((), ())),
+            preferred_element_type=jnp.float32,
+        )
+        score = jnp.where(allowed, score * scale, -jnp.inf)
+        weights = jnp.exp(score - jnp.max(score, axis=1, keepdims=True))
+        probs = weights * (1.0 / jnp.sum(weights, axis=1, keepdims=True))
+        out_ref[:, head * head_dim : (head + 1) * head_dim] = jnp.dot(
+            probs.astype(jnp.bfloat16), values_ref[...], preferred_element_type=jnp.float32
+        ).astype(jnp.bfloat16)
+
+
+def experts_kernel(seq_count, exp_count, order, *refs):
+    place_ref, weight_ref, gain_ref, w_in_ref, w_out_ref = refs[:5]
+    blocks = refs[5 : 5 + seq_count * exp_count]
+    outs = refs[5 + seq_count * exp_count : -2]
+    kept, sent, own_ref = outs[:seq_count], outs[seq_count : 2 * seq_count], outs[-1]
+    hidden_ref, split_ref = refs[-2:]
+    place = place_ref[0]
+    block_len, part_width = blocks[0].shape
+    token_count = block_len // exp_count
+    width = part_width * exp_count
+    inverse = []
+    for d in range(seq_count):
+        total = jnp.zeros((block_len, 1), jnp.float32)
+        for j in range(exp_count):
+            value = blocks[d * exp_count + j][...].astype(jnp.float32)
+            total = total + jnp.sum(value * value, axis=1, keepdims=True)
+        inverse.append(lax.rsqrt(total * (1.0 / width) + epsilon))
+    hidden = None
+    for j in range(exp_count):
+        source = place ^ j
+        gain = gain_ref[source]
+        normed = []
+        for d in range(seq_count):
+            value = blocks[d * exp_count + j][...].astype(jnp.float32)
+            normed.append((value * inverse[d] * gain).astype(jnp.bfloat16))
+            if d == 0:
+                split_ref[...] = value.reshape(exp_count, token_count, part_width)
+                own_ref[source] = split_ref[place].astype(jnp.bfloat16)
+        rows = pl.ds(pl.multiple_of(source * part_width, part_width), part_width)
+        product = jnp.dot(
+            jnp.concatenate(normed, axis=0), w_in_ref[rows, :], preferred_element_type=jnp.float32
+        )
+        hidden = product if hidden is None else hidden + product
+    hidden = hidden * (1.0 / (1.0 + jnp.exp(-hidden)))
+    hidden_ref[...] = hidden.reshape(seq_count * exp_count, token_count, hidden.shape[1])
+    hidden = jnp.concatenate(
+        [hidden_ref[d * exp_count + (place ^ j)] for d in range(seq_count) for j in order], axis=0
+    ).astype(jnp.bfloat16)
+    half = block_len // 2
+    tile = part_width
+    weight = weight_ref[...]
+    for start in range(0, width, tile):
+        columns = slice(start, start + tile)
+        product = jnp.dot(hidden, w_out_ref[:, columns], preferred_element_type=jnp.float32)
+        product = (product * weight).astype(jnp.bfloat16)
+        for d in range(seq_count):
+            low = d * block_len
+            kept[d][:, columns] = product[low : low + half]
+            sent[d][:, columns] = product[low + half : low + block_len]
+
+
+def vmem():
+    return pl.BlockSpec(memory_space=pltpu.VMEM)
+
+
+def gathered_shards(
+    queries, keys, values, doc_ids, norm_gain, expert_ids, route_weights, w_in, w_out
+):
+    block_len, heads_dev, head_dim = queries.shape
+    seq_count = lax.axis_size("seq")
+    exp_count = lax.axis_size("exp")
+    seq_index = lax.axis_index("seq")
+    exp_index = lax.axis_index("exp")
+    token_count = expert_ids.shape[0]
+    part_width = heads_dev * head_dim
+    width = part_width * exp_count
+    hidden_width = w_in.shape[2]
+    half = block_len // 2
+    far = range(1, seq_count)
+
+    named = expert_ids[:, :, None] == jnp.arange(exp_count, dtype=jnp.int32)[None, None, :]
+    dense = jnp.sum(jnp.where(named, route_weights[:, :, None], 0.0), axis=1).T
+    pieces = []
+    for _ in range(3):
+        piece = lax.reduce_precision(dense, 8, 7)
+        pieces.append(piece.astype(jnp.bfloat16))
+        dense = dense - piece
+    pieces = jnp.concatenate(pieces, axis=0)
+    pieces = jnp.pad(pieces, ((0, 16 - 3 * exp_count), (0, head_dim - token_count)))
+
+    pack = jnp.concatenate([keys[:, 0, :], values[:, 0, :], pieces], axis=0)
+    packs = [pack] + [flipped(pack, "seq", d) for d in far]
+
+    blocks_docs = doc_ids.reshape(seq_count, block_len)
+    block_of = seq_index ^ jnp.arange(seq_count, dtype=jnp.int32)
+    offsets = jnp.arange(block_len, dtype=jnp.int32)
+    key_pos = (block_of[:, None] * block_len + offsets[None, :]).reshape(-1)
+    key_docs = jnp.concatenate(
+        [lax.dynamic_slice_in_dim(doc_ids, (seq_index ^ d) * block_len, block_len, 0) for d in range(seq_count)]
+    )
+    key_info = jnp.stack([key_pos, key_docs])
+    query_info = jnp.stack([key_pos[:block_len], key_docs[:block_len]], axis=1)
+    attended = pl.pallas_call(
+        functools.partial(attend_kernel, block_len, 1.0 / head_dim**0.5),
+        out_shape=jax.ShapeDtypeStruct((block_len, part_width), jnp.bfloat16),
+        in_specs=[vmem()] * (seq_count + 3),
+        out_specs=vmem(),
+        scratch_shapes=[pltpu.VMEM((seq_count * block_len, head_dim), jnp.bfloat16)] * 2,
+        cost_estimate=pl.CostEstimate(
+            flops=4 * heads_dev * block_len * seq_count * block_len * head_dim,
+            bytes_accessed=1 << 20,
+            transcendentals=heads_dev * block_len * seq_count * block_len,
+        ),
+        name="attend",
+    )(jnp.transpose(queries, (1, 0, 2)), *packs, query_info, key_info)
+
+    blocks = {(d, 0): attended if d == 0 else flipped(attended, "seq", d) for d in range(seq_count)}
+    shares = {0: jnp.stack([p[2 * block_len :] for p in packs])}
+    bit = exp_count // 2
+    while bit:
+        blocks |= {(d, j ^ bit): flipped(block, "exp", bit) for (d, j), block in blocks.items()}
+        held = sorted(shares)
+        arrived = flipped(jnp.stack([shares[j] for j in held]), "exp", bit)
+        shares |= {j ^ bit: arrived[i] for i, j in enumerate(held)}
+        bit //= 2
+
+    order = [j for j in range(exp_count) if not j & 1] + [j for j in range(exp_count) if j & 1]
+    share = jnp.stack([shares[j] for j in order], axis=1)
+    share = share.reshape(seq_count * exp_count, 16, head_dim)
+    share = share[:, : 3 * exp_count, :token_count].reshape(-1, 3, exp_count, token_count)
+    mine = jnp.arange(exp_count, dtype=jnp.int32) == exp_index
+    weight = jnp.sum(
+        jnp.where(mine[None, None, :, None], share.astype(jnp.float32), 0.0), axis=(1, 2)
+    ).reshape(-1, 1)
+
+    *returned, own = pl.pallas_call(
+        functools.partial(experts_kernel, seq_count, exp_count, order),
+        out_shape=[jax.ShapeDtypeStruct((half, width), jnp.bfloat16)] * (2 * seq_count)
+        + [jax.ShapeDtypeStruct((exp_count, token_count, part_width), jnp.bfloat16)],
+        in_specs=[pl.BlockSpec(memory_space=pltpu.SMEM)] + [vmem()] * (4 + seq_count * exp_count),
+        out_specs=[vmem()] * (2 * seq_count + 1),
+        scratch_shapes=[
+            pltpu.VMEM((seq_count * exp_count, token_count, hidden_width), jnp.float32),
+            pltpu.VMEM((exp_count, token_count, part_width), jnp.float32),
+        ],
+        compiler_params=pltpu.CompilerParams(vmem_limit_bytes=48 << 20),
+        cost_estimate=pl.CostEstimate(
+            flops=4 * seq_count * block_len * width * hidden_width,
+            bytes_accessed=16 << 20,
+            transcendentals=seq_count * block_len * hidden_width,
+        ),
+        name="experts",
+    )(
+        exp_index.reshape(1),
+        weight,
+        norm_gain.reshape(exp_count, 1, part_width),
+        w_in[0],
+        w_out[0],
+        *[blocks[d, j] for d in range(seq_count) for j in range(exp_count)],
+    )
+
+    kept, sent = returned[:seq_count], returned[seq_count:]
+    total = jnp.transpose(own, (1, 0, 2)).reshape(token_count, width).astype(jnp.float32)
+    for d in reversed(range(seq_count)):
+        both = kept[d].astype(jnp.float32) + flipped(sent[d], "exp", 1).astype(jnp.float32)
+        away = flipped(both[token_count:].astype(jnp.bfloat16), "exp", 2)
+        mine = both[:token_count] + away.astype(jnp.float32)
+        if d:
+            mine = flipped(mine.astype(jnp.bfloat16), "seq", d).astype(jnp.float32)
+        total = total + mine
+    return total.astype(jnp.bfloat16)
+
+
 def solution(mesh):
     placed = (
         P(("dp", "seq"), "exp", None),
@@ -126,6 +326,11 @@
         P("exp", None, "seq"),
         P("exp", "seq", None),
     )
+    small = mesh.shape["seq"] == 4 and mesh.shape["exp"] == 4
     return jax.shard_map(
-        shards, mesh=mesh, in_specs=placed, out_specs=P(("dp", "seq", "exp"), None), check_vma=False
-    )
+        gathered_shards if small else routed_shards,
+        mesh=mesh,
+        in_specs=placed,
+        out_specs=P(("dp", "seq", "exp"), None),
+        check_vma=False,
+    )

time: 142 us -> 79 us (0.56)
  waiting for transfers between devices: 69.8 us -> 33.9 us
  between operations: 13.7 us -> 0.23 us
  blocking collectives: 11.6 us -> 0 us
  Pallas kernels: 0 us -> 10.1 us
  matrix products: 9.44 us -> 0 us
  local copies, waits for them, and re-layouts: 10.6 us -> 3.65 us
  starting transfers between devices: 22.4 us -> 27.2 us
    ppermute x6 -> x31, waiting for transfers between devices: 0.02 us -> 33.9 us  [flipped(): lax.ppermute(x, axis, [(i, i ^ by) for i in range(lax.axis_size(axis))])]
    all_gather x1 -> x0, waiting for transfers between devices: 29.2 us -> none  [shards(): lax.all_gather(arrived, 'seq', axis=0, tiled=True)]
    reduce_scatter x1 -> x0, waiting for transfers between devices: 28.4 us -> none  [shards(): lax.psum_scatter(jnp.dot(hidden, weight_out, preferred_element_type=jnp.f...]
    ppermute x6 -> x31, starting transfers between devices: 14.8 us -> 27.2 us  [flipped(): lax.ppermute(x, axis, [(i, i ^ by) for i in range(lax.axis_size(axis))])]
    all_to_all x2 -> x0, waiting for transfers between devices: 12.2 us -> none  [the longest x1 7.48 us: shards(): lax.all_to_all(expert_out, 'exp', split_axis=0, concat_axis=0, tiled=True)]
    all_to_all x1 -> x0, blocking collectives: 11.6 us -> none  [shards(): lax.all_to_all(outgoing.reshape(exp_count, capacity, width), 'exp', split...]
    pallas_call x0 -> x2, Pallas kernels: none -> 10.1 us  [the longest x1 6.27 us: gathered_shards(): pl.pallas_call(functools.partial(experts_kernel, seq_count, exp_count, or...]
    dot_general x5 -> x0, matrix products: 9.44 us -> none  [the longest x1 4.83 us: shards(): jnp.dot(hidden, weight_out, preferred_element_type=jnp.float32)]
  transfers between devices with their start and end apart: 10 -> 31, of which waited for: 4 -> 15; matrix products, arithmetic and copies ran while one was open for 4% -> 4% of each run, Pallas kernels for 0% -> 5%
where the time goes in v1:
time: 79 us; the launch traced here: 78.7 us
  waiting for transfers between devices  33.9 us (43%)
  starting transfers between devices  27.2 us (34%)
  Pallas kernels  10.1 us (13%)
  local copies, waits for them, and re-layouts  3.65 us (5%)
  other arithmetic  3.54 us (4%)
    ppermute x31, waiting for transfers between devices, flipped(): lax.ppermute(x, axis, [(i, i ^ by) for i in range(lax.axis_size(axis))])  33.9 us
    ppermute x31, starting transfers between devices, flipped(): lax.ppermute(x, axis, [(i, i ^ by) for i in range(lax.axis_size(axis))])  27.2 us
    pallas_call x1, Pallas kernels, gathered_shards(): pl.pallas_call(functools.partial(experts_kernel, seq_count, exp_count, or...  6.27 us
    pallas_call x1, Pallas kernels, gathered_shards(): pl.pallas_call(functools.partial(attend_kernel, block_len, 1.0 / head_dim...  3.84 us
    unnamed x12, local copies, waits for them, and re-layouts  1.63 us
  transfers between devices with their start and end apart: 31, of which 15 were waited for; matrix products, arithmetic and copies ran while one was open for 4% of the time, Pallas kernels for 5%

profile of v1, /device:TPU:0, one launch (start us, length us, event | category | flops | bytes accessed | tf_op | source)
XLA Modules:
  0.0 78.7 jit_solution(7259671164889989520)
XLA Ops:
  1.5 5.0 %collective-permute-start.2 = (bf16[208,128]{1,0:T(8,128)(2,1)S(1)}, bf16[208,128]{1,0:T(8,128)(2,1)S(1)}, u32[]{:S(2)}, u32[]{:S(2)}) collective-permute-start(bf16[208,128]{1,0:T(8,128)(2,1)S(1)} %pad_maximum_fusion.1.refs_1_), channel_id=1, source_target_pairs={{0,24},{8,16},{16,8},{24,0},{1,25},{9,17},{17,9},{25,1},{2,26},{10... | collective-permute-start | bytes 159752 | tf_op jit(solution)/shard_map/ppermute | solution.py:23
  8.9 2.7 %collective-permute-done.1.refs_3_ = bf16[208,128]{1,0:T(8,128)(2,1)S(1)} collective-permute-done((bf16[208,128]{1,0:T(8,128)(2,1)S(1)}, bf16[208,128]{1,0:T(8,128)(2,1)S(1)}, u32[]{:S(2)}, u32[]{:S(2)}) %collective-permute-start.1) | collective-permute-done | bytes 53280 | tf_op jit(solution)/shard_map/ppermute | solution.py:23
  11.6 1.6 %collective-permute-start.3 = (bf16[1,4,16,128]{3,2,1,0:T(8,128)(2,1)S(1)}, bf16[1,4,16,128]{3,2,1,0:T(8,128)(2,1)S(1)}, u32[]{:S(2)}, u32[]{:S(2)}) collective-permute-start(bf16[1,4,16,128]{3,2,1,0:T(8,128)(2,1)S(1)} %get-tuple-element.26), channel_id=1, source_target_pairs={{0,4},{2,6},{4,0},{6,2},{1,5},{3,7},{5,1},{7,3},{8,12},{10,14},{12... | collective-permute-start | bytes 49160 | tf_op jit(solution)/shard_map/ppermute | solution.py:23
  13.8 1.7 %collective-permute-done.3 = bf16[1,4,16,128]{3,2,1,0:T(8,128)(2,1)S(1)} collective-permute-done((bf16[1,4,16,128]{3,2,1,0:T(8,128)(2,1)S(1)}, bf16[1,4,16,128]{3,2,1,0:T(8,128)(2,1)S(1)}, u32[]{:S(2)}, u32[]{:S(2)}) %collective-permute-start.3) | collective-permute-done | bytes 16416 | tf_op jit(solution)/shard_map/ppermute | solution.py:23
  16.2 3.8 %attend.1.refs_5_ = bf16[96,768]{1,0:T(8,128)(2,1)} custom-call(bf16[6,96,128]{2,1,0:T(8,128)(2,1)} %bitcast.42, bf16[208,128]{1,0:T(8,128)(2,1)} %copy-done.2, bf16[208,128]{1,0:T(8,128)(2,1)} %copy-done.5, bf16[208,128]{1,0:T(8,128)(2,1)} %copy-done.4, bf16[208,128]{1,0:T(8,128)(2,1)} %copy-done.3, s32[96,2]{1,0:T(8,128)} %copy.28.refs_5_, ...), custom_call_target="tpu_custom_call" | custom-call | flops 113246208 | bytes 1048576 | tf_op jit(solution)/shard_map/attend/pallas_call | solution.py:246
  20.0 2.4 %collective-permute-start.16 = (bf16[96,768]{1,0:T(8,128)(2,1)}, bf16[96,768]{1,0:T(8,128)(2,1)S(1)}, u32[]{:S(2)}, u32[]{:S(2)}) collective-permute-start(bf16[96,768]{1,0:T(8,128)(2,1)} %attend.1.refs_5_), channel_id=1, source_target_pairs={{0,24},{8,16},{16,8},{24,0},{1,25},{9,17},{17,9},{25,1},{2,26},{10... | collective-permute-start | bytes 442376 | tf_op jit(solution)/shard_map/ppermute | solution.py:23
  22.4 2.0 %collective-permute-start.8 = (bf16[96,768]{1,0:T(8,128)(2,1)}, bf16[96,768]{1,0:T(8,128)(2,1)S(1)}, u32[]{:S(2)}, u32[]{:S(2)}) collective-permute-start(bf16[96,768]{1,0:T(8,128)(2,1)} %attend.1.refs_5_), channel_id=1, source_target_pairs={{0,8},{8,0},{16,24},{24,16},{1,9},{9,1},{17,25},{25,17},{2,10},{10... | collective-permute-start | bytes 442376 | tf_op jit(solution)/shard_map/ppermute | solution.py:23
  24.4 1.5 %collective-permute-start.6 = (bf16[96,768]{1,0:T(8,128)(2,1)}, bf16[96,768]{1,0:T(8,128)(2,1)S(1)}, u32[]{:S(2)}, u32[]{:S(2)}) collective-permute-start(bf16[96,768]{1,0:T(8,128)(2,1)} %attend.1.refs_5_), channel_id=1, source_target_pairs={{0,4},{2,6},{4,0},{6,2},{1,5},{3,7},{5,1},{7,3},{8,12},{10,14},{12... | collective-permute-start | bytes 442376 | tf_op jit(solution)/shard_map/ppermute | solution.py:23
  26.0 2.8 %collective-permute-done.16.refs_17_ = bf16[96,768]{1,0:T(8,128)(2,1)S(1)} collective-permute-done((bf16[96,768]{1,0:T(8,128)(2,1)}, bf16[96,768]{1,0:T(8,128)(2,1)S(1)}, u32[]{:S(2)}, u32[]{:S(2)}) %collective-permute-start.16) | collective-permute-done | bytes 147488 | tf_op jit(solution)/shard_map/ppermute | solution.py:23
  28.8 1.5 %collective-permute-start.18 = (bf16[96,768]{1,0:T(8,128)(2,1)S(1)}, bf16[96,768]{1,0:T(8,128)(2,1)S(1)}, u32[]{:S(2)}, u32[]{:S(2)}) collective-permute-start(bf16[96,768]{1,0:T(8,128)(2,1)S(1)} %collective-permute-done.16.refs_17_), channel_id=1, source_target_pairs={{0,4},{2,6},{4,0},{6,2},{1,5},{3,7},{5,1},{7,3},{8,12},{10,14},{12... | collective-permute-start | bytes 442376 | tf_op jit(solution)/shard_map/ppermute | solution.py:23
  30.3 5.9 %collective-permute-done.12.refs_13_ = bf16[96,768]{1,0:T(8,128)(2,1)S(1)} collective-permute-done((bf16[96,768]{1,0:T(8,128)(2,1)}, bf16[96,768]{1,0:T(8,128)(2,1)S(1)}, u32[]{:S(2)}, u32[]{:S(2)}) %collective-permute-start.12) | collective-permute-done | bytes 147488 | tf_op jit(solution)/shard_map/ppermute | solution.py:23
  36.3 1.5 %collective-permute-start.14 = (bf16[96,768]{1,0:T(8,128)(2,1)S(1)}, bf16[96,768]{1,0:T(8,128)(2,1)S(1)}, u32[]{:S(2)}, u32[]{:S(2)}) collective-permute-start(bf16[96,768]{1,0:T(8,128)(2,1)S(1)} %collective-permute-done.12.refs_13_), channel_id=1, source_target_pairs={{0,4},{2,6},{4,0},{6,2},{1,5},{3,7},{5,1},{7,3},{8,12},{10,14},{12... | collective-permute-start | bytes 442376 | tf_op jit(solution)/shard_map/ppermute | solution.py:23
  39.0 3.9 %collective-permute-done.14.refs_15_ = bf16[96,768]{1,0:T(8,128)(2,1)S(1)} collective-permute-done((bf16[96,768]{1,0:T(8,128)(2,1)S(1)}, bf16[96,768]{1,0:T(8,128)(2,1)S(1)}, u32[]{:S(2)}, u32[]{:S(2)}) %collective-permute-start.14) | collective-permute-done | bytes 147488 | tf_op jit(solution)/shard_map/ppermute | solution.py:23
  43.4 2.3 %collective-permute-done.10.refs_11_ = bf16[96,768]{1,0:T(8,128)(2,1)S(1)} collective-permute-done((bf16[96,768]{1,0:T(8,128)(2,1)S(1)}, bf16[96,768]{1,0:T(8,128)(2,1)S(1)}, u32[]{:S(2)}, u32[]{:S(2)}) %collective-permute-start.10) | collective-permute-done | bytes 147488 | tf_op jit(solution)/shard_map/ppermute | solution.py:23
  46.0 1.1 %collective-permute-done.11.refs_12_ = bf16[96,768]{1,0:T(8,128)(2,1)S(1)} collective-permute-done((bf16[96,768]{1,0:T(8,128)(2,1)S(1)}, bf16[96,768]{1,0:T(8,128)(2,1)S(1)}, u32[]{:S(2)}, u32[]{:S(2)}) %collective-permute-start.11) | collective-permute-done | bytes 147488 | tf_op jit(solution)/shard_map/ppermute | solution.py:23
  48.7 6.3 %experts.1 = (bf16[48,3072]{1,0:T(8,128)(2,1)S(1)}, bf16[48,3072]{1,0:T(8,128)(2,1)S(1)}, bf16[48,3072]{1,0:T(8,128)(2,1)S(1)}, bf16[48,3072]{1,0:T(8,128)(2,1)S...) custom-call(s32[1]{0:T(128)} %bitcast.refs_0_, ...), custom_call_target="tpu_custom_call" | custom-call | flops 2415919104 | bytes 16777216 | tf_op jit(solution)/shard_map/experts/pallas_call | solution.py:279
  56.7 1.6 %collective-permute-start.21 = (bf16[24,3072]{1,0:T(8,128)(2,1)S(1)}, bf16[24,3072]{1,0:T(8,128)(2,1)S(1)}, u32[]{:S(2)}, u32[]{:S(2)}) collective-permute-start(bf16[24,3072]{1,0:T(8,128)(2,1)S(1)} %slice.107), channel_id=1, source_target_pairs={{0,4},{2,6},{4,0},{6,2},{1,5},{3,7},{5,1},{7,3},{8,12},{10,14},{12... | collective-permute-start | bytes 442376 | tf_op jit(solution)/shard_map/ppermute | solution.py:23
  59.0 1.6 %collective-permute-start.27 = (bf16[24,3072]{1,0:T(8,128)(2,1)S(1)}, bf16[24,3072]{1,0:T(8,128)(2,1)S(1)}, u32[]{:S(2)}, u32[]{:S(2)}) collective-permute-start(bf16[24,3072]{1,0:T(8,128)(2,1)S(1)} %slice.105), channel_id=1, source_target_pairs={{0,4},{2,6},{4,0},{6,2},{1,5},{3,7},{5,1},{7,3},{8,12},{10,14},{12... | collective-permute-start | bytes 442376 | tf_op jit(solution)/shard_map/ppermute | solution.py:23
  61.3 2.1 %collective-permute-done.21 = bf16[24,3072]{1,0:T(8,128)(2,1)S(1)} collective-permute-done((bf16[24,3072]{1,0:T(8,128)(2,1)S(1)}, bf16[24,3072]{1,0:T(8,128)(2,1)S(1)}, u32[]{:S(2)}, u32[]{:S(2)}) %collective-permute-start.21) | collective-permute-done | bytes 147488 | tf_op jit(solution)/shard_map/ppermute | solution.py:23
  63.5 2.7 %collective-permute-start.22 = (bf16[24,3072]{1,0:T(8,128)(2,1)S(1)}, bf16[24,3072]{1,0:T(8,128)(2,1)S(1)}, u32[]{:S(2)}, u32[]{:S(2)}) collective-permute-start(bf16[24,3072]{1,0:T(8,128)(2,1)S(1)} %fusion.4), channel_id=1, source_target_pairs={{0,24},{8,16},{16,8},{24,0},{1,25},{9,17},{17,9},{25,1},{2,26},{10... | collective-permute-start | bytes 442376 | tf_op jit(solution)/shard_map/ppermute | solution.py:23
  66.6 1.1 %collective-permute-start.25 = (bf16[24,3072]{1,0:T(8,128)(2,1)S(1)}, bf16[24,3072]{1,0:T(8,128)(2,1)S(1)}, u32[]{:S(2)}, u32[]{:S(2)}) collective-permute-start(bf16[24,3072]{1,0:T(8,128)(2,1)S(1)} %fusion.3), channel_id=1, source_target_pairs={{0,16},{8,24},{16,0},{24,8},{1,17},{9,25},{17,1},{25,9},{2,18},{10... | collective-permute-start | bytes 442376 | tf_op jit(solution)/shard_map/ppermute | solution.py:23
  67.7 2.1 %collective-permute-done.27 = bf16[24,3072]{1,0:T(8,128)(2,1)S(1)} collective-permute-done((bf16[24,3072]{1,0:T(8,128)(2,1)S(1)}, bf16[24,3072]{1,0:T(8,128)(2,1)S(1)}, u32[]{:S(2)}, u32[]{:S(2)}) %collective-permute-start.27) | collective-permute-done | bytes 147488 | tf_op jit(solution)/shard_map/ppermute | solution.py:23
  70.0 2.1 %collective-permute-done.30 = bf16[24,3072]{1,0:T(8,128)(2,1)S(1)} collective-permute-done((bf16[24,3072]{1,0:T(8,128)(2,1)S(1)}, bf16[24,3072]{1,0:T(8,128)(2,1)S(1)}, u32[]{:S(2)}, u32[]{:S(2)}) %collective-permute-start.30) | collective-permute-done | bytes 147488 | tf_op jit(solution)/shard_map/ppermute | solution.py:23
  72.1 5.4 %collective-permute-done.25 = bf16[24,3072]{1,0:T(8,128)(2,1)S(1)} collective-permute-done((bf16[24,3072]{1,0:T(8,128)(2,1)S(1)}, bf16[24,3072]{1,0:T(8,128)(2,1)S(1)}, u32[]{:S(2)}, u32[]{:S(2)}) %collective-permute-start.25) | collective-permute-done | bytes 147488 | tf_op jit(solution)/shard_map/ppermute | solution.py:23
  (94 shorter events, 14.0 us)
Async XLA Ops:
  1.5 7.4 %collective-permute-start.2 = (bf16[208,128]{1,0:T(8,128)(2,1)S(1)}, bf16[208,128]{1,0:T(8,128)(2,1)S(1)}, u32[]{:S(2)}, u32[]{:S(2)}) collective-permute-start(bf16[208,128]{1,0:T(8,128)(2,1)S(1)} %pad_maximum_fusion.1.refs_1_), channel_id=1, source_target_pairs={{0,24},{8,16},{16,8},{24,0},{1,25},{9,17},{17,9},{25,1},{2,26},{10... | collective-permute-start | bytes 159752 | tf_op jit(solution)/shard_map/ppermute | solution.py:23
  6.5 5.0 %collective-permute-start.1 = (bf16[208,128]{1,0:T(8,128)(2,1)S(1)}, bf16[208,128]{1,0:T(8,128)(2,1)S(1)}, u32[]{:S(2)}, u32[]{:S(2)}) collective-permute-start(bf16[208,128]{1,0:T(8,128)(2,1)S(1)} %pad_maximum_fusion.1.refs_1_), channel_id=1, source_target_pairs={{0,16},{8,24},{16,0},{24,8},{1,17},{9,25},{17,1},{25,9},{2,18},{10... | collective-permute-start | bytes 159752 | tf_op jit(solution)/shard_map/ppermute | solution.py:23
  6.6 5.0 %collective-permute-start = (bf16[208,128]{1,0:T(8,128)(2,1)S(1)}, bf16[208,128]{1,0:T(8,128)(2,1)S(1)}, u32[]{:S(2)}, u32[]{:S(2)}) collective-permute-start(bf16[208,128]{1,0:T(8,128)(2,1)S(1)} %pad_maximum_fusion.1.refs_1_), channel_id=1, source_target_pairs={{0,8},{8,0},{16,24},{24,16},{1,9},{9,1},{17,25},{25,17},{2,10},{10... | collective-permute-start | bytes 159752 | tf_op jit(solution)/shard_map/ppermute | solution.py:23
  11.6 3.8 %collective-permute-start.3 = (bf16[1,4,16,128]{3,2,1,0:T(8,128)(2,1)S(1)}, bf16[1,4,16,128]{3,2,1,0:T(8,128)(2,1)S(1)}, u32[]{:S(2)}, u32[]{:S(2)}) collective-permute-start(bf16[1,4,16,128]{3,2,1,0:T(8,128)(2,1)S(1)} %get-tuple-element.26), channel_id=1, source_target_pairs={{0,4},{2,6},{4,0},{6,2},{1,5},{3,7},{5,1},{7,3},{8,12},{10,14},{12... | collective-permute-start | bytes 49160 | tf_op jit(solution)/shard_map/ppermute | solution.py:23
  15.4 10.5 %collective-permute-start.4 = (bf16[2,4,16,128]{3,2,1,0:T(8,128)(2,1)S(1)}, bf16[2,4,16,128]{3,2,1,0:T(8,128)(2,1)S(1)}, u32[]{:S(2)}, u32[]{:S(2)}) collective-permute-start(bf16[2,4,16,128]{3,2,1,0:T(8,128)(2,1)S(1)} %pad_maximum_fusion.2), channel_id=1, source_target_pairs={{0,2},{2,0},{4,6},{6,4},{1,3},{3,1},{5,7},{7,5},{8,10},{10,8},{12,... | collective-permute-start | bytes 98312 | tf_op jit(solution)/shard_map/ppermute | solution.py:23
  20.0 8.8 %collective-permute-start.16 = (bf16[96,768]{1,0:T(8,128)(2,1)}, bf16[96,768]{1,0:T(8,128)(2,1)S(1)}, u32[]{:S(2)}, u32[]{:S(2)}) collective-permute-start(bf16[96,768]{1,0:T(8,128)(2,1)} %attend.1.refs_5_), channel_id=1, source_target_pairs={{0,24},{8,16},{16,8},{24,0},{1,25},{9,17},{17,9},{25,1},{2,26},{10... | collective-permute-start | bytes 442376 | tf_op jit(solution)/shard_map/ppermute | solution.py:23
  22.4 13.9 %collective-permute-start.12 = (bf16[96,768]{1,0:T(8,128)(2,1)}, bf16[96,768]{1,0:T(8,128)(2,1)S(1)}, u32[]{:S(2)}, u32[]{:S(2)}) collective-permute-start(bf16[96,768]{1,0:T(8,128)(2,1)} %attend.1.refs_5_), channel_id=1, source_target_pairs={{0,16},{8,24},{16,0},{24,8},{1,17},{9,25},{17,1},{25,9},{2,18},{10... | collective-permute-start | bytes 442376 | tf_op jit(solution)/shard_map/ppermute | solution.py:23
  22.4 13.9 %collective-permute-start.8 = (bf16[96,768]{1,0:T(8,128)(2,1)}, bf16[96,768]{1,0:T(8,128)(2,1)S(1)}, u32[]{:S(2)}, u32[]{:S(2)}) collective-permute-start(bf16[96,768]{1,0:T(8,128)(2,1)} %attend.1.refs_5_), channel_id=1, source_target_pairs={{0,8},{8,0},{16,24},{24,16},{1,9},{9,1},{17,25},{25,17},{2,10},{10... | collective-permute-start | bytes 442376 | tf_op jit(solution)/shard_map/ppermute | solution.py:23
  24.4 13.3 %collective-permute-start.6 = (bf16[96,768]{1,0:T(8,128)(2,1)}, bf16[96,768]{1,0:T(8,128)(2,1)S(1)}, u32[]{:S(2)}, u32[]{:S(2)}) collective-permute-start(bf16[96,768]{1,0:T(8,128)(2,1)} %attend.1.refs_5_), channel_id=1, source_target_pairs={{0,4},{2,6},{4,0},{6,2},{1,5},{3,7},{5,1},{7,3},{8,12},{10,14},{12... | collective-permute-start | bytes 442376 | tf_op jit(solution)/shard_map/ppermute | solution.py:23
  25.9 12.1 %collective-permute-start.5 = (bf16[96,768]{1,0:T(8,128)(2,1)}, bf16[96,768]{1,0:T(8,128)(2,1)S(1)}, u32[]{:S(2)}, u32[]{:S(2)}) collective-permute-start(bf16[96,768]{1,0:T(8,128)(2,1)} %attend.1.refs_5_), channel_id=1, source_target_pairs={{0,2},{2,0},{4,6},{6,4},{1,3},{3,1},{5,7},{7,5},{8,10},{10,8},{12,... | collective-permute-start | bytes 442376 | tf_op jit(solution)/shard_map/ppermute | solution.py:23
  28.8 9.7 %collective-permute-start.18 = (bf16[96,768]{1,0:T(8,128)(2,1)S(1)}, bf16[96,768]{1,0:T(8,128)(2,1)S(1)}, u32[]{:S(2)}, u32[]{:S(2)}) collective-permute-start(bf16[96,768]{1,0:T(8,128)(2,1)S(1)} %collective-permute-done.16.refs_17_), channel_id=1, source_target_pairs={{0,4},{2,6},{4,0},{6,2},{1,5},{3,7},{5,1},{7,3},{8,12},{10,14},{12... | collective-permute-start | bytes 442376 | tf_op jit(solution)/shard_map/ppermute | solution.py:23
  36.3 6.6 %collective-permute-start.14 = (bf16[96,768]{1,0:T(8,128)(2,1)S(1)}, bf16[96,768]{1,0:T(8,128)(2,1)S(1)}, u32[]{:S(2)}, u32[]{:S(2)}) collective-permute-start(bf16[96,768]{1,0:T(8,128)(2,1)S(1)} %collective-permute-done.12.refs_13_), channel_id=1, source_target_pairs={{0,4},{2,6},{4,0},{6,2},{1,5},{3,7},{5,1},{7,3},{8,12},{10,14},{12... | collective-permute-start | bytes 442376 | tf_op jit(solution)/shard_map/ppermute | solution.py:23
  37.7 5.2 %collective-permute-start.13 = (bf16[96,768]{1,0:T(8,128)(2,1)S(1)}, bf16[96,768]{1,0:T(8,128)(2,1)S(1)}, u32[]{:S(2)}, u32[]{:S(2)}) collective-permute-start(bf16[96,768]{1,0:T(8,128)(2,1)S(1)} %collective-permute-done.12.refs_13_), channel_id=1, source_target_pairs={{0,2},{2,0},{4,6},{6,4},{1,3},{3,1},{5,7},{7,5},{8,10},{10,8},{12,... | collective-permute-start | bytes 442376 | tf_op jit(solution)/shard_map/ppermute | solution.py:23
  38.0 7.7 %collective-permute-start.10 = (bf16[96,768]{1,0:T(8,128)(2,1)S(1)}, bf16[96,768]{1,0:T(8,128)(2,1)S(1)}, u32[]{:S(2)}, u32[]{:S(2)}) collective-permute-start(bf16[96,768]{1,0:T(8,128)(2,1)S(1)} %collective-permute-done.8.refs_9_), channel_id=1, source_target_pairs={{0,4},{2,6},{4,0},{6,2},{1,5},{3,7},{5,1},{7,3},{8,12},{10,14},{12... | collective-permute-start | bytes 442376 | tf_op jit(solution)/shard_map/ppermute | solution.py:23
  38.5 7.4 %collective-permute-start.9 = (bf16[96,768]{1,0:T(8,128)(2,1)S(1)}, bf16[96,768]{1,0:T(8,128)(2,1)S(1)}, u32[]{:S(2)}, u32[]{:S(2)}) collective-permute-start(bf16[96,768]{1,0:T(8,128)(2,1)S(1)} %collective-permute-done.8.refs_9_), channel_id=1, source_target_pairs={{0,2},{2,0},{4,6},{6,4},{1,3},{3,1},{5,7},{7,5},{8,10},{10,8},{12,... | collective-permute-start | bytes 442376 | tf_op jit(solution)/shard_map/ppermute | solution.py:23
  38.5 7.4 %collective-permute-start.7 = (bf16[96,768]{1,0:T(8,128)(2,1)S(1)}, bf16[96,768]{1,0:T(8,128)(2,1)S(1)}, u32[]{:S(2)}, u32[]{:S(2)}) collective-permute-start(bf16[96,768]{1,0:T(8,128)(2,1)S(1)} %collective-permute-done.6.refs_7_), channel_id=1, source_target_pairs={{0,2},{2,0},{4,6},{6,4},{1,3},{3,1},{5,7},{7,5},{8,10},{10,8},{12,... | collective-permute-start | bytes 442376 | tf_op jit(solution)/shard_map/ppermute | solution.py:23
  55.7 4.9 %collective-permute-start.29 = (bf16[48,3072]{1,0:T(8,128)(2,1)S(1)}, bf16[48,3072]{1,0:T(8,128)(2,1)S(1)}, u32[]{:S(2)}, u32[]{:S(2)}) collective-permute-start(bf16[48,3072]{1,0:T(8,128)(2,1)S(1)} %get-tuple-element.22), channel_id=1, source_target_pairs={{0,2},{2,0},{4,6},{6,4},{1,3},{3,1},{5,7},{7,5},{8,10},{10,8},{12,... | collective-permute-start | bytes 884744 | tf_op jit(solution)/shard_map/ppermute | solution.py:23
  56.7 6.8 %collective-permute-start.21 = (bf16[24,3072]{1,0:T(8,128)(2,1)S(1)}, bf16[24,3072]{1,0:T(8,128)(2,1)S(1)}, u32[]{:S(2)}, u32[]{:S(2)}) collective-permute-start(bf16[24,3072]{1,0:T(8,128)(2,1)S(1)} %slice.107), channel_id=1, source_target_pairs={{0,4},{2,6},{4,0},{6,2},{1,5},{3,7},{5,1},{7,3},{8,12},{10,14},{12... | collective-permute-start | bytes 442376 | tf_op jit(solution)/shard_map/ppermute | solution.py:23
  58.3 8.3 %collective-permute-start.24 = (bf16[24,3072]{1,0:T(8,128)(2,1)S(1)}, bf16[24,3072]{1,0:T(8,128)(2,1)S(1)}, u32[]{:S(2)}, u32[]{:S(2)}) collective-permute-start(bf16[24,3072]{1,0:T(8,128)(2,1)S(1)} %slice.106), channel_id=1, source_target_pairs={{0,4},{2,6},{4,0},{6,2},{1,5},{3,7},{5,1},{7,3},{8,12},{10,14},{12... | collective-permute-start | bytes 442376 | tf_op jit(solution)/shard_map/ppermute | solution.py:23
  59.0 10.7 %collective-permute-start.27 = (bf16[24,3072]{1,0:T(8,128)(2,1)S(1)}, bf16[24,3072]{1,0:T(8,128)(2,1)S(1)}, u32[]{:S(2)}, u32[]{:S(2)}) collective-permute-start(bf16[24,3072]{1,0:T(8,128)(2,1)S(1)} %slice.105), channel_id=1, source_target_pairs={{0,4},{2,6},{4,0},{6,2},{1,5},{3,7},{5,1},{7,3},{8,12},{10,14},{12... | collective-permute-start | bytes 442376 | tf_op jit(solution)/shard_map/ppermute | solution.py:23
  60.7 11.4 %collective-permute-start.30 = (bf16[24,3072]{1,0:T(8,128)(2,1)S(1)}, bf16[24,3072]{1,0:T(8,128)(2,1)S(1)}, u32[]{:S(2)}, u32[]{:S(2)}) collective-permute-start(bf16[24,3072]{1,0:T(8,128)(2,1)S(1)} %slice.104), channel_id=1, source_target_pairs={{0,4},{2,6},{4,0},{6,2},{1,5},{3,7},{5,1},{7,3},{8,12},{10,14},{12... | collective-permute-start | bytes 442376 | tf_op jit(solution)/shard_map/ppermute | solution.py:23
  63.5 8.7 %collective-permute-start.22 = (bf16[24,3072]{1,0:T(8,128)(2,1)S(1)}, bf16[24,3072]{1,0:T(8,128)(2,1)S(1)}, u32[]{:S(2)}, u32[]{:S(2)}) collective-permute-start(bf16[24,3072]{1,0:T(8,128)(2,1)S(1)} %fusion.4), channel_id=1, source_target_pairs={{0,24},{8,16},{16,8},{24,0},{1,25},{9,17},{17,9},{25,1},{2,26},{10... | collective-permute-start | bytes 442376 | tf_op jit(solution)/shard_map/ppermute | solution.py:23
  66.6 10.9 %collective-permute-start.25 = (bf16[24,3072]{1,0:T(8,128)(2,1)S(1)}, bf16[24,3072]{1,0:T(8,128)(2,1)S(1)}, u32[]{:S(2)}, u32[]{:S(2)}) collective-permute-start(bf16[24,3072]{1,0:T(8,128)(2,1)S(1)} %fusion.3), channel_id=1, source_target_pairs={{0,16},{8,24},{16,0},{24,8},{1,17},{9,25},{17,1},{25,9},{2,18},{10... | collective-permute-start | bytes 442376 | tf_op jit(solution)/shard_map/ppermute | solution.py:23
  69.8 8.1 %collective-permute-start.28 = (bf16[24,3072]{1,0:T(8,128)(2,1)S(1)}, bf16[24,3072]{1,0:T(8,128)(2,1)S(1)}, u32[]{:S(2)}, u32[]{:S(2)}) collective-permute-start(bf16[24,3072]{1,0:T(8,128)(2,1)S(1)} %fusion.2), channel_id=1, source_target_pairs={{0,8},{8,0},{16,24},{24,16},{1,9},{9,1},{17,25},{25,17},{2,10},{10... | collective-permute-start | bytes 442376 | tf_op jit(solution)/shard_map/ppermute | solution.py:23
  (13 other events, 50.7 us)

commit v2 on v0

--- a/solution.py
+++ b/solution.py
@@ -1,6 +1,10 @@
+import functools
+
 import jax
 import jax.numpy as jnp
 from jax import lax
+from jax.experimental import pallas as pl
+from jax.experimental.pallas import tpu as pltpu
 from jax.sharding import PartitionSpec as P
 
 WINDOW = 2048
@@ -15,7 +19,13 @@
     return lax.ppermute(x, axis, pairs)
 
 
-def shards(queries, keys, values, doc_ids, norm_gain, expert_ids, route_weights, w_in, w_out):
+def flipped(x, axis, by):
+    return lax.ppermute(x, axis, [(i, i ^ by) for i in range(lax.axis_size(axis))])
+
+
+def routed_shards(
+    queries, keys, values, doc_ids, norm_gain, expert_ids, route_weights, w_in, w_out
+):
     block_len, heads_dev, head_dim = queries.shape
     seq_count = lax.axis_size("seq")
     exp_count = lax.axis_size("exp")
@@ -114,6 +124,262 @@
     return (attn_float + moe_part).astype(jnp.bfloat16)
 
 
+def attend_kernel(block_len, scale, *refs):
+    place_ref, query_ref, doc_row, *packs = refs[:-4]
+    out_ref, marked_ref, keys_ref, values_ref = refs[-4:]
+    place = place_ref[0]
+    lanes = packs[0].shape[1]
+    for i, pack in enumerate(packs):
+        rows = pl.ds(pl.multiple_of((place ^ i) * block_len, block_len), block_len)
+        keys_ref[rows] = pack[0:block_len]
+        values_ref[rows] = pack[block_len : 2 * block_len]
+        marked_ref[block_len:, i * lanes : (i + 1) * lanes] = pack[2 * block_len :]
+    marked_ref[block_len:, len(packs) * lanes :] = jnp.zeros(
+        (marked_ref.shape[0] - block_len, marked_ref.shape[1] - len(packs) * lanes), jnp.bfloat16
+    )
+    start = pl.multiple_of(place * block_len, block_len)
+    query_pos = start + lax.broadcasted_iota(jnp.int32, (block_len, 1), 0)
+    key_pos = lax.broadcasted_iota(jnp.int32, doc_row.shape, 1)
+    key_doc = doc_row[...]
+    query_doc = jnp.sum(jnp.where(query_pos == key_pos, key_doc, 0), axis=1, keepdims=True)
+    allowed = (key_pos <= query_pos) & (query_pos - key_pos < WINDOW) & (query_doc == key_doc)
+    head_dim = query_ref.shape[2]
+    heads = range(query_ref.shape[0])
+    scores = [
+        lax.dot_general(
+            query_ref[head],
+            keys_ref[...],
+            (((1,), (1,)), ((), ())),
+            preferred_element_type=jnp.float32,
+        )
+        for head in heads
+    ]
+    scores = [jnp.where(allowed, score * scale, -jnp.inf) for score in scores]
+    tops = [jnp.max(score, axis=1, keepdims=True) for score in scores]
+    weights = [jnp.exp(score - top) for score, top in zip(scores, tops)]
+    inverses = [1.0 / jnp.sum(weight, axis=1, keepdims=True) for weight in weights]
+    for head in heads:
+        columns = slice(head * head_dim, (head + 1) * head_dim)
+        attended = jnp.dot(
+            (weights[head] * inverses[head]).astype(jnp.bfloat16),
+            values_ref[...],
+            preferred_element_type=jnp.float32,
+        ).astype(jnp.bfloat16)
+        out_ref[:, columns] = attended
+        marked_ref[0:block_len, columns] = attended
+
+
+def experts_kernel(seq_count, group, order, *refs):
+    exp_count = len(order)
+    place_ref, gain_hbm, w_in_hbm, w_out_hbm = refs[:4]
+    marked = refs[4 : 4 + exp_count]
+    refs = refs[4 + exp_count :]
+    blocks = {0: marked}
+    for d in group:
+        if d:
+            blocks[d], refs = refs[:exp_count], refs[exp_count:]
+    kept, sent, refs = refs[: len(group)], refs[len(group) : 2 * len(group)], refs[2 * len(group) :]
+    if 0 in group:
+        own_ref, *refs, split_ref = refs
+    hidden_ref, share_ref, gain_ref, w_in_ref, w_out_ref, sems = refs
+    place = place_ref[0]
+    block_len, token_count = marked[0].shape[0] - 16, hidden_ref.shape[1]
+    part_width = marked[0].shape[1]
+    width = part_width * exp_count
+    lanes = 128
+
+    def rows_of(j):
+        return pl.ds(pl.multiple_of((place ^ j) * part_width, part_width), part_width)
+
+    reads = [
+        pltpu.make_async_copy(w_in_hbm.at[0, rows_of(j)], w_in_ref.at[j], sems.at[j])
+        for j in range(exp_count)
+    ]
+    reads.append(pltpu.make_async_copy(w_out_hbm.at[0], w_out_ref, sems.at[exp_count]))
+    reads.insert(0, pltpu.make_async_copy(gain_hbm, gain_ref, sems.at[exp_count + 1]))
+    for read in reads:
+        read.start()
+
+    share_ref[...] = jnp.zeros_like(share_ref)
+    for j in range(exp_count):
+        share = marked[j][block_len:].astype(jnp.float32)
+        row = lax.broadcasted_iota(jnp.int32, share.shape, 0)
+        share = jnp.where(row % exp_count == place, share, 0.0)
+        share = jnp.sum(share, axis=0, keepdims=True)
+        for i, d in enumerate(group):
+            line = i * exp_count + order.index(j)
+            share_ref[line : line + 1] = share[:, d * lanes : (d + 1) * lanes]
+    share = share_ref[...].T
+    weight = jnp.concatenate(
+        [share[:token_count, i : i + 1] for i in range(len(group) * exp_count)], axis=0
+    )
+
+    reads[0].wait()
+    squares = [jnp.zeros((block_len, lanes), jnp.float32)] * len(group)
+    hidden = None
+    for j in range(exp_count):
+        source = place ^ j
+        gain = gain_ref[source]
+        gained = []
+        for i, d in enumerate(group):
+            value = blocks[d][j][0:block_len].astype(jnp.float32)
+            square = value * value
+            for start in range(0, part_width, lanes):
+                squares[i] = squares[i] + square[:, start : start + lanes]
+            gained.append((value * gain).astype(jnp.bfloat16))
+            if d == 0:
+                split_ref[...] = value.reshape(exp_count, token_count, part_width)
+                own_ref[source] = split_ref[place].astype(jnp.bfloat16)
+        reads[1 + j].wait()
+        product = jnp.dot(
+            jnp.concatenate(gained, axis=0), w_in_ref[j], preferred_element_type=jnp.float32
+        )
+        hidden = product if hidden is None else hidden + product
+    mean_square = jnp.sum(jnp.concatenate(squares, axis=0), axis=1, keepdims=True) * (1.0 / width)
+    hidden = hidden * lax.rsqrt(mean_square + epsilon)
+    hidden = hidden * (1.0 / (1.0 + jnp.exp(-hidden)))
+    hidden_ref[...] = hidden.reshape(len(group) * exp_count, token_count, hidden.shape[1])
+    hidden = jnp.concatenate(
+        [hidden_ref[i * exp_count + (place ^ j)] for i in range(len(group)) for j in order], axis=0
+    ).astype(jnp.bfloat16)
+    half = block_len // 2
+    reads[1 + exp_count].wait()
+    for start in range(0, width, part_width):
+        columns = slice(start, start + part_width)
+        product = jnp.dot(hidden, w_out_ref[:, columns], preferred_element_type=jnp.float32)
+        product = (product * weight).astype(jnp.bfloat16)
+        for i in range(len(group)):
+            low = i * block_len
+            kept[i][:, columns] = product[low : low + half]
+            sent[i][:, columns] = product[low + half : low + block_len]
+
+
+def vmem():
+    return pl.BlockSpec(memory_space=pltpu.VMEM)
+
+
+def anywhere():
+    return pl.BlockSpec(memory_space=pltpu.HBM)
+
+
+def gathered_shards(
+    queries, keys, values, doc_ids, norm_gain, expert_ids, route_weights, w_in, w_out
+):
+    block_len, heads_dev, head_dim = queries.shape
+    seq_count = lax.axis_size("seq")
+    exp_count = lax.axis_size("exp")
+    seq_index = lax.axis_index("seq")
+    exp_index = lax.axis_index("exp")
+    token_count = expert_ids.shape[0]
+    part_width = heads_dev * head_dim
+    width = part_width * exp_count
+    hidden_width = w_in.shape[2]
+    half = block_len // 2
+    far = range(1, seq_count)
+
+    named = expert_ids[:, :, None] == jnp.arange(exp_count, dtype=jnp.int32)[None, None, :]
+    rest = jnp.sum(jnp.where(named, route_weights[:, :, None], 0.0), axis=1).T
+    pieces = []
+    for _ in range(3):
+        piece = lax.reduce_precision(rest, 8, 7)
+        pieces.append(piece.astype(jnp.bfloat16))
+        rest = rest - piece
+    pieces = jnp.concatenate(pieces, axis=0)
+    pieces = jnp.pad(pieces, ((0, 16 - 3 * exp_count), (0, head_dim - token_count)))
+    pack = jnp.concatenate([keys[:, 0, :], values[:, 0, :], pieces], axis=0)
+    packs = [pack] + [flipped(pack, "seq", d) for d in far]
+
+    heads, pack = lax.optimization_barrier((jnp.transpose(queries, (1, 0, 2)), pack))
+    heads = heads * jnp.bfloat16(0.125)
+    packs[0] = pack
+
+    attended, marked = pl.pallas_call(
+        functools.partial(attend_kernel, block_len, 8.0 / head_dim**0.5),
+        out_shape=[
+            jax.ShapeDtypeStruct((block_len, part_width), jnp.bfloat16),
+            jax.ShapeDtypeStruct((block_len + 16, part_width), jnp.bfloat16),
+        ],
+        in_specs=[pl.BlockSpec(memory_space=pltpu.SMEM)] + [vmem()] * (seq_count + 2),
+        out_specs=[vmem()] * 2,
+        scratch_shapes=[pltpu.VMEM((seq_count * block_len, head_dim), jnp.bfloat16)] * 2,
+        compiler_params=pltpu.CompilerParams(vmem_limit_bytes=8 << 20),
+        cost_estimate=pl.CostEstimate(
+            flops=4 * heads_dev * block_len * seq_count * block_len * head_dim,
+            bytes_accessed=1 << 20,
+            transcendentals=heads_dev * block_len * seq_count * block_len,
+        ),
+        name="attend",
+    )(seq_index.reshape(1), heads, doc_ids.reshape(1, -1), *packs)
+
+    first = [seq_count - 1, 1]
+    second = [d for d in range(seq_count - 2, -1, -1) if d not in first]
+    blocks = {(d, 0): flipped(attended, "seq", d) for d in first}
+    blocks[0, 0] = marked
+    blocks |= {(d, 0): flipped(attended, "seq", d) for d in second if d}
+    bit = exp_count // 2
+    while bit:
+        blocks |= {(d, j ^ bit): flipped(block, "exp", bit) for (d, j), block in blocks.items()}
+        bit //= 2
+
+    order = [j for j in range(exp_count) if not j & 1] + [j for j in range(exp_count) if j & 1]
+    gain = norm_gain.reshape(exp_count, 1, part_width)
+    weights = [pltpu.with_memory_space_constraint(w, pltpu.HBM) for w in (gain, w_in, w_out)]
+
+    def experts(group):
+        size = len(group)
+        operands = [blocks[0, j] for j in range(exp_count)]
+        operands += [blocks[d, j] for d in group if d for j in range(exp_count)]
+        out_shape = [jax.ShapeDtypeStruct((half, width), jnp.bfloat16)] * (2 * size)
+        scratch = [
+            pltpu.VMEM((size * exp_count, token_count, hidden_width), jnp.float32),
+            pltpu.VMEM((head_dim, head_dim), jnp.float32),
+            pltpu.VMEM((exp_count, 1, part_width), jnp.float32),
+            pltpu.VMEM((exp_count, part_width, hidden_width), jnp.bfloat16),
+            pltpu.VMEM((hidden_width, width), jnp.bfloat16),
+            pltpu.SemaphoreType.DMA((exp_count + 2,)),
+        ]
+        if 0 in group:
+            split = (exp_count, token_count, part_width)
+            out_shape.append(jax.ShapeDtypeStruct(split, jnp.bfloat16))
+            scratch.append(pltpu.VMEM(split, jnp.float32))
+        in_specs = [pl.BlockSpec(memory_space=pltpu.SMEM)] + [vmem()] * (3 + len(operands))
+        in_specs[1:4] = [anywhere()] * 3
+        outs = pl.pallas_call(
+            functools.partial(experts_kernel, seq_count, group, order),
+            out_shape=out_shape,
+            in_specs=in_specs,
+            out_specs=[vmem()] * len(out_shape),
+            scratch_shapes=scratch,
+            compiler_params=pltpu.CompilerParams(vmem_limit_bytes=16 << 20),
+            cost_estimate=pl.CostEstimate(
+                flops=4 * size * block_len * width * hidden_width,
+                bytes_accessed=8 << 20,
+                transcendentals=size * block_len * hidden_width,
+            ),
+            name="experts",
+        )(exp_index.reshape(1), *weights, *operands)
+        return dict(zip(group, zip(outs[:size], outs[size : 2 * size]))), outs[-1]
+
+    def send(returned):
+        sums = {}
+        for d, (kept, sent) in returned.items():
+            both = kept.astype(jnp.float32) + flipped(sent, "exp", 1).astype(jnp.float32)
+            sums[d] = both[:token_count], both[token_count:].astype(jnp.bfloat16)
+        return sums
+
+    early, _ = experts(first)
+    early = send(early)
+    late, own = experts(second)
+    late = send(late)
+    total = jnp.transpose(own, (1, 0, 2)).reshape(token_count, width).astype(jnp.float32)
+    for d, (mine, away) in sorted((early | late).items(), reverse=True):
+        mine = mine + flipped(away, "exp", 2).astype(jnp.float32)
+        if d:
+            mine = flipped(mine.astype(jnp.bfloat16), "seq", d).astype(jnp.float32)
+        total = total + mine
+    return total.astype(jnp.bfloat16)
+
+
 def solution(mesh):
     placed = (
         P(("dp", "seq"), "exp", None),
@@ -126,6 +392,11 @@
         P("exp", None, "seq"),
         P("exp", "seq", None),
     )
+    small = mesh.shape["seq"] == 4 and mesh.shape["exp"] == 4
     return jax.shard_map(
-        shards, mesh=mesh, in_specs=placed, out_specs=P(("dp", "seq", "exp"), None), check_vma=False
-    )
+        gathered_shards if small else routed_shards,
+        mesh=mesh,
+        in_specs=placed,
+        out_specs=P(("dp", "seq", "exp"), None),
+        check_vma=False,
+    )

time: 142 us -> 63.7 us (0.45)
  waiting for transfers between devices: 69.8 us -> 26.3 us
  between operations: 13.7 us -> 0.16 us
  blocking collectives: 11.6 us -> 0 us
  local copies, waits for them, and re-layouts: 10.6 us -> 0.78 us
  matrix products: 9.44 us -> 0 us
  Pallas kernels: 0 us -> 8.43 us
  starting transfers between devices: 22.4 us -> 24.2 us
    all_gather x1 -> x0, waiting for transfers between devices: 29.2 us -> none  [shards(): lax.all_gather(arrived, 'seq', axis=0, tiled=True)]
    reduce_scatter x1 -> x0, waiting for transfers between devices: 28.4 us -> none  [shards(): lax.psum_scatter(jnp.dot(hidden, weight_out, preferred_element_type=jnp.f...]
    ppermute x6 -> x29, waiting for transfers between devices: 0.02 us -> 26.3 us  [flipped(): lax.ppermute(x, axis, [(i, i ^ by) for i in range(lax.axis_size(axis))])]
    all_to_all x2 -> x0, waiting for transfers between devices: 12.2 us -> none  [the longest x1 7.48 us: shards(): lax.all_to_all(expert_out, 'exp', split_axis=0, concat_axis=0, tiled=True)]
    all_to_all x1 -> x0, blocking collectives: 11.6 us -> none  [shards(): lax.all_to_all(outgoing.reshape(exp_count, capacity, width), 'exp', split...]
    dot_general x5 -> x0, matrix products: 9.44 us -> none  [the longest x1 4.83 us: shards(): jnp.dot(hidden, weight_out, preferred_element_type=jnp.float32)]
    ppermute x6 -> x29, starting transfers between devices: 14.8 us -> 24.2 us  [flipped(): lax.ppermute(x, axis, [(i, i ^ by) for i in range(lax.axis_size(axis))])]
    pallas_call x0 -> x3, Pallas kernels: none -> 8.43 us  [the longest x2 7.68 us: experts(): pl.pallas_call(functools.partial(experts_kernel, seq_count, group, order)...]
  transfers between devices with their start and end apart: 10 -> 29, of which waited for: 4 -> 15; matrix products, arithmetic and copies ran while one was open for 4% -> 3% of each run, Pallas kernels for 0% -> 12%
where the time goes in v2:
time: 63.7 us; the launch traced here: 63.4 us
  waiting for transfers between devices  26.3 us (41%)
  starting transfers between devices  24.2 us (38%)
  Pallas kernels  8.43 us (13%)
  other arithmetic  3.56 us (6%)
  local copies, waits for them, and re-layouts  0.78 us (1%)
    ppermute x29, waiting for transfers between devices, flipped(): lax.ppermute(x, axis, [(i, i ^ by) for i in range(lax.axis_size(axis))])  26.3 us
    ppermute x29, starting transfers between devices, flipped(): lax.ppermute(x, axis, [(i, i ^ by) for i in range(lax.axis_size(axis))])  24.2 us
    pallas_call x2, Pallas kernels, experts(): pl.pallas_call(functools.partial(experts_kernel, seq_count, group, order)...  7.68 us
  transfers between devices with their start and end apart: 29, of which 15 were waited for; matrix products, arithmetic and copies ran while one was open for 3% of the time, Pallas kernels for 12%

profile of v2, /device:TPU:0, one launch (start us, length us, event | category | flops | bytes accessed | tf_op | source)
XLA Modules:
  0.0 63.4 jit_solution(18144183249616040516)
XLA Ops:
  1.5 3.0 %collective-permute-start = (bf16[208,128]{1,0:T(8,128)(2,1)S(1)}, bf16[208,128]{1,0:T(8,128)(2,1)S(1)}, u32[]{:S(2)}, u32[]{:S(2)}) collective-permute-start(bf16[208,128]{1,0:T(8,128)(2,1)S(1)} %pad_maximum_fusion.refs_3_), channel_id=1, source_target_pairs={{0,8},{8,0},{16,24},{24,16},{1,9},{9,1},{17,25},{25,17},{2,10},{10... | collective-permute-start | bytes 159752 | tf_op jit(solution)/shard_map/ppermute | solution.py:23
  4.5 2.6 %collective-permute-start.1 = (bf16[208,128]{1,0:T(8,128)(2,1)S(1)}, bf16[208,128]{1,0:T(8,128)(2,1)S(1)}, u32[]{:S(2)}, u32[]{:S(2)}) collective-permute-start(bf16[208,128]{1,0:T(8,128)(2,1)S(1)} %pad_maximum_fusion.refs_3_), channel_id=1, source_target_pairs={{0,16},{8,24},{16,0},{24,8},{1,17},{9,25},{17,1},{25,9},{2,18},{10... | collective-permute-start | bytes 159752 | tf_op jit(solution)/shard_map/ppermute | solution.py:23
  8.7 1.8 %collective-permute-done.1.refs_5_ = bf16[208,128]{1,0:T(8,128)(2,1)S(1)} collective-permute-done((bf16[208,128]{1,0:T(8,128)(2,1)S(1)}, bf16[208,128]{1,0:T(8,128)(2,1)S(1)}, u32[]{:S(2)}, u32[]{:S(2)}) %collective-permute-start.1) | collective-permute-done | bytes 53280 | tf_op jit(solution)/shard_map/ppermute | solution.py:23
  10.6 2.5 %collective-permute-done.2.refs_6_ = bf16[208,128]{1,0:T(8,128)(2,1)S(1)} collective-permute-done((bf16[208,128]{1,0:T(8,128)(2,1)S(1)}, bf16[208,128]{1,0:T(8,128)(2,1)S(1)}, u32[]{:S(2)}, u32[]{:S(2)}) %collective-permute-start.2) | collective-permute-done | bytes 53280 | tf_op jit(solution)/shard_map/ppermute | solution.py:23
  13.8 1.1 %collective-permute-start.10 = (bf16[96,768]{1,0:T(8,128)(2,1)S(1)}, bf16[96,768]{1,0:T(8,128)(2,1)S(1)}, u32[]{:S(2)}, u32[]{:S(2)}) collective-permute-start(bf16[96,768]{1,0:T(8,128)(2,1)S(1)} %get-tuple-element.21), channel_id=1, source_target_pairs={{0,24},{8,16},{16,8},{24,0},{1,25},{9,17},{17,9},{25,1},{2,26},{10... | collective-permute-start | bytes 442376 | tf_op jit(solution)/shard_map/ppermute | solution.py:23
  15.1 1.5 %collective-permute-start.4 = (bf16[112,768]{1,0:T(8,128)(2,1)S(1)}, bf16[112,768]{1,0:T(8,128)(2,1)S(1)}, u32[]{:S(2)}, u32[]{:S(2)}) collective-permute-start(bf16[112,768]{1,0:T(8,128)(2,1)S(1)} %get-tuple-element.20.refs_4_), channel_id=1, source_target_pairs={{0,4},{2,6},{4,0},{6,2},{1,5},{3,7},{5,1},{7,3},{8,12},{10,14},{12... | collective-permute-start | bytes 516104 | tf_op jit(solution)/shard_map/ppermute | solution.py:23
  16.6 3.2 %collective-permute-start.6 = (bf16[96,768]{1,0:T(8,128)(2,1)S(1)}, bf16[96,768]{1,0:T(8,128)(2,1)S(1)}, u32[]{:S(2)}, u32[]{:S(2)}) collective-permute-start(bf16[96,768]{1,0:T(8,128)(2,1)S(1)} %get-tuple-element.21), channel_id=1, source_target_pairs={{0,16},{8,24},{16,0},{24,8},{1,17},{9,25},{17,1},{25,9},{2,18},{10... | collective-permute-start | bytes 442376 | tf_op jit(solution)/shard_map/ppermute | solution.py:23
  19.8 1.6 %collective-permute-done.10.refs_8_ = bf16[96,768]{1,0:T(8,128)(2,1)S(1)} collective-permute-done((bf16[96,768]{1,0:T(8,128)(2,1)S(1)}, bf16[96,768]{1,0:T(8,128)(2,1)S(1)}, u32[]{:S(2)}, u32[]{:S(2)}) %collective-permute-start.10) | collective-permute-done | bytes 147488 | tf_op jit(solution)/shard_map/ppermute | solution.py:23
  21.4 1.8 %collective-permute-start.12 = (bf16[96,768]{1,0:T(8,128)(2,1)S(1)}, bf16[96,768]{1,0:T(8,128)(2,1)S(1)}, u32[]{:S(2)}, u32[]{:S(2)}) collective-permute-start(bf16[96,768]{1,0:T(8,128)(2,1)S(1)} %collective-permute-done.10.refs_8_), channel_id=1, source_target_pairs={{0,4},{2,6},{4,0},{6,2},{1,5},{3,7},{5,1},{7,3},{8,12},{10,14},{12... | collective-permute-start | bytes 442376 | tf_op jit(solution)/shard_map/ppermute | solution.py:23
  23.4 4.2 %collective-permute-done.6.refs_8_ = bf16[96,768]{1,0:T(8,128)(2,1)S(1)} collective-permute-done((bf16[96,768]{1,0:T(8,128)(2,1)S(1)}, bf16[96,768]{1,0:T(8,128)(2,1)S(1)}, u32[]{:S(2)}, u32[]{:S(2)}) %collective-permute-start.6) | collective-permute-done | bytes 147488 | tf_op jit(solution)/shard_map/ppermute | solution.py:23
  29.0 1.5 %collective-permute-start.8 = (bf16[96,768]{1,0:T(8,128)(2,1)S(1)}, bf16[96,768]{1,0:T(8,128)(2,1)S(1)}, u32[]{:S(2)}, u32[]{:S(2)}) collective-permute-start(bf16[96,768]{1,0:T(8,128)(2,1)S(1)} %collective-permute-done.6.refs_8_), channel_id=1, source_target_pairs={{0,4},{2,6},{4,0},{6,2},{1,5},{3,7},{5,1},{7,3},{8,12},{10,14},{12... | collective-permute-start | bytes 442376 | tf_op jit(solution)/shard_map/ppermute | solution.py:23
  30.5 3.8 %experts.3 = (bf16[48,3072]{1,0:T(8,128)(2,1)S(1)}, bf16[48,3072]{1,0:T(8,128)(2,1)S(1)}, bf16[48,3072]{1,0:T(8,128)(2,1)S(1)}, bf16[48,3072]{1,0:T(8,128)(2,1)S(1)}) custom-call(s32[1]{0:T(128)} %bitcast.refs_0_, f32[4,1,768]{2,1,0:T(1,128)} %bitcast.19, bf16[1,3072,512]{2,1,0:T(8,128)(2,1)} %refs_2_.3, bf16[1,512,3072]{2,1,0:T(8,128)(2,1)} %refs_3_.3, ...), custom_call_target="tpu_custom_call" | custom-call | flops 1207959552 | bytes 8388608 | tf_op jit(solution)/shard_map/experts/pallas_call | solution.py:347
  35.2 1.0 %collective-permute-done.7.refs_9_ = bf16[96,768]{1,0:T(8,128)(2,1)S(1)} collective-permute-done((bf16[96,768]{1,0:T(8,128)(2,1)S(1)}, bf16[96,768]{1,0:T(8,128)(2,1)S(1)}, u32[]{:S(2)}, u32[]{:S(2)}) %collective-permute-start.7) | collective-permute-done | bytes 147488 | tf_op jit(solution)/shard_map/ppermute | solution.py:23
  36.6 3.8 %experts.2 = (bf16[48,3072]{1,0:T(8,128)(2,1)S(1)}, bf16[48,3072]{1,0:T(8,128)(2,1)S(1)}, bf16[48,3072]{1,0:T(8,128)(2,1)S(1)}, bf16[48,3072]{1,0:T(8,128)(2,1)S(1)}, bf16[4,24,768]{2,1,0:T(8,128)(2,1)S(1)}) custom-call(s32[1]{0:T(128)} %bitcast.refs_0_, f32[4,1,768]{2,1,0:T(1,128)} %bitcast.20, bf16[1,3072,512]{2,1,0:T(8,128)(2,1)} %refs_2_.3, ...), custom_call_target="tpu_custom_call" | custom-call | flops 1207959552 | bytes 8388608 | tf_op jit(solution)/shard_map/experts/pallas_call | solution.py:347
  41.2 1.2 %collective-permute-start.19 = (bf16[24,3072]{1,0:T(8,128)(2,1)S(1)}, bf16[24,3072]{1,0:T(8,128)(2,1)S(1)}, u32[]{:S(2)}, u32[]{:S(2)}) collective-permute-start(bf16[24,3072]{1,0:T(8,128)(2,1)S(1)} %slice.65), channel_id=1, source_target_pairs={{0,4},{2,6},{4,0},{6,2},{1,5},{3,7},{5,1},{7,3},{8,12},{10,14},{12... | collective-permute-start | bytes 442376 | tf_op jit(solution)/shard_map/ppermute | solution.py:23
  43.6 1.2 %collective-permute-start.25 = (bf16[24,3072]{1,0:T(8,128)(2,1)S(1)}, bf16[24,3072]{1,0:T(8,128)(2,1)S(1)}, u32[]{:S(2)}, u32[]{:S(2)}) collective-permute-start(bf16[24,3072]{1,0:T(8,128)(2,1)S(1)} %slice.63), channel_id=1, source_target_pairs={{0,4},{2,6},{4,0},{6,2},{1,5},{3,7},{5,1},{7,3},{8,12},{10,14},{12... | collective-permute-start | bytes 442376 | tf_op jit(solution)/shard_map/ppermute | solution.py:23
  44.9 0.9 %collective-permute-start.28 = (bf16[24,3072]{1,0:T(8,128)(2,1)S(1)}, bf16[24,3072]{1,0:T(8,128)(2,1)S(1)}, u32[]{:S(2)}, u32[]{:S(2)}) collective-permute-start(bf16[24,3072]{1,0:T(8,128)(2,1)S(1)} %slice.62), channel_id=1, source_target_pairs={{0,4},{2,6},{4,0},{6,2},{1,5},{3,7},{5,1},{7,3},{8,12},{10,14},{12... | collective-permute-start | bytes 442376 | tf_op jit(solution)/shard_map/ppermute | solution.py:23
  45.8 2.1 %collective-permute-done.19 = bf16[24,3072]{1,0:T(8,128)(2,1)S(1)} collective-permute-done((bf16[24,3072]{1,0:T(8,128)(2,1)S(1)}, bf16[24,3072]{1,0:T(8,128)(2,1)S(1)}, u32[]{:S(2)}, u32[]{:S(2)}) %collective-permute-start.19) | collective-permute-done | bytes 147488 | tf_op jit(solution)/shard_map/ppermute | solution.py:23
  48.0 1.7 %collective-permute-start.20 = (bf16[24,3072]{1,0:T(8,128)(2,1)S(1)}, bf16[24,3072]{1,0:T(8,128)(2,1)S(1)}, u32[]{:S(2)}, u32[]{:S(2)}) collective-permute-start(bf16[24,3072]{1,0:T(8,128)(2,1)S(1)} %fusion.4), channel_id=1, source_target_pairs={{0,24},{8,16},{16,8},{24,0},{1,25},{9,17},{17,9},{25,1},{2,26},{10... | collective-permute-start | bytes 442376 | tf_op jit(solution)/shard_map/ppermute | solution.py:23
  49.7 1.4 %collective-permute-done.22 = bf16[24,3072]{1,0:T(8,128)(2,1)S(1)} collective-permute-done((bf16[24,3072]{1,0:T(8,128)(2,1)S(1)}, bf16[24,3072]{1,0:T(8,128)(2,1)S(1)}, u32[]{:S(2)}, u32[]{:S(2)}) %collective-permute-start.22) | collective-permute-done | bytes 147488 | tf_op jit(solution)/shard_map/ppermute | solution.py:23
  51.2 1.2 %collective-permute-start.23 = (bf16[24,3072]{1,0:T(8,128)(2,1)S(1)}, bf16[24,3072]{1,0:T(8,128)(2,1)S(1)}, u32[]{:S(2)}, u32[]{:S(2)}) collective-permute-start(bf16[24,3072]{1,0:T(8,128)(2,1)S(1)} %fusion.3), channel_id=1, source_target_pairs={{0,16},{8,24},{16,0},{24,8},{1,17},{9,25},{17,1},{25,9},{2,18},{10... | collective-permute-start | bytes 442376 | tf_op jit(solution)/shard_map/ppermute | solution.py:23
  52.3 2.0 %collective-permute-done.25 = bf16[24,3072]{1,0:T(8,128)(2,1)S(1)} collective-permute-done((bf16[24,3072]{1,0:T(8,128)(2,1)S(1)}, bf16[24,3072]{1,0:T(8,128)(2,1)S(1)}, u32[]{:S(2)}, u32[]{:S(2)}) %collective-permute-start.25) | collective-permute-done | bytes 147488 | tf_op jit(solution)/shard_map/ppermute | solution.py:23
  54.5 2.4 %collective-permute-done.28 = bf16[24,3072]{1,0:T(8,128)(2,1)S(1)} collective-permute-done((bf16[24,3072]{1,0:T(8,128)(2,1)S(1)}, bf16[24,3072]{1,0:T(8,128)(2,1)S(1)}, u32[]{:S(2)}, u32[]{:S(2)}) %collective-permute-start.28) | collective-permute-done | bytes 147488 | tf_op jit(solution)/shard_map/ppermute | solution.py:23
  56.9 5.3 %collective-permute-done.23 = bf16[24,3072]{1,0:T(8,128)(2,1)S(1)} collective-permute-done((bf16[24,3072]{1,0:T(8,128)(2,1)S(1)}, bf16[24,3072]{1,0:T(8,128)(2,1)S(1)}, u32[]{:S(2)}, u32[]{:S(2)}) %collective-permute-start.23) | collective-permute-done | bytes 147488 | tf_op jit(solution)/shard_map/ppermute | solution.py:23
  (57 shorter events, 10.3 us)
Async XLA Ops:
  1.5 7.2 %collective-permute-start = (bf16[208,128]{1,0:T(8,128)(2,1)S(1)}, bf16[208,128]{1,0:T(8,128)(2,1)S(1)}, u32[]{:S(2)}, u32[]{:S(2)}) collective-permute-start(bf16[208,128]{1,0:T(8,128)(2,1)S(1)} %pad_maximum_fusion.refs_3_), channel_id=1, source_target_pairs={{0,8},{8,0},{16,24},{24,16},{1,9},{9,1},{17,25},{25,17},{2,10},{10... | collective-permute-start | bytes 159752 | tf_op jit(solution)/shard_map/ppermute | solution.py:23
  4.5 6.1 %collective-permute-start.1 = (bf16[208,128]{1,0:T(8,128)(2,1)S(1)}, bf16[208,128]{1,0:T(8,128)(2,1)S(1)}, u32[]{:S(2)}, u32[]{:S(2)}) collective-permute-start(bf16[208,128]{1,0:T(8,128)(2,1)S(1)} %pad_maximum_fusion.refs_3_), channel_id=1, source_target_pairs={{0,16},{8,24},{16,0},{24,8},{1,17},{9,25},{17,1},{25,9},{2,18},{10... | collective-permute-start | bytes 159752 | tf_op jit(solution)/shard_map/ppermute | solution.py:23
  7.1 5.9 %collective-permute-start.2 = (bf16[208,128]{1,0:T(8,128)(2,1)S(1)}, bf16[208,128]{1,0:T(8,128)(2,1)S(1)}, u32[]{:S(2)}, u32[]{:S(2)}) collective-permute-start(bf16[208,128]{1,0:T(8,128)(2,1)S(1)} %pad_maximum_fusion.refs_3_), channel_id=1, source_target_pairs={{0,24},{8,16},{16,8},{24,0},{1,25},{9,17},{17,9},{25,1},{2,26},{10... | collective-permute-start | bytes 159752 | tf_op jit(solution)/shard_map/ppermute | solution.py:23
  13.8 7.6 %collective-permute-start.10 = (bf16[96,768]{1,0:T(8,128)(2,1)S(1)}, bf16[96,768]{1,0:T(8,128)(2,1)S(1)}, u32[]{:S(2)}, u32[]{:S(2)}) collective-permute-start(bf16[96,768]{1,0:T(8,128)(2,1)S(1)} %get-tuple-element.21), channel_id=1, source_target_pairs={{0,24},{8,16},{16,8},{24,0},{1,25},{9,17},{17,9},{25,1},{2,26},{10... | collective-permute-start | bytes 442376 | tf_op jit(solution)/shard_map/ppermute | solution.py:23
  14.9 8.3 %collective-permute-start.14 = (bf16[96,768]{1,0:T(8,128)(2,1)S(1)}, bf16[96,768]{1,0:T(8,128)(2,1)S(1)}, u32[]{:S(2)}, u32[]{:S(2)}) collective-permute-start(bf16[96,768]{1,0:T(8,128)(2,1)S(1)} %get-tuple-element.21), channel_id=1, source_target_pairs={{0,8},{8,0},{16,24},{24,16},{1,9},{9,1},{17,25},{25,17},{2,10},{10... | collective-permute-start | bytes 442376 | tf_op jit(solution)/shard_map/ppermute | solution.py:23
  15.1 8.3 %collective-permute-start.4 = (bf16[112,768]{1,0:T(8,128)(2,1)S(1)}, bf16[112,768]{1,0:T(8,128)(2,1)S(1)}, u32[]{:S(2)}, u32[]{:S(2)}) collective-permute-start(bf16[112,768]{1,0:T(8,128)(2,1)S(1)} %get-tuple-element.20.refs_4_), channel_id=1, source_target_pairs={{0,4},{2,6},{4,0},{6,2},{1,5},{3,7},{5,1},{7,3},{8,12},{10,14},{12... | collective-permute-start | bytes 516104 | tf_op jit(solution)/shard_map/ppermute | solution.py:23
  16.6 11.2 %collective-permute-start.3 = (bf16[112,768]{1,0:T(8,128)(2,1)S(1)}, bf16[112,768]{1,0:T(8,128)(2,1)S(1)}, u32[]{:S(2)}, u32[]{:S(2)}) collective-permute-start(bf16[112,768]{1,0:T(8,128)(2,1)S(1)} %get-tuple-element.20.refs_4_), channel_id=1, source_target_pairs={{0,2},{2,0},{4,6},{6,4},{1,3},{3,1},{5,7},{7,5},{8,10},{10,8},{12,... | collective-permute-start | bytes 516104 | tf_op jit(solution)/shard_map/ppermute | solution.py:23
  16.6 11.0 %collective-permute-start.6 = (bf16[96,768]{1,0:T(8,128)(2,1)S(1)}, bf16[96,768]{1,0:T(8,128)(2,1)S(1)}, u32[]{:S(2)}, u32[]{:S(2)}) collective-permute-start(bf16[96,768]{1,0:T(8,128)(2,1)S(1)} %get-tuple-element.21), channel_id=1, source_target_pairs={{0,16},{8,24},{16,0},{24,8},{1,17},{9,25},{17,1},{25,9},{2,18},{10... | collective-permute-start | bytes 442376 | tf_op jit(solution)/shard_map/ppermute | solution.py:23
  21.4 6.8 %collective-permute-start.12 = (bf16[96,768]{1,0:T(8,128)(2,1)S(1)}, bf16[96,768]{1,0:T(8,128)(2,1)S(1)}, u32[]{:S(2)}, u32[]{:S(2)}) collective-permute-start(bf16[96,768]{1,0:T(8,128)(2,1)S(1)} %collective-permute-done.10.refs_8_), channel_id=1, source_target_pairs={{0,4},{2,6},{4,0},{6,2},{1,5},{3,7},{5,1},{7,3},{8,12},{10,14},{12... | collective-permute-start | bytes 442376 | tf_op jit(solution)/shard_map/ppermute | solution.py:23
  23.2 5.7 %collective-permute-start.16 = (bf16[96,768]{1,0:T(8,128)(2,1)S(1)}, bf16[96,768]{1,0:T(8,128)(2,1)S(1)}, u32[]{:S(2)}, u32[]{:S(2)}) collective-permute-start(bf16[96,768]{1,0:T(8,128)(2,1)S(1)} %collective-permute-done.14.refs_12_), channel_id=1, source_target_pairs={{0,4},{2,6},{4,0},{6,2},{1,5},{3,7},{5,1},{7,3},{8,12},{10,14},{12... | collective-permute-start | bytes 442376 | tf_op jit(solution)/shard_map/ppermute | solution.py:23
  23.4 7.0 %collective-permute-start.5 = (bf16[112,768]{1,0:T(8,128)(2,1)S(1)}, bf16[112,768]{1,0:T(8,128)(2,1)S(1)}, u32[]{:S(2)}, u32[]{:S(2)}) collective-permute-start(bf16[112,768]{1,0:T(8,128)(2,1)S(1)} %collective-permute-done.4.refs_6_), channel_id=1, source_target_pairs={{0,2},{2,0},{4,6},{6,4},{1,3},{3,1},{5,7},{7,5},{8,10},{10,8},{12,... | collective-permute-start | bytes 516104 | tf_op jit(solution)/shard_map/ppermute | solution.py:23
  27.7 2.7 %collective-permute-start.15 = (bf16[96,768]{1,0:T(8,128)(2,1)S(1)}, bf16[96,768]{1,0:T(8,128)(2,1)S(1)}, u32[]{:S(2)}, u32[]{:S(2)}) collective-permute-start(bf16[96,768]{1,0:T(8,128)(2,1)S(1)} %collective-permute-done.14.refs_12_), channel_id=1, source_target_pairs={{0,2},{2,0},{4,6},{6,4},{1,3},{3,1},{5,7},{7,5},{8,10},{10,8},{12,... | collective-permute-start | bytes 442376 | tf_op jit(solution)/shard_map/ppermute | solution.py:23
  28.2 2.3 %collective-permute-start.13 = (bf16[96,768]{1,0:T(8,128)(2,1)S(1)}, bf16[96,768]{1,0:T(8,128)(2,1)S(1)}, u32[]{:S(2)}, u32[]{:S(2)}) collective-permute-start(bf16[96,768]{1,0:T(8,128)(2,1)S(1)} %collective-permute-done.12.refs_10_), channel_id=1, source_target_pairs={{0,2},{2,0},{4,6},{6,4},{1,3},{3,1},{5,7},{7,5},{8,10},{10,8},{12,... | collective-permute-start | bytes 442376 | tf_op jit(solution)/shard_map/ppermute | solution.py:23
  29.0 6.2 %collective-permute-start.8 = (bf16[96,768]{1,0:T(8,128)(2,1)S(1)}, bf16[96,768]{1,0:T(8,128)(2,1)S(1)}, u32[]{:S(2)}, u32[]{:S(2)}) collective-permute-start(bf16[96,768]{1,0:T(8,128)(2,1)S(1)} %collective-permute-done.6.refs_8_), channel_id=1, source_target_pairs={{0,4},{2,6},{4,0},{6,2},{1,5},{3,7},{5,1},{7,3},{8,12},{10,14},{12... | collective-permute-start | bytes 442376 | tf_op jit(solution)/shard_map/ppermute | solution.py:23
  34.3 6.8 %collective-permute-start.18 = (bf16[48,3072]{1,0:T(8,128)(2,1)S(1)}, bf16[48,3072]{1,0:T(8,128)(2,1)S(1)}, u32[]{:S(2)}, u32[]{:S(2)}) collective-permute-start(bf16[48,3072]{1,0:T(8,128)(2,1)S(1)} %get-tuple-element.24), channel_id=1, source_target_pairs={{0,2},{2,0},{4,6},{6,4},{1,3},{3,1},{5,7},{7,5},{8,10},{10,8},{12,... | collective-permute-start | bytes 884744 | tf_op jit(solution)/shard_map/ppermute | solution.py:23
  40.6 2.9 %collective-permute-start.24 = (bf16[48,3072]{1,0:T(8,128)(2,1)S(1)}, bf16[48,3072]{1,0:T(8,128)(2,1)S(1)}, u32[]{:S(2)}, u32[]{:S(2)}) collective-permute-start(bf16[48,3072]{1,0:T(8,128)(2,1)S(1)} %get-tuple-element.28), channel_id=1, source_target_pairs={{0,2},{2,0},{4,6},{6,4},{1,3},{3,1},{5,7},{7,5},{8,10},{10,8},{12,... | collective-permute-start | bytes 884744 | tf_op jit(solution)/shard_map/ppermute | solution.py:23
  41.0 3.8 %collective-permute-start.27 = (bf16[48,3072]{1,0:T(8,128)(2,1)S(1)}, bf16[48,3072]{1,0:T(8,128)(2,1)S(1)}, u32[]{:S(2)}, u32[]{:S(2)}) collective-permute-start(bf16[48,3072]{1,0:T(8,128)(2,1)S(1)} %get-tuple-element.30), channel_id=1, source_target_pairs={{0,2},{2,0},{4,6},{6,4},{1,3},{3,1},{5,7},{7,5},{8,10},{10,8},{12,... | collective-permute-start | bytes 884744 | tf_op jit(solution)/shard_map/ppermute | solution.py:23
  41.2 6.7 %collective-permute-start.19 = (bf16[24,3072]{1,0:T(8,128)(2,1)S(1)}, bf16[24,3072]{1,0:T(8,128)(2,1)S(1)}, u32[]{:S(2)}, u32[]{:S(2)}) collective-permute-start(bf16[24,3072]{1,0:T(8,128)(2,1)S(1)} %slice.65), channel_id=1, source_target_pairs={{0,4},{2,6},{4,0},{6,2},{1,5},{3,7},{5,1},{7,3},{8,12},{10,14},{12... | collective-permute-start | bytes 442376 | tf_op jit(solution)/shard_map/ppermute | solution.py:23
  42.6 8.6 %collective-permute-start.22 = (bf16[24,3072]{1,0:T(8,128)(2,1)S(1)}, bf16[24,3072]{1,0:T(8,128)(2,1)S(1)}, u32[]{:S(2)}, u32[]{:S(2)}) collective-permute-start(bf16[24,3072]{1,0:T(8,128)(2,1)S(1)} %slice.64), channel_id=1, source_target_pairs={{0,4},{2,6},{4,0},{6,2},{1,5},{3,7},{5,1},{7,3},{8,12},{10,14},{12... | collective-permute-start | bytes 442376 | tf_op jit(solution)/shard_map/ppermute | solution.py:23
  43.6 10.7 %collective-permute-start.25 = (bf16[24,3072]{1,0:T(8,128)(2,1)S(1)}, bf16[24,3072]{1,0:T(8,128)(2,1)S(1)}, u32[]{:S(2)}, u32[]{:S(2)}) collective-permute-start(bf16[24,3072]{1,0:T(8,128)(2,1)S(1)} %slice.63), channel_id=1, source_target_pairs={{0,4},{2,6},{4,0},{6,2},{1,5},{3,7},{5,1},{7,3},{8,12},{10,14},{12... | collective-permute-start | bytes 442376 | tf_op jit(solution)/shard_map/ppermute | solution.py:23
  44.9 12.0 %collective-permute-start.28 = (bf16[24,3072]{1,0:T(8,128)(2,1)S(1)}, bf16[24,3072]{1,0:T(8,128)(2,1)S(1)}, u32[]{:S(2)}, u32[]{:S(2)}) collective-permute-start(bf16[24,3072]{1,0:T(8,128)(2,1)S(1)} %slice.62), channel_id=1, source_target_pairs={{0,4},{2,6},{4,0},{6,2},{1,5},{3,7},{5,1},{7,3},{8,12},{10,14},{12... | collective-permute-start | bytes 442376 | tf_op jit(solution)/shard_map/ppermute | solution.py:23
  48.0 8.9 %collective-permute-start.20 = (bf16[24,3072]{1,0:T(8,128)(2,1)S(1)}, bf16[24,3072]{1,0:T(8,128)(2,1)S(1)}, u32[]{:S(2)}, u32[]{:S(2)}) collective-permute-start(bf16[24,3072]{1,0:T(8,128)(2,1)S(1)} %fusion.4), channel_id=1, source_target_pairs={{0,24},{8,16},{16,8},{24,0},{1,25},{9,17},{17,9},{25,1},{2,26},{10... | collective-permute-start | bytes 442376 | tf_op jit(solution)/shard_map/ppermute | solution.py:23
  51.2 11.0 %collective-permute-start.23 = (bf16[24,3072]{1,0:T(8,128)(2,1)S(1)}, bf16[24,3072]{1,0:T(8,128)(2,1)S(1)}, u32[]{:S(2)}, u32[]{:S(2)}) collective-permute-start(bf16[24,3072]{1,0:T(8,128)(2,1)S(1)} %fusion.3), channel_id=1, source_target_pairs={{0,16},{8,24},{16,0},{24,8},{1,17},{9,25},{17,1},{25,9},{2,18},{10... | collective-permute-start | bytes 442376 | tf_op jit(solution)/shard_map/ppermute | solution.py:23
  54.3 8.3 %collective-permute-start.26 = (bf16[24,3072]{1,0:T(8,128)(2,1)S(1)}, bf16[24,3072]{1,0:T(8,128)(2,1)S(1)}, u32[]{:S(2)}, u32[]{:S(2)}) collective-permute-start(bf16[24,3072]{1,0:T(8,128)(2,1)S(1)} %fusion.2), channel_id=1, source_target_pairs={{0,8},{8,0},{16,24},{24,16},{1,9},{9,1},{17,25},{25,17},{2,10},{10... | collective-permute-start | bytes 442376 | tf_op jit(solution)/shard_map/ppermute | solution.py:23
  (5 other events, 8.2 us)

commit v3 on v2

--- a/solution.py
+++ b/solution.py
@@ -181,7 +181,7 @@
     kept, sent, refs = refs[: len(group)], refs[len(group) : 2 * len(group)], refs[2 * len(group) :]
     if 0 in group:
         own_ref, *refs, split_ref = refs
-    hidden_ref, share_ref, gain_ref, w_in_ref, w_out_ref, sems = refs
+    hidden_ref, share_ref, gain_ref, w_in_ref, w_out_ref, sum_ref, sems = refs
     place = place_ref[0]
     block_len, token_count = marked[0].shape[0] - 16, hidden_ref.shape[1]
     part_width = marked[0].shape[1]
@@ -195,8 +195,16 @@
         pltpu.make_async_copy(w_in_hbm.at[0, rows_of(j)], w_in_ref.at[j], sems.at[j])
         for j in range(exp_count)
     ]
-    reads.append(pltpu.make_async_copy(w_out_hbm.at[0], w_out_ref, sems.at[exp_count]))
-    reads.insert(0, pltpu.make_async_copy(gain_hbm, gain_ref, sems.at[exp_count + 1]))
+    depth = hidden_ref.shape[2] // 2
+    reads += [
+        pltpu.make_async_copy(
+            w_out_hbm.at[0, i * depth : (i + 1) * depth],
+            w_out_ref.at[i * depth : (i + 1) * depth],
+            sems.at[exp_count + i],
+        )
+        for i in range(2)
+    ]
+    reads.insert(0, pltpu.make_async_copy(gain_hbm, gain_ref, sems.at[exp_count + 2]))
     for read in reads:
         read.start()
 
@@ -243,15 +251,26 @@
         [hidden_ref[i * exp_count + (place ^ j)] for i in range(len(group)) for j in order], axis=0
     ).astype(jnp.bfloat16)
     half = block_len // 2
+    tiles = [slice(start, start + part_width) for start in range(0, width, part_width)]
     reads[1 + exp_count].wait()
-    for start in range(0, width, part_width):
-        columns = slice(start, start + part_width)
-        product = jnp.dot(hidden, w_out_ref[:, columns], preferred_element_type=jnp.float32)
+    for columns in tiles:
+        sum_ref[:, columns] = jnp.dot(
+            hidden[:, :depth], w_out_ref[:depth, columns], preferred_element_type=jnp.float32
+        )
+    reads[2 + exp_count].wait()
+    for columns in tiles:
+        product = sum_ref[:, columns] + jnp.dot(
+            hidden[:, depth:], w_out_ref[depth:, columns], preferred_element_type=jnp.float32
+        )
         product = (product * weight).astype(jnp.bfloat16)
         for i in range(len(group)):
             low = i * block_len
             kept[i][:, columns] = product[low : low + half]
             sent[i][:, columns] = product[low + half : low + block_len]
+
+
+def after(value, *others):
+    return lax.optimization_barrier((value, *others))[0]
 
 
 def vmem():
@@ -311,16 +330,20 @@
         name="attend",
     )(seq_index.reshape(1), heads, doc_ids.reshape(1, -1), *packs)
 
-    first = [seq_count - 1, 1]
-    second = [d for d in range(seq_count - 2, -1, -1) if d not in first]
-    blocks = {(d, 0): flipped(attended, "seq", d) for d in first}
+    first, second = [3, 1], [2, 0]
+    far_bit = exp_count // 2
+    blocks = {(d, 0): flipped(attended, "seq", d) for d in [3, 1, 2]}
     blocks[0, 0] = marked
-    blocks |= {(d, 0): flipped(attended, "seq", d) for d in second if d}
-    bit = exp_count // 2
-    while bit:
-        blocks |= {(d, j ^ bit): flipped(block, "exp", bit) for (d, j), block in blocks.items()}
-        bit //= 2
-
+
+    def spread(d, bit):
+        for j in range(0, exp_count, 2 * bit):
+            blocks[d, j ^ bit] = flipped(blocks[d, j], "exp", bit)
+
+    for d in [0, 3, 1, 2]:
+        spread(d, 2)
+        blocks[d, 1], blocks[d, 3] = flipped(blocks[d, 0], "exp", 1), flipped(blocks[d, 2], "exp", 1)
+    blocks[3, 2] = after(blocks[3, 2], blocks[2, 0])
+    blocks[3, 3] = flipped(blocks[3, 2], 'exp', 1)
     order = [j for j in range(exp_count) if not j & 1] + [j for j in range(exp_count) if j & 1]
     gain = norm_gain.reshape(exp_count, 1, part_width)
     weights = [pltpu.with_memory_space_constraint(w, pltpu.HBM) for w in (gain, w_in, w_out)]
@@ -336,7 +359,8 @@
             pltpu.VMEM((exp_count, 1, part_width), jnp.float32),
             pltpu.VMEM((exp_count, part_width, hidden_width), jnp.bfloat16),
             pltpu.VMEM((hidden_width, width), jnp.bfloat16),
-            pltpu.SemaphoreType.DMA((exp_count + 2,)),
+            pltpu.VMEM((size * block_len, width), jnp.float32),
+            pltpu.SemaphoreType.DMA((exp_count + 3,)),
         ]
         if 0 in group:
             split = (exp_count, token_count, part_width)
@@ -367,13 +391,21 @@
             sums[d] = both[:token_count], both[token_count:].astype(jnp.bfloat16)
         return sums
 
-    early, _ = experts(first)
+    early, own_e = experts(first)
+    early[3], early[1] = [(kept, after(sent, blocks[2, 2])) for kept, sent in (early[3], early[1])]
     early = send(early)
-    late, own = experts(second)
+    blocks[2, 3] = after(blocks[2, 3], early[3][1])
+    late, own_l = experts(second)
+    own = own_e if 0 in first else own_l
     late = send(late)
     total = jnp.transpose(own, (1, 0, 2)).reshape(token_count, width).astype(jnp.float32)
     for d, (mine, away) in sorted((early | late).items(), reverse=True):
-        mine = mine + flipped(away, "exp", 2).astype(jnp.float32)
+        if d == 1:
+            away = after(away, late[2][1])
+        came = flipped(away, "exp", 2)
+        if d == 3:
+            came3 = came
+        mine = mine + came.astype(jnp.float32)
         if d:
             mine = flipped(mine.astype(jnp.bfloat16), "seq", d).astype(jnp.float32)
         total = total + mine

time: 63.7 us -> 61.5 us (0.965)
  waiting for transfers between devices: 26.3 us -> 21.3 us
  starting transfers between devices: 24.2 us -> 27.5 us
    ppermute x29, waiting for transfers between devices: 26.3 us -> 21.3 us  [flipped(): lax.ppermute(x, axis, [(i, i ^ by) for i in range(lax.axis_size(axis))])]
    ppermute x29, starting transfers between devices: 24.2 us -> 27.5 us  [flipped(): lax.ppermute(x, axis, [(i, i ^ by) for i in range(lax.axis_size(axis))])]
  transfers between devices with their start and end apart: 29 -> 29, of which waited for: 15 -> 12; matrix products, arithmetic and copies ran while one was open for 3% -> 3% of each run, Pallas kernels for 12% -> 12%
where the time goes in v3:
time: 61.5 us; the launch traced here: 61.2 us
  starting transfers between devices  27.5 us (45%)
  waiting for transfers between devices  21.3 us (35%)
  Pallas kernels  7.88 us (13%)
  other arithmetic  3.55 us (6%)
  local copies, waits for them, and re-layouts  0.78 us (1%)
    ppermute x29, starting transfers between devices, flipped(): lax.ppermute(x, axis, [(i, i ^ by) for i in range(lax.axis_size(axis))])  27.5 us
    ppermute x29, waiting for transfers between devices, flipped(): lax.ppermute(x, axis, [(i, i ^ by) for i in range(lax.axis_size(axis))])  21.3 us
    pallas_call x2, Pallas kernels, experts(): pl.pallas_call(functools.partial(experts_kernel, seq_count, group, order)...  7.13 us
  transfers between devices with their start and end apart: 29, of which 12 were waited for; matrix products, arithmetic and copies ran while one was open for 3% of the time, Pallas kernels for 12%

profile of v3, /device:TPU:0, one launch (start us, length us, event | category | flops | bytes accessed | tf_op | source)
XLA Modules:
  0.0 61.2 jit_solution(3383718577457472885)
XLA Ops:
  1.5 3.0 %collective-permute-start = (bf16[208,128]{1,0:T(8,128)(2,1)S(1)}, bf16[208,128]{1,0:T(8,128)(2,1)S(1)}, u32[]{:S(2)}, u32[]{:S(2)}) collective-permute-start(bf16[208,128]{1,0:T(8,128)(2,1)S(1)} %pad_maximum_fusion.refs_3_), channel_id=1, source_target_pairs={{0,8},{8,0},{16,24},{24,16},{1,9},{9,1},{17,25},{25,17},{2,10},{10... | collective-permute-start | bytes 159752 | tf_op jit(solution)/shard_map/ppermute | solution.py:23
  4.5 2.6 %collective-permute-start.1 = (bf16[208,128]{1,0:T(8,128)(2,1)S(1)}, bf16[208,128]{1,0:T(8,128)(2,1)S(1)}, u32[]{:S(2)}, u32[]{:S(2)}) collective-permute-start(bf16[208,128]{1,0:T(8,128)(2,1)S(1)} %pad_maximum_fusion.refs_3_), channel_id=1, source_target_pairs={{0,16},{8,24},{16,0},{24,8},{1,17},{9,25},{17,1},{25,9},{2,18},{10... | collective-permute-start | bytes 159752 | tf_op jit(solution)/shard_map/ppermute | solution.py:23
  8.7 1.8 %collective-permute-done.1.refs_5_ = bf16[208,128]{1,0:T(8,128)(2,1)S(1)} collective-permute-done((bf16[208,128]{1,0:T(8,128)(2,1)S(1)}, bf16[208,128]{1,0:T(8,128)(2,1)S(1)}, u32[]{:S(2)}, u32[]{:S(2)}) %collective-permute-start.1) | collective-permute-done | bytes 53280 | tf_op jit(solution)/shard_map/ppermute | solution.py:23
  10.6 2.5 %collective-permute-done.2.refs_6_ = bf16[208,128]{1,0:T(8,128)(2,1)S(1)} collective-permute-done((bf16[208,128]{1,0:T(8,128)(2,1)S(1)}, bf16[208,128]{1,0:T(8,128)(2,1)S(1)}, u32[]{:S(2)}, u32[]{:S(2)}) %collective-permute-start.2) | collective-permute-done | bytes 53280 | tf_op jit(solution)/shard_map/ppermute | solution.py:23
  13.8 1.1 %collective-permute-start.10 = (bf16[96,768]{1,0:T(8,128)(2,1)S(1)}, bf16[96,768]{1,0:T(8,128)(2,1)S(1)}, u32[]{:S(2)}, u32[]{:S(2)}) collective-permute-start(bf16[96,768]{1,0:T(8,128)(2,1)S(1)} %get-tuple-element.26), channel_id=1, source_target_pairs={{0,24},{8,16},{16,8},{24,0},{1,25},{9,17},{17,9},{25,1},{2,26},{10... | collective-permute-start | bytes 442376 | tf_op jit(solution)/shard_map/ppermute | solution.py:23
  15.1 1.5 %collective-permute-start.4 = (bf16[112,768]{1,0:T(8,128)(2,1)S(1)}, bf16[112,768]{1,0:T(8,128)(2,1)S(1)}, u32[]{:S(2)}, u32[]{:S(2)}) collective-permute-start(bf16[112,768]{1,0:T(8,128)(2,1)S(1)} %get-tuple-element.25.refs_4_), channel_id=1, source_target_pairs={{0,4},{2,6},{4,0},{6,2},{1,5},{3,7},{5,1},{7,3},{8,12},{10,14},{12... | collective-permute-start | bytes 516104 | tf_op jit(solution)/shard_map/ppermute | solution.py:23
  16.6 3.2 %collective-permute-start.6 = (bf16[96,768]{1,0:T(8,128)(2,1)S(1)}, bf16[96,768]{1,0:T(8,128)(2,1)S(1)}, u32[]{:S(2)}, u32[]{:S(2)}) collective-permute-start(bf16[96,768]{1,0:T(8,128)(2,1)S(1)} %get-tuple-element.26), channel_id=1, source_target_pairs={{0,16},{8,24},{16,0},{24,8},{1,17},{9,25},{17,1},{25,9},{2,18},{10... | collective-permute-start | bytes 442376 | tf_op jit(solution)/shard_map/ppermute | solution.py:23
  19.8 2.8 %collective-permute-done.10.refs_8_ = bf16[96,768]{1,0:T(8,128)(2,1)S(1)} collective-permute-done((bf16[96,768]{1,0:T(8,128)(2,1)S(1)}, bf16[96,768]{1,0:T(8,128)(2,1)S(1)}, u32[]{:S(2)}, u32[]{:S(2)}) %collective-permute-start.10) | collective-permute-done | bytes 147488 | tf_op jit(solution)/shard_map/ppermute | solution.py:23
  22.5 1.5 %collective-permute-start.12 = (bf16[96,768]{1,0:T(8,128)(2,1)S(1)}, bf16[96,768]{1,0:T(8,128)(2,1)S(1)}, u32[]{:S(2)}, u32[]{:S(2)}) collective-permute-start(bf16[96,768]{1,0:T(8,128)(2,1)S(1)} %collective-permute-done.10.refs_8_), channel_id=1, source_target_pairs={{0,4},{2,6},{4,0},{6,2},{1,5},{3,7},{5,1},{7,3},{8,12},{10,14},{12... | collective-permute-start | bytes 442376 | tf_op jit(solution)/shard_map/ppermute | solution.py:23
  24.6 2.6 %collective-permute-done.6.refs_8_ = bf16[96,768]{1,0:T(8,128)(2,1)S(1)} collective-permute-done((bf16[96,768]{1,0:T(8,128)(2,1)S(1)}, bf16[96,768]{1,0:T(8,128)(2,1)S(1)}, u32[]{:S(2)}, u32[]{:S(2)}) %collective-permute-start.6) | collective-permute-done | bytes 147488 | tf_op jit(solution)/shard_map/ppermute | solution.py:23
  28.2 1.1 %collective-permute-done.16.refs_14_ = bf16[96,768]{1,0:T(8,128)(2,1)S(1)} collective-permute-done((bf16[96,768]{1,0:T(8,128)(2,1)S(1)}, bf16[96,768]{1,0:T(8,128)(2,1)S(1)}, u32[]{:S(2)}, u32[]{:S(2)}) %collective-permute-start.16) | collective-permute-done | bytes 147488 | tf_op jit(solution)/shard_map/ppermute | solution.py:23
  29.3 1.5 %collective-permute-start.8 = (bf16[96,768]{1,0:T(8,128)(2,1)S(1)}, bf16[96,768]{1,0:T(8,128)(2,1)S(1)}, u32[]{:S(2)}, u32[]{:S(2)}) collective-permute-start(bf16[96,768]{1,0:T(8,128)(2,1)S(1)} %collective-permute-done.6.refs_8_), channel_id=1, source_target_pairs={{0,4},{2,6},{4,0},{6,2},{1,5},{3,7},{5,1},{7,3},{8,12},{10,14},{12... | collective-permute-start | bytes 442376 | tf_op jit(solution)/shard_map/ppermute | solution.py:23
  30.8 3.5 %experts.2 = (bf16[48,3072]{1,0:T(8,128)(2,1)S(1)}, bf16[48,3072]{1,0:T(8,128)(2,1)S(1)}, bf16[48,3072]{1,0:T(8,128)(2,1)S(1)}, bf16[48,3072]{1,0:T(8,128)(2,1)S(1)}) custom-call(s32[1]{0:T(128)} %bitcast.refs_0_, f32[4,1,768]{2,1,0:T(1,128)} %bitcast.19, bf16[1,3072,512]{2,1,0:T(8,128)(2,1)} %refs_2_.3, bf16[1,512,3072]{2,1,0:T(8,128)(2,1)} %refs_3_.3, ...), custom_call_target="tpu_custom_call" | custom-call | flops 1207959552 | bytes 8388608 | tf_op jit(solution)/shard_map/experts/pallas_call | solution.py:371
  34.3 1.2 %collective-permute-done.8.refs_10_ = bf16[96,768]{1,0:T(8,128)(2,1)S(1)} collective-permute-done((bf16[96,768]{1,0:T(8,128)(2,1)S(1)}, bf16[96,768]{1,0:T(8,128)(2,1)S(1)}, u32[]{:S(2)}, u32[]{:S(2)}) %collective-permute-start.8) | collective-permute-done | bytes 147488 | tf_op jit(solution)/shard_map/ppermute | solution.py:23
  37.2 1.6 %collective-permute-start.19 = (bf16[24,3072]{1,0:T(8,128)(2,1)S(1)}, bf16[24,3072]{1,0:T(8,128)(2,1)S(1)}, u32[]{:S(2)}, u32[]{:S(2)}) collective-permute-start(bf16[24,3072]{1,0:T(8,128)(2,1)S(1)} %slice.65), channel_id=1, source_target_pairs={{0,4},{2,6},{4,0},{6,2},{1,5},{3,7},{5,1},{7,3},{8,12},{10,14},{12... | collective-permute-start | bytes 442376 | tf_op jit(solution)/shard_map/ppermute | solution.py:23
  38.8 3.6 %experts.3 = (bf16[48,3072]{1,0:T(8,128)(2,1)S(1)}, bf16[48,3072]{1,0:T(8,128)(2,1)S(1)}, bf16[48,3072]{1,0:T(8,128)(2,1)S(1)}, bf16[48,3072]{1,0:T(8,128)(2,1)S(1)}, bf16[4,24,768]{2,1,0:T(8,128)(2,1)S(1)}) custom-call(s32[1]{0:T(128)} %bitcast.refs_0_, f32[4,1,768]{2,1,0:T(1,128)} %bitcast.20, bf16[1,3072,512]{2,1,0:T(8,128)(2,1)} %refs_2_.3, ...), custom_call_target="tpu_custom_call" | custom-call | flops 1207959552 | bytes 8388608 | tf_op jit(solution)/shard_map/experts/pallas_call | solution.py:371
  43.2 1.0 %collective-permute-start.20 = (bf16[24,3072]{1,0:T(8,128)(2,1)S(1)}, bf16[24,3072]{1,0:T(8,128)(2,1)S(1)}, u32[]{:S(2)}, u32[]{:S(2)}) collective-permute-start(bf16[24,3072]{1,0:T(8,128)(2,1)S(1)} %fusion.4), channel_id=1, source_target_pairs={{0,24},{8,16},{16,8},{24,0},{1,25},{9,17},{17,9},{25,1},{2,26},{10... | collective-permute-start | bytes 442376 | tf_op jit(solution)/shard_map/ppermute | solution.py:23
  44.3 1.6 %collective-permute-start.22 = (bf16[24,3072]{1,0:T(8,128)(2,1)S(1)}, bf16[24,3072]{1,0:T(8,128)(2,1)S(1)}, u32[]{:S(2)}, u32[]{:S(2)}) collective-permute-start(bf16[24,3072]{1,0:T(8,128)(2,1)S(1)} %slice.64), channel_id=1, source_target_pairs={{0,4},{2,6},{4,0},{6,2},{1,5},{3,7},{5,1},{7,3},{8,12},{10,14},{12... | collective-permute-start | bytes 442376 | tf_op jit(solution)/shard_map/ppermute | solution.py:23
  46.5 1.6 %collective-permute-start.28 = (bf16[24,3072]{1,0:T(8,128)(2,1)S(1)}, bf16[24,3072]{1,0:T(8,128)(2,1)S(1)}, u32[]{:S(2)}, u32[]{:S(2)}) collective-permute-start(bf16[24,3072]{1,0:T(8,128)(2,1)S(1)} %slice.62), channel_id=1, source_target_pairs={{0,4},{2,6},{4,0},{6,2},{1,5},{3,7},{5,1},{7,3},{8,12},{10,14},{12... | collective-permute-start | bytes 442376 | tf_op jit(solution)/shard_map/ppermute | solution.py:23
  48.1 3.0 %collective-permute-done.22 = bf16[24,3072]{1,0:T(8,128)(2,1)S(1)} collective-permute-done((bf16[24,3072]{1,0:T(8,128)(2,1)S(1)}, bf16[24,3072]{1,0:T(8,128)(2,1)S(1)}, u32[]{:S(2)}, u32[]{:S(2)}) %collective-permute-start.22) | collective-permute-done | bytes 147488 | tf_op jit(solution)/shard_map/ppermute | solution.py:23
  51.1 2.1 %collective-permute-start.23 = (bf16[24,3072]{1,0:T(8,128)(2,1)S(1)}, bf16[24,3072]{1,0:T(8,128)(2,1)S(1)}, u32[]{:S(2)}, u32[]{:S(2)}) collective-permute-start(bf16[24,3072]{1,0:T(8,128)(2,1)S(1)} %fusion.3), channel_id=1, source_target_pairs={{0,16},{8,24},{16,0},{24,8},{1,17},{9,25},{17,1},{25,9},{2,18},{10... | collective-permute-start | bytes 442376 | tf_op jit(solution)/shard_map/ppermute | solution.py:23
  53.3 1.0 %collective-permute-done.25 = bf16[24,3072]{1,0:T(8,128)(2,1)S(1)} collective-permute-done((bf16[24,3072]{1,0:T(8,128)(2,1)S(1)}, bf16[24,3072]{1,0:T(8,128)(2,1)S(1)}, u32[]{:S(2)}, u32[]{:S(2)}) %collective-permute-start.25) | collective-permute-done | bytes 147488 | tf_op jit(solution)/shard_map/ppermute | solution.py:23
  54.3 1.4 %collective-permute-start.26 = (bf16[24,3072]{1,0:T(8,128)(2,1)S(1)}, bf16[24,3072]{1,0:T(8,128)(2,1)S(1)}, u32[]{:S(2)}, u32[]{:S(2)}) collective-permute-start(bf16[24,3072]{1,0:T(8,128)(2,1)S(1)} %fusion.2), channel_id=1, source_target_pairs={{0,8},{8,0},{16,24},{24,16},{1,9},{9,1},{17,25},{25,17},{2,10},{10... | collective-permute-start | bytes 442376 | tf_op jit(solution)/shard_map/ppermute | solution.py:23
  56.4 3.1 %collective-permute-done.23 = bf16[24,3072]{1,0:T(8,128)(2,1)S(1)} collective-permute-done((bf16[24,3072]{1,0:T(8,128)(2,1)S(1)}, bf16[24,3072]{1,0:T(8,128)(2,1)S(1)}, u32[]{:S(2)}, u32[]{:S(2)}) %collective-permute-start.23) | collective-permute-done | bytes 147488 | tf_op jit(solution)/shard_map/ppermute | solution.py:23
  (57 shorter events, 11.3 us)
Async XLA Ops:
  1.5 7.2 %collective-permute-start = (bf16[208,128]{1,0:T(8,128)(2,1)S(1)}, bf16[208,128]{1,0:T(8,128)(2,1)S(1)}, u32[]{:S(2)}, u32[]{:S(2)}) collective-permute-start(bf16[208,128]{1,0:T(8,128)(2,1)S(1)} %pad_maximum_fusion.refs_3_), channel_id=1, source_target_pairs={{0,8},{8,0},{16,24},{24,16},{1,9},{9,1},{17,25},{25,17},{2,10},{10... | collective-permute-start | bytes 159752 | tf_op jit(solution)/shard_map/ppermute | solution.py:23
  4.5 6.1 %collective-permute-start.1 = (bf16[208,128]{1,0:T(8,128)(2,1)S(1)}, bf16[208,128]{1,0:T(8,128)(2,1)S(1)}, u32[]{:S(2)}, u32[]{:S(2)}) collective-permute-start(bf16[208,128]{1,0:T(8,128)(2,1)S(1)} %pad_maximum_fusion.refs_3_), channel_id=1, source_target_pairs={{0,16},{8,24},{16,0},{24,8},{1,17},{9,25},{17,1},{25,9},{2,18},{10... | collective-permute-start | bytes 159752 | tf_op jit(solution)/shard_map/ppermute | solution.py:23
  7.1 5.9 %collective-permute-start.2 = (bf16[208,128]{1,0:T(8,128)(2,1)S(1)}, bf16[208,128]{1,0:T(8,128)(2,1)S(1)}, u32[]{:S(2)}, u32[]{:S(2)}) collective-permute-start(bf16[208,128]{1,0:T(8,128)(2,1)S(1)} %pad_maximum_fusion.refs_3_), channel_id=1, source_target_pairs={{0,24},{8,16},{16,8},{24,0},{1,25},{9,17},{17,9},{25,1},{2,26},{10... | collective-permute-start | bytes 159752 | tf_op jit(solution)/shard_map/ppermute | solution.py:23
  13.8 8.7 %collective-permute-start.10 = (bf16[96,768]{1,0:T(8,128)(2,1)S(1)}, bf16[96,768]{1,0:T(8,128)(2,1)S(1)}, u32[]{:S(2)}, u32[]{:S(2)}) collective-permute-start(bf16[96,768]{1,0:T(8,128)(2,1)S(1)} %get-tuple-element.26), channel_id=1, source_target_pairs={{0,24},{8,16},{16,8},{24,0},{1,25},{9,17},{17,9},{25,1},{2,26},{10... | collective-permute-start | bytes 442376 | tf_op jit(solution)/shard_map/ppermute | solution.py:23
  14.9 9.2 %collective-permute-start.14 = (bf16[96,768]{1,0:T(8,128)(2,1)S(1)}, bf16[96,768]{1,0:T(8,128)(2,1)S(1)}, u32[]{:S(2)}, u32[]{:S(2)}) collective-permute-start(bf16[96,768]{1,0:T(8,128)(2,1)S(1)} %get-tuple-element.26), channel_id=1, source_target_pairs={{0,8},{8,0},{16,24},{24,16},{1,9},{9,1},{17,25},{25,17},{2,10},{10... | collective-permute-start | bytes 442376 | tf_op jit(solution)/shard_map/ppermute | solution.py:23
  15.1 12.1 %collective-permute-start.4 = (bf16[112,768]{1,0:T(8,128)(2,1)S(1)}, bf16[112,768]{1,0:T(8,128)(2,1)S(1)}, u32[]{:S(2)}, u32[]{:S(2)}) collective-permute-start(bf16[112,768]{1,0:T(8,128)(2,1)S(1)} %get-tuple-element.25.refs_4_), channel_id=1, source_target_pairs={{0,4},{2,6},{4,0},{6,2},{1,5},{3,7},{5,1},{7,3},{8,12},{10,14},{12... | collective-permute-start | bytes 516104 | tf_op jit(solution)/shard_map/ppermute | solution.py:23
  16.6 10.6 %collective-permute-start.6 = (bf16[96,768]{1,0:T(8,128)(2,1)S(1)}, bf16[96,768]{1,0:T(8,128)(2,1)S(1)}, u32[]{:S(2)}, u32[]{:S(2)}) collective-permute-start(bf16[96,768]{1,0:T(8,128)(2,1)S(1)} %get-tuple-element.26), channel_id=1, source_target_pairs={{0,16},{8,24},{16,0},{24,8},{1,17},{9,25},{17,1},{25,9},{2,18},{10... | collective-permute-start | bytes 442376 | tf_op jit(solution)/shard_map/ppermute | solution.py:23
  19.7 8.0 %collective-permute-start.3 = (bf16[112,768]{1,0:T(8,128)(2,1)S(1)}, bf16[112,768]{1,0:T(8,128)(2,1)S(1)}, u32[]{:S(2)}, u32[]{:S(2)}) collective-permute-start(bf16[112,768]{1,0:T(8,128)(2,1)S(1)} %get-tuple-element.25.refs_4_), channel_id=1, source_target_pairs={{0,2},{2,0},{4,6},{6,4},{1,3},{3,1},{5,7},{7,5},{8,10},{10,8},{12,... | collective-permute-start | bytes 516104 | tf_op jit(solution)/shard_map/ppermute | solution.py:23
  22.5 5.1 %collective-permute-start.12 = (bf16[96,768]{1,0:T(8,128)(2,1)S(1)}, bf16[96,768]{1,0:T(8,128)(2,1)S(1)}, u32[]{:S(2)}, u32[]{:S(2)}) collective-permute-start(bf16[96,768]{1,0:T(8,128)(2,1)S(1)} %collective-permute-done.10.refs_8_), channel_id=1, source_target_pairs={{0,4},{2,6},{4,0},{6,2},{1,5},{3,7},{5,1},{7,3},{8,12},{10,14},{12... | collective-permute-start | bytes 442376 | tf_op jit(solution)/shard_map/ppermute | solution.py:23
  24.0 5.2 %collective-permute-start.16 = (bf16[96,768]{1,0:T(8,128)(2,1)S(1)}, bf16[96,768]{1,0:T(8,128)(2,1)S(1)}, u32[]{:S(2)}, u32[]{:S(2)}) collective-permute-start(bf16[96,768]{1,0:T(8,128)(2,1)S(1)} %collective-permute-done.14.refs_12_), channel_id=1, source_target_pairs={{0,4},{2,6},{4,0},{6,2},{1,5},{3,7},{5,1},{7,3},{8,12},{10,14},{12... | collective-permute-start | bytes 442376 | tf_op jit(solution)/shard_map/ppermute | solution.py:23
  27.2 3.6 %collective-permute-start.5 = (bf16[112,768]{1,0:T(8,128)(2,1)S(1)}, bf16[112,768]{1,0:T(8,128)(2,1)S(1)}, u32[]{:S(2)}, u32[]{:S(2)}) collective-permute-start(bf16[112,768]{1,0:T(8,128)(2,1)S(1)} %collective-permute-done.4.refs_6_), channel_id=1, source_target_pairs={{0,2},{2,0},{4,6},{6,4},{1,3},{3,1},{5,7},{7,5},{8,10},{10,8},{12,... | collective-permute-start | bytes 516104 | tf_op jit(solution)/shard_map/ppermute | solution.py:23
  27.7 3.1 %collective-permute-start.15 = (bf16[96,768]{1,0:T(8,128)(2,1)S(1)}, bf16[96,768]{1,0:T(8,128)(2,1)S(1)}, u32[]{:S(2)}, u32[]{:S(2)}) collective-permute-start(bf16[96,768]{1,0:T(8,128)(2,1)S(1)} %collective-permute-done.14.refs_12_), channel_id=1, source_target_pairs={{0,2},{2,0},{4,6},{6,4},{1,3},{3,1},{5,7},{7,5},{8,10},{10,8},{12,... | collective-permute-start | bytes 442376 | tf_op jit(solution)/shard_map/ppermute | solution.py:23
  27.8 3.0 %collective-permute-start.13 = (bf16[96,768]{1,0:T(8,128)(2,1)S(1)}, bf16[96,768]{1,0:T(8,128)(2,1)S(1)}, u32[]{:S(2)}, u32[]{:S(2)}) collective-permute-start(bf16[96,768]{1,0:T(8,128)(2,1)S(1)} %collective-permute-done.12.refs_10_), channel_id=1, source_target_pairs={{0,2},{2,0},{4,6},{6,4},{1,3},{3,1},{5,7},{7,5},{8,10},{10,8},{12,... | collective-permute-start | bytes 442376 | tf_op jit(solution)/shard_map/ppermute | solution.py:23
  29.3 6.3 %collective-permute-start.8 = (bf16[96,768]{1,0:T(8,128)(2,1)S(1)}, bf16[96,768]{1,0:T(8,128)(2,1)S(1)}, u32[]{:S(2)}, u32[]{:S(2)}) collective-permute-start(bf16[96,768]{1,0:T(8,128)(2,1)S(1)} %collective-permute-done.6.refs_8_), channel_id=1, source_target_pairs={{0,4},{2,6},{4,0},{6,2},{1,5},{3,7},{5,1},{7,3},{8,12},{10,14},{12... | collective-permute-start | bytes 442376 | tf_op jit(solution)/shard_map/ppermute | solution.py:23
  35.5 3.2 %collective-permute-start.7 = (bf16[96,768]{1,0:T(8,128)(2,1)S(1)}, bf16[96,768]{1,0:T(8,128)(2,1)S(1)}, u32[]{:S(2)}, u32[]{:S(2)}) collective-permute-start(bf16[96,768]{1,0:T(8,128)(2,1)S(1)} %collective-permute-done.6.refs_8_), channel_id=1, source_target_pairs={{0,2},{2,0},{4,6},{6,4},{1,3},{3,1},{5,7},{7,5},{8,10},{10,8},{12,... | collective-permute-start | bytes 442376 | tf_op jit(solution)/shard_map/ppermute | solution.py:23
  36.1 6.4 %collective-permute-start.24 = (bf16[48,3072]{1,0:T(8,128)(2,1)S(1)}, bf16[48,3072]{1,0:T(8,128)(2,1)S(1)}, u32[]{:S(2)}, u32[]{:S(2)}) collective-permute-start(bf16[48,3072]{1,0:T(8,128)(2,1)S(1)} %get-tuple-element.37), channel_id=1, source_target_pairs={{0,2},{2,0},{4,6},{6,4},{1,3},{3,1},{5,7},{7,5},{8,10},{10,8},{12,... | collective-permute-start | bytes 884744 | tf_op jit(solution)/shard_map/ppermute | solution.py:23
  37.2 6.0 %collective-permute-start.19 = (bf16[24,3072]{1,0:T(8,128)(2,1)S(1)}, bf16[24,3072]{1,0:T(8,128)(2,1)S(1)}, u32[]{:S(2)}, u32[]{:S(2)}) collective-permute-start(bf16[24,3072]{1,0:T(8,128)(2,1)S(1)} %slice.65), channel_id=1, source_target_pairs={{0,4},{2,6},{4,0},{6,2},{1,5},{3,7},{5,1},{7,3},{8,12},{10,14},{12... | collective-permute-start | bytes 442376 | tf_op jit(solution)/shard_map/ppermute | solution.py:23
  42.6 3.8 %collective-permute-start.27 = (bf16[48,3072]{1,0:T(8,128)(2,1)S(1)}, bf16[48,3072]{1,0:T(8,128)(2,1)S(1)}, u32[]{:S(2)}, u32[]{:S(2)}) collective-permute-start(bf16[48,3072]{1,0:T(8,128)(2,1)S(1)} %get-tuple-element.40), channel_id=1, source_target_pairs={{0,2},{2,0},{4,6},{6,4},{1,3},{3,1},{5,7},{7,5},{8,10},{10,8},{12,... | collective-permute-start | bytes 884744 | tf_op jit(solution)/shard_map/ppermute | solution.py:23
  43.2 12.6 %collective-permute-start.20 = (bf16[24,3072]{1,0:T(8,128)(2,1)S(1)}, bf16[24,3072]{1,0:T(8,128)(2,1)S(1)}, u32[]{:S(2)}, u32[]{:S(2)}) collective-permute-start(bf16[24,3072]{1,0:T(8,128)(2,1)S(1)} %fusion.4), channel_id=1, source_target_pairs={{0,24},{8,16},{16,8},{24,0},{1,25},{9,17},{17,9},{25,1},{2,26},{10... | collective-permute-start | bytes 442376 | tf_op jit(solution)/shard_map/ppermute | solution.py:23
  44.3 6.8 %collective-permute-start.22 = (bf16[24,3072]{1,0:T(8,128)(2,1)S(1)}, bf16[24,3072]{1,0:T(8,128)(2,1)S(1)}, u32[]{:S(2)}, u32[]{:S(2)}) collective-permute-start(bf16[24,3072]{1,0:T(8,128)(2,1)S(1)} %slice.64), channel_id=1, source_target_pairs={{0,4},{2,6},{4,0},{6,2},{1,5},{3,7},{5,1},{7,3},{8,12},{10,14},{12... | collective-permute-start | bytes 442376 | tf_op jit(solution)/shard_map/ppermute | solution.py:23
  45.9 8.3 %collective-permute-start.25 = (bf16[24,3072]{1,0:T(8,128)(2,1)S(1)}, bf16[24,3072]{1,0:T(8,128)(2,1)S(1)}, u32[]{:S(2)}, u32[]{:S(2)}) collective-permute-start(bf16[24,3072]{1,0:T(8,128)(2,1)S(1)} %slice.63), channel_id=1, source_target_pairs={{0,4},{2,6},{4,0},{6,2},{1,5},{3,7},{5,1},{7,3},{8,12},{10,14},{12... | collective-permute-start | bytes 442376 | tf_op jit(solution)/shard_map/ppermute | solution.py:23
  46.5 9.9 %collective-permute-start.28 = (bf16[24,3072]{1,0:T(8,128)(2,1)S(1)}, bf16[24,3072]{1,0:T(8,128)(2,1)S(1)}, u32[]{:S(2)}, u32[]{:S(2)}) collective-permute-start(bf16[24,3072]{1,0:T(8,128)(2,1)S(1)} %slice.62), channel_id=1, source_target_pairs={{0,4},{2,6},{4,0},{6,2},{1,5},{3,7},{5,1},{7,3},{8,12},{10,14},{12... | collective-permute-start | bytes 442376 | tf_op jit(solution)/shard_map/ppermute | solution.py:23
  51.1 8.4 %collective-permute-start.23 = (bf16[24,3072]{1,0:T(8,128)(2,1)S(1)}, bf16[24,3072]{1,0:T(8,128)(2,1)S(1)}, u32[]{:S(2)}, u32[]{:S(2)}) collective-permute-start(bf16[24,3072]{1,0:T(8,128)(2,1)S(1)} %fusion.3), channel_id=1, source_target_pairs={{0,16},{8,24},{16,0},{24,8},{1,17},{9,25},{17,1},{25,9},{2,18},{10... | collective-permute-start | bytes 442376 | tf_op jit(solution)/shard_map/ppermute | solution.py:23
  54.3 6.1 %collective-permute-start.26 = (bf16[24,3072]{1,0:T(8,128)(2,1)S(1)}, bf16[24,3072]{1,0:T(8,128)(2,1)S(1)}, u32[]{:S(2)}, u32[]{:S(2)}) collective-permute-start(bf16[24,3072]{1,0:T(8,128)(2,1)S(1)} %fusion.2), channel_id=1, source_target_pairs={{0,8},{8,0},{16,24},{24,16},{1,9},{9,1},{17,25},{25,17},{2,10},{10... | collective-permute-start | bytes 442376 | tf_op jit(solution)/shard_map/ppermute | solution.py:23
  (5 other events, 9.8 us)

commit v4 on v3

--- a/solution.py
+++ b/solution.py
@@ -11,6 +11,10 @@
 
 
 epsilon = 1e-05
+
+GROUPS = [[3, 1], [2, 0]]
+SEQUENCE = ['z3', 'z1', 'z2', 'x0', 'd0', 'e0', 'x3', 'd3', 'x1', 'd1', 'x2', 'd2', 'e3', 'e1', 'e2', 'g0', 'r3', 'r1', 'g1', 'r2', 'r0', 'y3', 'w3', 'y2', 'w2', 'y1', 'w1', 'y0']
+WAITS = {'g1': ('r3',), 'r1': ('x2',), 'r3': ('x2',), 'y1': ('r2',)}
 
 
 def shifted(x, axis, by):
@@ -124,6 +128,39 @@
     return (attn_float + moe_part).astype(jnp.bfloat16)
 
 
+def pack_kernel(
+    exp_count, keys_ref, values_ref, ids_hbm, route_hbm, out_ref, ids_ref, route_ref, share_ref, sems
+):
+    block_len = keys_ref.shape[0]
+    token_count = ids_ref.shape[1]
+    copies = [
+        pltpu.make_async_copy(source, target, sems.at[i])
+        for i, (source, target) in enumerate(
+            [
+                (ids_hbm, ids_ref),
+                (route_hbm, route_ref),
+                (keys_ref, out_ref.at[0:block_len]),
+                (values_ref, out_ref.at[block_len : 2 * block_len]),
+            ]
+        )
+    ]
+    for copy in copies:
+        copy.start()
+    share_ref[...] = jnp.zeros_like(share_ref)
+    copies[0].wait()
+    copies[1].wait()
+    for expert in range(exp_count):
+        rest = jnp.sum(jnp.where(ids_ref[...] == expert, route_ref[...], 0.0), axis=0, keepdims=True)
+        for piece in range(3):
+            row = piece * exp_count + expert
+            part = rest.astype(jnp.bfloat16).astype(jnp.float32)
+            share_ref[row : row + 1, 0:token_count] = part
+            rest = rest - part
+    out_ref[2 * block_len :] = share_ref[...].astype(jnp.bfloat16)
+    copies[2].wait()
+    copies[3].wait()
+
+
 def attend_kernel(block_len, scale, *refs):
     place_ref, query_ref, doc_row, *packs = refs[:-4]
     out_ref, marked_ref, keys_ref, values_ref = refs[-4:]
@@ -269,10 +306,6 @@
             sent[i][:, columns] = product[low + half : low + block_len]
 
 
-def after(value, *others):
-    return lax.optimization_barrier((value, *others))[0]
-
-
 def vmem():
     return pl.BlockSpec(memory_space=pltpu.VMEM)
 
@@ -296,16 +329,25 @@
     half = block_len // 2
     far = range(1, seq_count)
 
-    named = expert_ids[:, :, None] == jnp.arange(exp_count, dtype=jnp.int32)[None, None, :]
-    rest = jnp.sum(jnp.where(named, route_weights[:, :, None], 0.0), axis=1).T
-    pieces = []
-    for _ in range(3):
-        piece = lax.reduce_precision(rest, 8, 7)
-        pieces.append(piece.astype(jnp.bfloat16))
-        rest = rest - piece
-    pieces = jnp.concatenate(pieces, axis=0)
-    pieces = jnp.pad(pieces, ((0, 16 - 3 * exp_count), (0, head_dim - token_count)))
-    pack = jnp.concatenate([keys[:, 0, :], values[:, 0, :], pieces], axis=0)
+    pack = pl.pallas_call(
+        functools.partial(pack_kernel, exp_count),
+        out_shape=jax.ShapeDtypeStruct((2 * block_len + 16, head_dim), jnp.bfloat16),
+        in_specs=[anywhere()] * 4,
+        out_specs=vmem(),
+        scratch_shapes=[
+            pltpu.VMEM(expert_ids.shape[::-1], jnp.int32),
+            pltpu.VMEM(route_weights.shape[::-1], jnp.float32),
+            pltpu.VMEM((16, head_dim), jnp.float32),
+            pltpu.SemaphoreType.DMA((4,)),
+        ],
+        compiler_params=pltpu.CompilerParams(vmem_limit_bytes=4 << 20),
+        name="pack",
+    )(
+        *[
+            pltpu.with_memory_space_constraint(x, pltpu.HBM)
+            for x in (keys[:, 0, :], values[:, 0, :], expert_ids.T, route_weights.T)
+        ]
+    )
     packs = [pack] + [flipped(pack, "seq", d) for d in far]
 
     heads, pack = lax.optimization_barrier((jnp.transpose(queries, (1, 0, 2)), pack))
@@ -330,28 +372,17 @@
         name="attend",
     )(seq_index.reshape(1), heads, doc_ids.reshape(1, -1), *packs)
 
-    first, second = [3, 1], [2, 0]
-    far_bit = exp_count // 2
-    blocks = {(d, 0): flipped(attended, "seq", d) for d in [3, 1, 2]}
-    blocks[0, 0] = marked
-
-    def spread(d, bit):
-        for j in range(0, exp_count, 2 * bit):
-            blocks[d, j ^ bit] = flipped(blocks[d, j], "exp", bit)
-
-    for d in [0, 3, 1, 2]:
-        spread(d, 2)
-        blocks[d, 1], blocks[d, 3] = flipped(blocks[d, 0], "exp", 1), flipped(blocks[d, 2], "exp", 1)
-    blocks[3, 2] = after(blocks[3, 2], blocks[2, 0])
-    blocks[3, 3] = flipped(blocks[3, 2], 'exp', 1)
     order = [j for j in range(exp_count) if not j & 1] + [j for j in range(exp_count) if j & 1]
     gain = norm_gain.reshape(exp_count, 1, part_width)
     weights = [pltpu.with_memory_space_constraint(w, pltpu.HBM) for w in (gain, w_in, w_out)]
 
-    def experts(group):
+    def experts(group, last):
         size = len(group)
-        operands = [blocks[0, j] for j in range(exp_count)]
-        operands += [blocks[d, j] for d in group if d for j in range(exp_count)]
+        operands = list(marked_blocks)
+        for d in group:
+            if d:
+                operands += [there[kind + str(d)] for kind in "zdx"]
+                operands.append(there["e" + str(d)] if d != group[0] else last)
         out_shape = [jax.ShapeDtypeStruct((half, width), jnp.bfloat16)] * (2 * size)
         scratch = [
             pltpu.VMEM((size * exp_count, token_count, hidden_width), jnp.float32),
@@ -384,31 +415,48 @@
         )(exp_index.reshape(1), *weights, *operands)
         return dict(zip(group, zip(outs[:size], outs[size : 2 * size]))), outs[-1]
 
-    def send(returned):
-        sums = {}
-        for d, (kept, sent) in returned.items():
-            both = kept.astype(jnp.float32) + flipped(sent, "exp", 1).astype(jnp.float32)
-            sums[d] = both[:token_count], both[token_count:].astype(jnp.bfloat16)
-        return sums
-
-    early, own_e = experts(first)
-    early[3], early[1] = [(kept, after(sent, blocks[2, 2])) for kept, sent in (early[3], early[1])]
-    early = send(early)
-    blocks[2, 3] = after(blocks[2, 3], early[3][1])
-    late, own_l = experts(second)
-    own = own_e if 0 in first else own_l
-    late = send(late)
+    there = {"z0": marked}
+    near = {}
+    for name in SEQUENCE:
+        kind, d = name[0], int(name[1])
+
+        def held(value):
+            others = [there[other] for other in WAITS.get(name, ())]
+            return lax.optimization_barrier((value, *others))[0] if others else value
+
+        if kind == "z":
+            there[name] = flipped(held(attended), "seq", d)
+        elif kind in "dx":
+            there[name] = flipped(held(there[f"z{d}"]), "exp", 1 if kind == "d" else 2)
+        elif kind == "e":
+            there[name] = flipped(held(there[f"x{d}"]), "exp", 1)
+        elif kind == "g":
+            group = GROUPS[d]
+            marked_blocks = [there[k + "0"] for k in "zdxe"]
+            if group[0]:
+                last = held(there[f"e{group[0]}"])
+            else:
+                last = None
+                marked_blocks[3] = held(marked_blocks[3])
+            outs, extra = experts(group, last)
+            if 0 in group:
+                own = extra
+            for member, (kept, sent) in outs.items():
+                there[f"k{member}"], there[f"s{member}"] = kept, sent
+            there[name] = there[f"s{group[0]}"]
+        elif kind == "r":
+            both = there[f"k{d}"].astype(jnp.float32)
+            both = both + flipped(held(there[f"s{d}"]), "exp", 1).astype(jnp.float32)
+            near[d], there[name] = both[:token_count], both[token_count:].astype(jnp.bfloat16)
+        elif kind == "y":
+            there[name] = flipped(held(there[f"r{d}"]), "exp", 2)
+            near[d] = near[d] + there[name].astype(jnp.float32)
+        elif kind == "w":
+            there[name] = flipped(held(near[d].astype(jnp.bfloat16)), "seq", d)
+            near[d] = there[name].astype(jnp.float32)
     total = jnp.transpose(own, (1, 0, 2)).reshape(token_count, width).astype(jnp.float32)
-    for d, (mine, away) in sorted((early | late).items(), reverse=True):
-        if d == 1:
-            away = after(away, late[2][1])
-        came = flipped(away, "exp", 2)
-        if d == 3:
-            came3 = came
-        mine = mine + came.astype(jnp.float32)
-        if d:
-            mine = flipped(mine.astype(jnp.bfloat16), "seq", d).astype(jnp.float32)
-        total = total + mine
+    for d in sorted(near, reverse=True):
+        total = total + near[d]
     return total.astype(jnp.bfloat16)
 
 

time: 61.5 us -> 60.9 us (level)
  other arithmetic: 3.55 us -> 2.06 us
  Pallas kernels: 7.88 us -> 8.7 us
    pallas_call x0 -> x1, Pallas kernels: none -> 0.82 us  [gathered_shards(): pl.pallas_call(functools.partial(pack_kernel, exp_count), out_shape=jax.S...]
    concatenate x2 -> x0, other arithmetic: 0.78 us -> none  [the longest x1 0.76 us: gathered_shards(): pack = jnp.concatenate([keys[:, 0, :], values[:, 0, :], pieces], axis=0)]
    reduce_sum x1 -> x0, other arithmetic: 0.71 us -> none  [gathered_shards(): rest = jnp.sum(jnp.where(named, route_weights[:, :, None], 0.0), axis=1).T]
  transfers between devices with their start and end apart: 29 -> 29, of which waited for: 12 -> 13; matrix products, arithmetic and copies ran while one was open for 3% -> 3% of each run, Pallas kernels for 12% -> 12%
where the time goes in v4:
time: 60.9 us; the launch traced here: 60.6 us
  starting transfers between devices  27.6 us (45%)
  waiting for transfers between devices  21.3 us (35%)
  Pallas kernels  8.7 us (14%)
  other arithmetic  2.06 us (3%)
  local copies, waits for them, and re-layouts  0.78 us (1%)
    ppermute x29, starting transfers between devices, flipped(): lax.ppermute(x, axis, [(i, i ^ by) for i in range(lax.axis_size(axis))])  27.6 us
    ppermute x29, waiting for transfers between devices, flipped(): lax.ppermute(x, axis, [(i, i ^ by) for i in range(lax.axis_size(axis))])  21.3 us
    pallas_call x2, Pallas kernels, experts(): pl.pallas_call(functools.partial(experts_kernel, seq_count, group, order)...  7.13 us
  transfers between devices with their start and end apart: 29, of which 13 were waited for; matrix products, arithmetic and copies ran while one was open for 3% of the time, Pallas kernels for 12%

profile of v4, /device:TPU:0, one launch (start us, length us, event | category | flops | bytes accessed | tf_op | source)
XLA Modules:
  0.0 60.6 jit_solution(1464850712761401577)
XLA Ops:
  0.8 3.1 %collective-permute-start = (bf16[208,128]{1,0:T(8,128)(2,1)S(1)}, bf16[208,128]{1,0:T(8,128)(2,1)S(1)}, u32[]{:S(2)}, u32[]{:S(2)}) collective-permute-start(bf16[208,128]{1,0:T(8,128)(2,1)S(1)} %pack.1.refs_3_), channel_id=1, source_target_pairs={{0,8},{8,0},{16,24},{24,16},{1,9},{9,1},{17,25},{25,17},{2,10},{10... | collective-permute-start | bytes 159752 | tf_op jit(solution)/shard_map/ppermute | solution.py:27
  3.9 2.6 %collective-permute-start.1 = (bf16[208,128]{1,0:T(8,128)(2,1)S(1)}, bf16[208,128]{1,0:T(8,128)(2,1)S(1)}, u32[]{:S(2)}, u32[]{:S(2)}) collective-permute-start(bf16[208,128]{1,0:T(8,128)(2,1)S(1)} %pack.1.refs_3_), channel_id=1, source_target_pairs={{0,16},{8,24},{16,0},{24,8},{1,17},{9,25},{17,1},{25,9},{2,18},{10... | collective-permute-start | bytes 159752 | tf_op jit(solution)/shard_map/ppermute | solution.py:27
  8.1 1.8 %collective-permute-done.1.refs_5_ = bf16[208,128]{1,0:T(8,128)(2,1)S(1)} collective-permute-done((bf16[208,128]{1,0:T(8,128)(2,1)S(1)}, bf16[208,128]{1,0:T(8,128)(2,1)S(1)}, u32[]{:S(2)}, u32[]{:S(2)}) %collective-permute-start.1) | collective-permute-done | bytes 53280 | tf_op jit(solution)/shard_map/ppermute | solution.py:27
  10.0 2.5 %collective-permute-done.2.refs_6_ = bf16[208,128]{1,0:T(8,128)(2,1)S(1)} collective-permute-done((bf16[208,128]{1,0:T(8,128)(2,1)S(1)}, bf16[208,128]{1,0:T(8,128)(2,1)S(1)}, u32[]{:S(2)}, u32[]{:S(2)}) %collective-permute-start.2) | collective-permute-done | bytes 53280 | tf_op jit(solution)/shard_map/ppermute | solution.py:27
  13.2 1.1 %collective-permute-start.10 = (bf16[96,768]{1,0:T(8,128)(2,1)S(1)}, bf16[96,768]{1,0:T(8,128)(2,1)S(1)}, u32[]{:S(2)}, u32[]{:S(2)}) collective-permute-start(bf16[96,768]{1,0:T(8,128)(2,1)S(1)} %get-tuple-element.25), channel_id=1, source_target_pairs={{0,24},{8,16},{16,8},{24,0},{1,25},{9,17},{17,9},{25,1},{2,26},{10... | collective-permute-start | bytes 442376 | tf_op jit(solution)/shard_map/ppermute | solution.py:27
  14.5 1.5 %collective-permute-start.4 = (bf16[112,768]{1,0:T(8,128)(2,1)S(1)}, bf16[112,768]{1,0:T(8,128)(2,1)S(1)}, u32[]{:S(2)}, u32[]{:S(2)}) collective-permute-start(bf16[112,768]{1,0:T(8,128)(2,1)S(1)} %get-tuple-element.24.refs_4_), channel_id=1, source_target_pairs={{0,4},{2,6},{4,0},{6,2},{1,5},{3,7},{5,1},{7,3},{8,12},{10,14},{12... | collective-permute-start | bytes 516104 | tf_op jit(solution)/shard_map/ppermute | solution.py:27
  16.0 3.2 %collective-permute-start.6 = (bf16[96,768]{1,0:T(8,128)(2,1)S(1)}, bf16[96,768]{1,0:T(8,128)(2,1)S(1)}, u32[]{:S(2)}, u32[]{:S(2)}) collective-permute-start(bf16[96,768]{1,0:T(8,128)(2,1)S(1)} %get-tuple-element.25), channel_id=1, source_target_pairs={{0,16},{8,24},{16,0},{24,8},{1,17},{9,25},{17,1},{25,9},{2,18},{10... | collective-permute-start | bytes 442376 | tf_op jit(solution)/shard_map/ppermute | solution.py:27
  19.1 2.8 %collective-permute-done.10.refs_8_ = bf16[96,768]{1,0:T(8,128)(2,1)S(1)} collective-permute-done((bf16[96,768]{1,0:T(8,128)(2,1)S(1)}, bf16[96,768]{1,0:T(8,128)(2,1)S(1)}, u32[]{:S(2)}, u32[]{:S(2)}) %collective-permute-start.10) | collective-permute-done | bytes 147488 | tf_op jit(solution)/shard_map/ppermute | solution.py:27
  21.9 1.5 %collective-permute-start.12 = (bf16[96,768]{1,0:T(8,128)(2,1)S(1)}, bf16[96,768]{1,0:T(8,128)(2,1)S(1)}, u32[]{:S(2)}, u32[]{:S(2)}) collective-permute-start(bf16[96,768]{1,0:T(8,128)(2,1)S(1)} %collective-permute-done.10.refs_8_), channel_id=1, source_target_pairs={{0,4},{2,6},{4,0},{6,2},{1,5},{3,7},{5,1},{7,3},{8,12},{10,14},{12... | collective-permute-start | bytes 442376 | tf_op jit(solution)/shard_map/ppermute | solution.py:27
  24.0 2.6 %collective-permute-done.6.refs_8_ = bf16[96,768]{1,0:T(8,128)(2,1)S(1)} collective-permute-done((bf16[96,768]{1,0:T(8,128)(2,1)S(1)}, bf16[96,768]{1,0:T(8,128)(2,1)S(1)}, u32[]{:S(2)}, u32[]{:S(2)}) %collective-permute-start.6) | collective-permute-done | bytes 147488 | tf_op jit(solution)/shard_map/ppermute | solution.py:27
  27.6 1.1 %collective-permute-done.16.refs_14_ = bf16[96,768]{1,0:T(8,128)(2,1)S(1)} collective-permute-done((bf16[96,768]{1,0:T(8,128)(2,1)S(1)}, bf16[96,768]{1,0:T(8,128)(2,1)S(1)}, u32[]{:S(2)}, u32[]{:S(2)}) %collective-permute-start.16) | collective-permute-done | bytes 147488 | tf_op jit(solution)/shard_map/ppermute | solution.py:27
  28.7 1.5 %collective-permute-start.8 = (bf16[96,768]{1,0:T(8,128)(2,1)S(1)}, bf16[96,768]{1,0:T(8,128)(2,1)S(1)}, u32[]{:S(2)}, u32[]{:S(2)}) collective-permute-start(bf16[96,768]{1,0:T(8,128)(2,1)S(1)} %collective-permute-done.6.refs_8_), channel_id=1, source_target_pairs={{0,4},{2,6},{4,0},{6,2},{1,5},{3,7},{5,1},{7,3},{8,12},{10,14},{12... | collective-permute-start | bytes 442376 | tf_op jit(solution)/shard_map/ppermute | solution.py:27
  30.2 3.5 %experts.2 = (bf16[48,3072]{1,0:T(8,128)(2,1)S(1)}, bf16[48,3072]{1,0:T(8,128)(2,1)S(1)}, bf16[48,3072]{1,0:T(8,128)(2,1)S(1)}, bf16[48,3072]{1,0:T(8,128)(2,1)S(1)}) custom-call(s32[1]{0:T(128)} %bitcast.refs_0_, f32[4,1,768]{2,1,0:T(1,128)} %bitcast.14, bf16[1,3072,512]{2,1,0:T(8,128)(2,1)} %refs_2_.3, bf16[1,512,3072]{2,1,0:T(8,128)(2,1)} %refs_3_.3, ...), custom_call_target="tpu_custom_call" | custom-call | flops 1207959552 | bytes 8388608 | tf_op jit(solution)/shard_map/experts/pallas_call | solution.py:402
  33.7 1.2 %collective-permute-done.8.refs_10_ = bf16[96,768]{1,0:T(8,128)(2,1)S(1)} collective-permute-done((bf16[96,768]{1,0:T(8,128)(2,1)S(1)}, bf16[96,768]{1,0:T(8,128)(2,1)S(1)}, u32[]{:S(2)}, u32[]{:S(2)}) %collective-permute-start.8) | collective-permute-done | bytes 147488 | tf_op jit(solution)/shard_map/ppermute | solution.py:27
  36.6 1.6 %collective-permute-start.19 = (bf16[24,3072]{1,0:T(8,128)(2,1)S(1)}, bf16[24,3072]{1,0:T(8,128)(2,1)S(1)}, u32[]{:S(2)}, u32[]{:S(2)}) collective-permute-start(bf16[24,3072]{1,0:T(8,128)(2,1)S(1)} %slice.65), channel_id=1, source_target_pairs={{0,4},{2,6},{4,0},{6,2},{1,5},{3,7},{5,1},{7,3},{8,12},{10,14},{12... | collective-permute-start | bytes 442376 | tf_op jit(solution)/shard_map/ppermute | solution.py:27
  38.2 3.6 %experts.3 = (bf16[48,3072]{1,0:T(8,128)(2,1)S(1)}, bf16[48,3072]{1,0:T(8,128)(2,1)S(1)}, bf16[48,3072]{1,0:T(8,128)(2,1)S(1)}, bf16[48,3072]{1,0:T(8,128)(2,1)S(1)}, bf16[4,24,768]{2,1,0:T(8,128)(2,1)S(1)}) custom-call(s32[1]{0:T(128)} %bitcast.refs_0_, f32[4,1,768]{2,1,0:T(1,128)} %bitcast.15, bf16[1,3072,512]{2,1,0:T(8,128)(2,1)} %refs_2_.3, ...), custom_call_target="tpu_custom_call" | custom-call | flops 1207959552 | bytes 8388608 | tf_op jit(solution)/shard_map/experts/pallas_call | solution.py:402
  42.6 1.0 %collective-permute-start.20 = (bf16[24,3072]{1,0:T(8,128)(2,1)S(1)}, bf16[24,3072]{1,0:T(8,128)(2,1)S(1)}, u32[]{:S(2)}, u32[]{:S(2)}) collective-permute-start(bf16[24,3072]{1,0:T(8,128)(2,1)S(1)} %fusion.4), channel_id=1, source_target_pairs={{0,24},{8,16},{16,8},{24,0},{1,25},{9,17},{17,9},{25,1},{2,26},{10... | collective-permute-start | bytes 442376 | tf_op jit(solution)/shard_map/ppermute | solution.py:27
  43.7 1.6 %collective-permute-start.22 = (bf16[24,3072]{1,0:T(8,128)(2,1)S(1)}, bf16[24,3072]{1,0:T(8,128)(2,1)S(1)}, u32[]{:S(2)}, u32[]{:S(2)}) collective-permute-start(bf16[24,3072]{1,0:T(8,128)(2,1)S(1)} %slice.64), channel_id=1, source_target_pairs={{0,4},{2,6},{4,0},{6,2},{1,5},{3,7},{5,1},{7,3},{8,12},{10,14},{12... | collective-permute-start | bytes 442376 | tf_op jit(solution)/shard_map/ppermute | solution.py:27
  45.9 1.6 %collective-permute-start.28 = (bf16[24,3072]{1,0:T(8,128)(2,1)S(1)}, bf16[24,3072]{1,0:T(8,128)(2,1)S(1)}, u32[]{:S(2)}, u32[]{:S(2)}) collective-permute-start(bf16[24,3072]{1,0:T(8,128)(2,1)S(1)} %slice.62), channel_id=1, source_target_pairs={{0,4},{2,6},{4,0},{6,2},{1,5},{3,7},{5,1},{7,3},{8,12},{10,14},{12... | collective-permute-start | bytes 442376 | tf_op jit(solution)/shard_map/ppermute | solution.py:27
  47.5 3.0 %collective-permute-done.22 = bf16[24,3072]{1,0:T(8,128)(2,1)S(1)} collective-permute-done((bf16[24,3072]{1,0:T(8,128)(2,1)S(1)}, bf16[24,3072]{1,0:T(8,128)(2,1)S(1)}, u32[]{:S(2)}, u32[]{:S(2)}) %collective-permute-start.22) | collective-permute-done | bytes 147488 | tf_op jit(solution)/shard_map/ppermute | solution.py:27
  50.5 2.1 %collective-permute-start.23 = (bf16[24,3072]{1,0:T(8,128)(2,1)S(1)}, bf16[24,3072]{1,0:T(8,128)(2,1)S(1)}, u32[]{:S(2)}, u32[]{:S(2)}) collective-permute-start(bf16[24,3072]{1,0:T(8,128)(2,1)S(1)} %fusion.3), channel_id=1, source_target_pairs={{0,16},{8,24},{16,0},{24,8},{1,17},{9,25},{17,1},{25,9},{2,18},{10... | collective-permute-start | bytes 442376 | tf_op jit(solution)/shard_map/ppermute | solution.py:27
  52.6 1.0 %collective-permute-done.25 = bf16[24,3072]{1,0:T(8,128)(2,1)S(1)} collective-permute-done((bf16[24,3072]{1,0:T(8,128)(2,1)S(1)}, bf16[24,3072]{1,0:T(8,128)(2,1)S(1)}, u32[]{:S(2)}, u32[]{:S(2)}) %collective-permute-start.25) | collective-permute-done | bytes 147488 | tf_op jit(solution)/shard_map/ppermute | solution.py:27
  53.7 1.4 %collective-permute-start.26 = (bf16[24,3072]{1,0:T(8,128)(2,1)S(1)}, bf16[24,3072]{1,0:T(8,128)(2,1)S(1)}, u32[]{:S(2)}, u32[]{:S(2)}) collective-permute-start(bf16[24,3072]{1,0:T(8,128)(2,1)S(1)} %fusion.2), channel_id=1, source_target_pairs={{0,8},{8,0},{16,24},{24,16},{1,9},{9,1},{17,25},{25,17},{2,10},{10... | collective-permute-start | bytes 442376 | tf_op jit(solution)/shard_map/ppermute | solution.py:27
  55.8 3.1 %collective-permute-done.23 = bf16[24,3072]{1,0:T(8,128)(2,1)S(1)} collective-permute-done((bf16[24,3072]{1,0:T(8,128)(2,1)S(1)}, bf16[24,3072]{1,0:T(8,128)(2,1)S(1)}, u32[]{:S(2)}, u32[]{:S(2)}) %collective-permute-start.23) | collective-permute-done | bytes 147488 | tf_op jit(solution)/shard_map/ppermute | solution.py:27
  (54 shorter events, 10.6 us)
Async XLA Ops:
  0.8 7.3 %collective-permute-start = (bf16[208,128]{1,0:T(8,128)(2,1)S(1)}, bf16[208,128]{1,0:T(8,128)(2,1)S(1)}, u32[]{:S(2)}, u32[]{:S(2)}) collective-permute-start(bf16[208,128]{1,0:T(8,128)(2,1)S(1)} %pack.1.refs_3_), channel_id=1, source_target_pairs={{0,8},{8,0},{16,24},{24,16},{1,9},{9,1},{17,25},{25,17},{2,10},{10... | collective-permute-start | bytes 159752 | tf_op jit(solution)/shard_map/ppermute | solution.py:27
  3.9 6.1 %collective-permute-start.1 = (bf16[208,128]{1,0:T(8,128)(2,1)S(1)}, bf16[208,128]{1,0:T(8,128)(2,1)S(1)}, u32[]{:S(2)}, u32[]{:S(2)}) collective-permute-start(bf16[208,128]{1,0:T(8,128)(2,1)S(1)} %pack.1.refs_3_), channel_id=1, source_target_pairs={{0,16},{8,24},{16,0},{24,8},{1,17},{9,25},{17,1},{25,9},{2,18},{10... | collective-permute-start | bytes 159752 | tf_op jit(solution)/shard_map/ppermute | solution.py:27
  6.5 5.9 %collective-permute-start.2 = (bf16[208,128]{1,0:T(8,128)(2,1)S(1)}, bf16[208,128]{1,0:T(8,128)(2,1)S(1)}, u32[]{:S(2)}, u32[]{:S(2)}) collective-permute-start(bf16[208,128]{1,0:T(8,128)(2,1)S(1)} %pack.1.refs_3_), channel_id=1, source_target_pairs={{0,24},{8,16},{16,8},{24,0},{1,25},{9,17},{17,9},{25,1},{2,26},{10... | collective-permute-start | bytes 159752 | tf_op jit(solution)/shard_map/ppermute | solution.py:27
  13.2 8.7 %collective-permute-start.10 = (bf16[96,768]{1,0:T(8,128)(2,1)S(1)}, bf16[96,768]{1,0:T(8,128)(2,1)S(1)}, u32[]{:S(2)}, u32[]{:S(2)}) collective-permute-start(bf16[96,768]{1,0:T(8,128)(2,1)S(1)} %get-tuple-element.25), channel_id=1, source_target_pairs={{0,24},{8,16},{16,8},{24,0},{1,25},{9,17},{17,9},{25,1},{2,26},{10... | collective-permute-start | bytes 442376 | tf_op jit(solution)/shard_map/ppermute | solution.py:27
  14.3 9.2 %collective-permute-start.14 = (bf16[96,768]{1,0:T(8,128)(2,1)S(1)}, bf16[96,768]{1,0:T(8,128)(2,1)S(1)}, u32[]{:S(2)}, u32[]{:S(2)}) collective-permute-start(bf16[96,768]{1,0:T(8,128)(2,1)S(1)} %get-tuple-element.25), channel_id=1, source_target_pairs={{0,8},{8,0},{16,24},{24,16},{1,9},{9,1},{17,25},{25,17},{2,10},{10... | collective-permute-start | bytes 442376 | tf_op jit(solution)/shard_map/ppermute | solution.py:27
  14.5 12.1 %collective-permute-start.4 = (bf16[112,768]{1,0:T(8,128)(2,1)S(1)}, bf16[112,768]{1,0:T(8,128)(2,1)S(1)}, u32[]{:S(2)}, u32[]{:S(2)}) collective-permute-start(bf16[112,768]{1,0:T(8,128)(2,1)S(1)} %get-tuple-element.24.refs_4_), channel_id=1, source_target_pairs={{0,4},{2,6},{4,0},{6,2},{1,5},{3,7},{5,1},{7,3},{8,12},{10,14},{12... | collective-permute-start | bytes 516104 | tf_op jit(solution)/shard_map/ppermute | solution.py:27
  16.0 10.6 %collective-permute-start.6 = (bf16[96,768]{1,0:T(8,128)(2,1)S(1)}, bf16[96,768]{1,0:T(8,128)(2,1)S(1)}, u32[]{:S(2)}, u32[]{:S(2)}) collective-permute-start(bf16[96,768]{1,0:T(8,128)(2,1)S(1)} %get-tuple-element.25), channel_id=1, source_target_pairs={{0,16},{8,24},{16,0},{24,8},{1,17},{9,25},{17,1},{25,9},{2,18},{10... | collective-permute-start | bytes 442376 | tf_op jit(solution)/shard_map/ppermute | solution.py:27
  19.1 7.9 %collective-permute-start.3 = (bf16[112,768]{1,0:T(8,128)(2,1)S(1)}, bf16[112,768]{1,0:T(8,128)(2,1)S(1)}, u32[]{:S(2)}, u32[]{:S(2)}) collective-permute-start(bf16[112,768]{1,0:T(8,128)(2,1)S(1)} %get-tuple-element.24.refs_4_), channel_id=1, source_target_pairs={{0,2},{2,0},{4,6},{6,4},{1,3},{3,1},{5,7},{7,5},{8,10},{10,8},{12,... | collective-permute-start | bytes 516104 | tf_op jit(solution)/shard_map/ppermute | solution.py:27
  21.9 5.2 %collective-permute-start.12 = (bf16[96,768]{1,0:T(8,128)(2,1)S(1)}, bf16[96,768]{1,0:T(8,128)(2,1)S(1)}, u32[]{:S(2)}, u32[]{:S(2)}) collective-permute-start(bf16[96,768]{1,0:T(8,128)(2,1)S(1)} %collective-permute-done.10.refs_8_), channel_id=1, source_target_pairs={{0,4},{2,6},{4,0},{6,2},{1,5},{3,7},{5,1},{7,3},{8,12},{10,14},{12... | collective-permute-start | bytes 442376 | tf_op jit(solution)/shard_map/ppermute | solution.py:27
  23.4 5.2 %collective-permute-start.16 = (bf16[96,768]{1,0:T(8,128)(2,1)S(1)}, bf16[96,768]{1,0:T(8,128)(2,1)S(1)}, u32[]{:S(2)}, u32[]{:S(2)}) collective-permute-start(bf16[96,768]{1,0:T(8,128)(2,1)S(1)} %collective-permute-done.14.refs_12_), channel_id=1, source_target_pairs={{0,4},{2,6},{4,0},{6,2},{1,5},{3,7},{5,1},{7,3},{8,12},{10,14},{12... | collective-permute-start | bytes 442376 | tf_op jit(solution)/shard_map/ppermute | solution.py:27
  26.6 3.6 %collective-permute-start.5 = (bf16[112,768]{1,0:T(8,128)(2,1)S(1)}, bf16[112,768]{1,0:T(8,128)(2,1)S(1)}, u32[]{:S(2)}, u32[]{:S(2)}) collective-permute-start(bf16[112,768]{1,0:T(8,128)(2,1)S(1)} %collective-permute-done.4.refs_6_), channel_id=1, source_target_pairs={{0,2},{2,0},{4,6},{6,4},{1,3},{3,1},{5,7},{7,5},{8,10},{10,8},{12,... | collective-permute-start | bytes 516104 | tf_op jit(solution)/shard_map/ppermute | solution.py:27
  27.1 3.1 %collective-permute-start.15 = (bf16[96,768]{1,0:T(8,128)(2,1)S(1)}, bf16[96,768]{1,0:T(8,128)(2,1)S(1)}, u32[]{:S(2)}, u32[]{:S(2)}) collective-permute-start(bf16[96,768]{1,0:T(8,128)(2,1)S(1)} %collective-permute-done.14.refs_12_), channel_id=1, source_target_pairs={{0,2},{2,0},{4,6},{6,4},{1,3},{3,1},{5,7},{7,5},{8,10},{10,8},{12,... | collective-permute-start | bytes 442376 | tf_op jit(solution)/shard_map/ppermute | solution.py:27
  27.2 3.0 %collective-permute-start.13 = (bf16[96,768]{1,0:T(8,128)(2,1)S(1)}, bf16[96,768]{1,0:T(8,128)(2,1)S(1)}, u32[]{:S(2)}, u32[]{:S(2)}) collective-permute-start(bf16[96,768]{1,0:T(8,128)(2,1)S(1)} %collective-permute-done.12.refs_10_), channel_id=1, source_target_pairs={{0,2},{2,0},{4,6},{6,4},{1,3},{3,1},{5,7},{7,5},{8,10},{10,8},{12,... | collective-permute-start | bytes 442376 | tf_op jit(solution)/shard_map/ppermute | solution.py:27
  28.7 6.3 %collective-permute-start.8 = (bf16[96,768]{1,0:T(8,128)(2,1)S(1)}, bf16[96,768]{1,0:T(8,128)(2,1)S(1)}, u32[]{:S(2)}, u32[]{:S(2)}) collective-permute-start(bf16[96,768]{1,0:T(8,128)(2,1)S(1)} %collective-permute-done.6.refs_8_), channel_id=1, source_target_pairs={{0,4},{2,6},{4,0},{6,2},{1,5},{3,7},{5,1},{7,3},{8,12},{10,14},{12... | collective-permute-start | bytes 442376 | tf_op jit(solution)/shard_map/ppermute | solution.py:27
  34.9 3.2 %collective-permute-start.7 = (bf16[96,768]{1,0:T(8,128)(2,1)S(1)}, bf16[96,768]{1,0:T(8,128)(2,1)S(1)}, u32[]{:S(2)}, u32[]{:S(2)}) collective-permute-start(bf16[96,768]{1,0:T(8,128)(2,1)S(1)} %collective-permute-done.6.refs_8_), channel_id=1, source_target_pairs={{0,2},{2,0},{4,6},{6,4},{1,3},{3,1},{5,7},{7,5},{8,10},{10,8},{12,... | collective-permute-start | bytes 442376 | tf_op jit(solution)/shard_map/ppermute | solution.py:27
  35.5 6.4 %collective-permute-start.24 = (bf16[48,3072]{1,0:T(8,128)(2,1)S(1)}, bf16[48,3072]{1,0:T(8,128)(2,1)S(1)}, u32[]{:S(2)}, u32[]{:S(2)}) collective-permute-start(bf16[48,3072]{1,0:T(8,128)(2,1)S(1)} %get-tuple-element.35), channel_id=1, source_target_pairs={{0,2},{2,0},{4,6},{6,4},{1,3},{3,1},{5,7},{7,5},{8,10},{10,8},{12,... | collective-permute-start | bytes 884744 | tf_op jit(solution)/shard_map/ppermute | solution.py:27
  36.6 6.0 %collective-permute-start.19 = (bf16[24,3072]{1,0:T(8,128)(2,1)S(1)}, bf16[24,3072]{1,0:T(8,128)(2,1)S(1)}, u32[]{:S(2)}, u32[]{:S(2)}) collective-permute-start(bf16[24,3072]{1,0:T(8,128)(2,1)S(1)} %slice.65), channel_id=1, source_target_pairs={{0,4},{2,6},{4,0},{6,2},{1,5},{3,7},{5,1},{7,3},{8,12},{10,14},{12... | collective-permute-start | bytes 442376 | tf_op jit(solution)/shard_map/ppermute | solution.py:27
  42.0 3.8 %collective-permute-start.27 = (bf16[48,3072]{1,0:T(8,128)(2,1)S(1)}, bf16[48,3072]{1,0:T(8,128)(2,1)S(1)}, u32[]{:S(2)}, u32[]{:S(2)}) collective-permute-start(bf16[48,3072]{1,0:T(8,128)(2,1)S(1)} %get-tuple-element.38), channel_id=1, source_target_pairs={{0,2},{2,0},{4,6},{6,4},{1,3},{3,1},{5,7},{7,5},{8,10},{10,8},{12,... | collective-permute-start | bytes 884744 | tf_op jit(solution)/shard_map/ppermute | solution.py:27
  42.6 12.6 %collective-permute-start.20 = (bf16[24,3072]{1,0:T(8,128)(2,1)S(1)}, bf16[24,3072]{1,0:T(8,128)(2,1)S(1)}, u32[]{:S(2)}, u32[]{:S(2)}) collective-permute-start(bf16[24,3072]{1,0:T(8,128)(2,1)S(1)} %fusion.4), channel_id=1, source_target_pairs={{0,24},{8,16},{16,8},{24,0},{1,25},{9,17},{17,9},{25,1},{2,26},{10... | collective-permute-start | bytes 442376 | tf_op jit(solution)/shard_map/ppermute | solution.py:27
  43.7 6.8 %collective-permute-start.22 = (bf16[24,3072]{1,0:T(8,128)(2,1)S(1)}, bf16[24,3072]{1,0:T(8,128)(2,1)S(1)}, u32[]{:S(2)}, u32[]{:S(2)}) collective-permute-start(bf16[24,3072]{1,0:T(8,128)(2,1)S(1)} %slice.64), channel_id=1, source_target_pairs={{0,4},{2,6},{4,0},{6,2},{1,5},{3,7},{5,1},{7,3},{8,12},{10,14},{12... | collective-permute-start | bytes 442376 | tf_op jit(solution)/shard_map/ppermute | solution.py:27
  45.3 8.3 %collective-permute-start.25 = (bf16[24,3072]{1,0:T(8,128)(2,1)S(1)}, bf16[24,3072]{1,0:T(8,128)(2,1)S(1)}, u32[]{:S(2)}, u32[]{:S(2)}) collective-permute-start(bf16[24,3072]{1,0:T(8,128)(2,1)S(1)} %slice.63), channel_id=1, source_target_pairs={{0,4},{2,6},{4,0},{6,2},{1,5},{3,7},{5,1},{7,3},{8,12},{10,14},{12... | collective-permute-start | bytes 442376 | tf_op jit(solution)/shard_map/ppermute | solution.py:27
  45.9 9.9 %collective-permute-start.28 = (bf16[24,3072]{1,0:T(8,128)(2,1)S(1)}, bf16[24,3072]{1,0:T(8,128)(2,1)S(1)}, u32[]{:S(2)}, u32[]{:S(2)}) collective-permute-start(bf16[24,3072]{1,0:T(8,128)(2,1)S(1)} %slice.62), channel_id=1, source_target_pairs={{0,4},{2,6},{4,0},{6,2},{1,5},{3,7},{5,1},{7,3},{8,12},{10,14},{12... | collective-permute-start | bytes 442376 | tf_op jit(solution)/shard_map/ppermute | solution.py:27
  50.5 8.3 %collective-permute-start.23 = (bf16[24,3072]{1,0:T(8,128)(2,1)S(1)}, bf16[24,3072]{1,0:T(8,128)(2,1)S(1)}, u32[]{:S(2)}, u32[]{:S(2)}) collective-permute-start(bf16[24,3072]{1,0:T(8,128)(2,1)S(1)} %fusion.3), channel_id=1, source_target_pairs={{0,16},{8,24},{16,0},{24,8},{1,17},{9,25},{17,1},{25,9},{2,18},{10... | collective-permute-start | bytes 442376 | tf_op jit(solution)/shard_map/ppermute | solution.py:27
  53.7 6.1 %collective-permute-start.26 = (bf16[24,3072]{1,0:T(8,128)(2,1)S(1)}, bf16[24,3072]{1,0:T(8,128)(2,1)S(1)}, u32[]{:S(2)}, u32[]{:S(2)}) collective-permute-start(bf16[24,3072]{1,0:T(8,128)(2,1)S(1)} %fusion.2), channel_id=1, source_target_pairs={{0,8},{8,0},{16,24},{24,16},{1,9},{9,1},{17,25},{25,17},{2,10},{10... | collective-permute-start | bytes 442376 | tf_op jit(solution)/shard_map/ppermute | solution.py:27
  (5 other events, 9.8 us)

commit v5 on v4

--- a/solution.py
+++ b/solution.py
@@ -13,8 +13,8 @@
 epsilon = 1e-05
 
 GROUPS = [[3, 1], [2, 0]]
-SEQUENCE = ['z3', 'z1', 'z2', 'x0', 'd0', 'e0', 'x3', 'd3', 'x1', 'd1', 'x2', 'd2', 'e3', 'e1', 'e2', 'g0', 'r3', 'r1', 'g1', 'r2', 'r0', 'y3', 'w3', 'y2', 'w2', 'y1', 'w1', 'y0']
-WAITS = {'g1': ('r3',), 'r1': ('x2',), 'r3': ('x2',), 'y1': ('r2',)}
+SEQUENCE = ['z3', 'z1', 'z2', 'd0', 'x3', 'd3', 'x1', 'd1', 'x2', 'd2', 'e1', 'e2', 'x0', 'e0', 'e3', 'g0', 'r1', 'r3', 'g1', 'r2', 'y1', 'r0', 'y3', 'w3', 'y2', 'w2', 'w1', 'y0']
+WAITS = {'e0': ('z3',), 'g1': ('r3',), 'r1': ('x1', 'x2'), 'r3': ('x2',), 'y0': ('y2',), 'y1': ('r2',)}
 
 
 def shifted(x, axis, by):
@@ -206,11 +206,29 @@
         marked_ref[0:block_len, columns] = attended
 
 
+def rows_of(part, part_width):
+    return pl.ds(pl.multiple_of(part * part_width, part_width), part_width)
+
+
+def near_kernel(place_ref, w_in_hbm, out_ref, sems):
+    place = place_ref[0]
+    reads = [
+        pltpu.make_async_copy(
+            w_in_hbm.at[0, rows_of(place ^ j, out_ref.shape[1])], out_ref.at[j], sems.at[j]
+        )
+        for j in range(out_ref.shape[0])
+    ]
+    for read in reads:
+        read.start()
+    for read in reads:
+        read.wait()
+
+
 def experts_kernel(seq_count, group, order, *refs):
     exp_count = len(order)
-    place_ref, gain_hbm, w_in_hbm, w_out_hbm = refs[:4]
-    marked = refs[4 : 4 + exp_count]
-    refs = refs[4 + exp_count :]
+    place_ref, gain_hbm, w_in_hbm, w_out_hbm, w_near_ref = refs[:5]
+    marked = refs[5 : 5 + exp_count]
+    refs = refs[5 + exp_count :]
     blocks = {0: marked}
     for d in group:
         if d:
@@ -225,12 +243,12 @@
     width = part_width * exp_count
     lanes = 128
 
-    def rows_of(j):
-        return pl.ds(pl.multiple_of((place ^ j) * part_width, part_width), part_width)
-
+    near_count = w_near_ref.shape[0]
     reads = [
-        pltpu.make_async_copy(w_in_hbm.at[0, rows_of(j)], w_in_ref.at[j], sems.at[j])
-        for j in range(exp_count)
+        pltpu.make_async_copy(
+            w_in_hbm.at[0, rows_of(place ^ j, part_width)], w_in_ref.at[j - near_count], sems.at[j]
+        )
+        for j in range(near_count, exp_count)
     ]
     depth = hidden_ref.shape[2] // 2
     reads += [
@@ -275,9 +293,11 @@
             if d == 0:
                 split_ref[...] = value.reshape(exp_count, token_count, part_width)
                 own_ref[source] = split_ref[place].astype(jnp.bfloat16)
-        reads[1 + j].wait()
+        if j >= near_count:
+            reads[1 + j - near_count].wait()
+        w_part = w_near_ref[j] if j < near_count else w_in_ref[j - near_count]
         product = jnp.dot(
-            jnp.concatenate(gained, axis=0), w_in_ref[j], preferred_element_type=jnp.float32
+            jnp.concatenate(gained, axis=0), w_part, preferred_element_type=jnp.float32
         )
         hidden = product if hidden is None else hidden + product
     mean_square = jnp.sum(jnp.concatenate(squares, axis=0), axis=1, keepdims=True) * (1.0 / width)
@@ -289,12 +309,12 @@
     ).astype(jnp.bfloat16)
     half = block_len // 2
     tiles = [slice(start, start + part_width) for start in range(0, width, part_width)]
-    reads[1 + exp_count].wait()
+    reads[1 + exp_count - near_count].wait()
     for columns in tiles:
         sum_ref[:, columns] = jnp.dot(
             hidden[:, :depth], w_out_ref[:depth, columns], preferred_element_type=jnp.float32
         )
-    reads[2 + exp_count].wait()
+    reads[2 + exp_count - near_count].wait()
     for columns in tiles:
         product = sum_ref[:, columns] + jnp.dot(
             hidden[:, depth:], w_out_ref[depth:, columns], preferred_element_type=jnp.float32
@@ -352,6 +372,17 @@
 
     heads, pack = lax.optimization_barrier((jnp.transpose(queries, (1, 0, 2)), pack))
     heads = heads * jnp.bfloat16(0.125)
+    w_in_here, _ = lax.optimization_barrier((w_in, pack))
+    w_near = pl.pallas_call(
+        near_kernel,
+        out_shape=pltpu.VMEM((2, part_width, hidden_width), w_in.dtype),
+        in_specs=[pl.BlockSpec(memory_space=pltpu.SMEM), anywhere()],
+        out_specs=vmem(),
+        scratch_shapes=[pltpu.SemaphoreType.DMA((2,))],
+        compiler_params=pltpu.CompilerParams(vmem_limit_bytes=4 << 20),
+        name="near",
+    )(exp_index.reshape(1), pltpu.with_memory_space_constraint(w_in_here, pltpu.HBM))
+    heads, w_near = lax.optimization_barrier((heads, w_near))
     packs[0] = pack
 
     attended, marked = pl.pallas_call(
@@ -388,7 +419,7 @@
             pltpu.VMEM((size * exp_count, token_count, hidden_width), jnp.float32),
             pltpu.VMEM((head_dim, head_dim), jnp.float32),
             pltpu.VMEM((exp_count, 1, part_width), jnp.float32),
-            pltpu.VMEM((exp_count, part_width, hidden_width), jnp.bfloat16),
+            pltpu.VMEM((exp_count - w_near.shape[0], part_width, hidden_width), jnp.bfloat16),
             pltpu.VMEM((hidden_width, width), jnp.bfloat16),
             pltpu.VMEM((size * block_len, width), jnp.float32),
             pltpu.SemaphoreType.DMA((exp_count + 3,)),
@@ -397,7 +428,7 @@
             split = (exp_count, token_count, part_width)
             out_shape.append(jax.ShapeDtypeStruct(split, jnp.bfloat16))
             scratch.append(pltpu.VMEM(split, jnp.float32))
-        in_specs = [pl.BlockSpec(memory_space=pltpu.SMEM)] + [vmem()] * (3 + len(operands))
+        in_specs = [pl.BlockSpec(memory_space=pltpu.SMEM)] + [vmem()] * (4 + len(operands))
         in_specs[1:4] = [anywhere()] * 3
         outs = pl.pallas_call(
             functools.partial(experts_kernel, seq_count, group, order),
@@ -412,7 +443,7 @@
                 transcendentals=size * block_len * hidden_width,
             ),
             name="experts",
-        )(exp_index.reshape(1), *weights, *operands)
+        )(exp_index.reshape(1), *weights, w_near, *operands)
         return dict(zip(group, zip(outs[:size], outs[size : 2 * size]))), outs[-1]
 
     there = {"z0": marked}

time: 60.9 us -> 59.8 us (0.982)
  starting transfers between devices: 27.6 us -> 24.3 us
  waiting for transfers between devices: 21.3 us -> 23.8 us
  local copies, waits for them, and re-layouts: 0.78 us -> 0.1 us
    ppermute x29, starting transfers between devices: 27.6 us -> 24.3 us  [flipped(): lax.ppermute(x, axis, [(i, i ^ by) for i in range(lax.axis_size(axis))])]
    ppermute x29, waiting for transfers between devices: 21.3 us -> 23.8 us  [flipped(): lax.ppermute(x, axis, [(i, i ^ by) for i in range(lax.axis_size(axis))])]
    pallas_call x0 -> x1, Pallas kernels: none -> 1.39 us  [gathered_shards(): pl.pallas_call(near_kernel, out_shape=pltpu.VMEM((2, part_width, hidden_w...]
    pallas_call x2, Pallas kernels: 7.13 us -> 6.08 us  [experts(): pl.pallas_call(functools.partial(experts_kernel, seq_count, group, order)...]
    reshape x1, local copies, waits for them, and re-layouts: 0.69 us -> 0.01 us  [gathered_shards(): doc_ids.reshape(1, -1)]
  transfers between devices with their start and end apart: 29 -> 29, of which waited for: 13 -> 13; matrix products, arithmetic and copies ran while one was open for 3% -> 2% of each run, Pallas kernels for 12% -> 13%
where the time goes in v5:
time: 59.8 us; the launch traced here: 59.5 us
  starting transfers between devices  24.3 us (41%)
  waiting for transfers between devices  23.8 us (40%)
  Pallas kernels  9.05 us (15%)
  other arithmetic  2.07 us (3%)
    ppermute x29, starting transfers between devices, flipped(): lax.ppermute(x, axis, [(i, i ^ by) for i in range(lax.axis_size(axis))])  24.3 us
    ppermute x29, waiting for transfers between devices, flipped(): lax.ppermute(x, axis, [(i, i ^ by) for i in range(lax.axis_size(axis))])  23.8 us
    pallas_call x2, Pallas kernels, experts(): pl.pallas_call(functools.partial(experts_kernel, seq_count, group, order)...  6.08 us
    pallas_call x1, Pallas kernels, gathered_shards(): pl.pallas_call(near_kernel, out_shape=pltpu.VMEM((2, part_width, hidden_w...  1.39 us
  transfers between devices with their start and end apart: 29, of which 13 were waited for; matrix products, arithmetic and copies ran while one was open for 2% of the time, Pallas kernels for 13%

profile of v5, /device:TPU:0, one launch (start us, length us, event | category | flops | bytes accessed | tf_op | source)
XLA Modules:
  0.0 59.5 jit_solution(17627094106180884440)
XLA Ops:
  0.8 3.1 %collective-permute-start = (bf16[208,128]{1,0:T(8,128)(2,1)S(1)}, bf16[208,128]{1,0:T(8,128)(2,1)S(1)}, u32[]{:S(2)}, u32[]{:S(2)}) collective-permute-start(bf16[208,128]{1,0:T(8,128)(2,1)S(1)} %pack.1.refs_3_), channel_id=1, source_target_pairs={{0,8},{8,0},{16,24},{24,16},{1,9},{9,1},{17,25},{25,17},{2,10},{10... | collective-permute-start | bytes 159752 | tf_op jit(solution)/shard_map/ppermute | solution.py:27
  3.9 2.6 %collective-permute-start.1 = (bf16[208,128]{1,0:T(8,128)(2,1)S(1)}, bf16[208,128]{1,0:T(8,128)(2,1)S(1)}, u32[]{:S(2)}, u32[]{:S(2)}) collective-permute-start(bf16[208,128]{1,0:T(8,128)(2,1)S(1)} %pack.1.refs_3_), channel_id=1, source_target_pairs={{0,16},{8,24},{16,0},{24,8},{1,17},{9,25},{17,1},{25,9},{2,18},{10... | collective-permute-start | bytes 159752 | tf_op jit(solution)/shard_map/ppermute | solution.py:27
  7.5 1.4 %near.1.refs_4_ = bf16[2,768,512]{2,1,0:T(8,128)(2,1)S(1)} custom-call(s32[1]{0:T(128)} %bitcast.place_ref.refs_0_, bf16[1,3072,512]{2,1,0:T(8,128)(2,1)} %refs_2_.3), custom_call_target="tpu_custom_call" | custom-call | tf_op jit(solution)/shard_map/near/pallas_call | solution.py:376
  8.9 1.1 %collective-permute-done.1.refs_5_ = bf16[208,128]{1,0:T(8,128)(2,1)S(1)} collective-permute-done((bf16[208,128]{1,0:T(8,128)(2,1)S(1)}, bf16[208,128]{1,0:T(8,128)(2,1)S(1)}, u32[]{:S(2)}, u32[]{:S(2)}) %collective-permute-start.1) | collective-permute-done | bytes 53280 | tf_op jit(solution)/shard_map/ppermute | solution.py:27
  10.0 2.5 %collective-permute-done.2.refs_6_ = bf16[208,128]{1,0:T(8,128)(2,1)S(1)} collective-permute-done((bf16[208,128]{1,0:T(8,128)(2,1)S(1)}, bf16[208,128]{1,0:T(8,128)(2,1)S(1)}, u32[]{:S(2)}, u32[]{:S(2)}) %collective-permute-start.2) | collective-permute-done | bytes 53280 | tf_op jit(solution)/shard_map/ppermute | solution.py:27
  13.2 1.1 %collective-permute-start.5 = (bf16[96,768]{1,0:T(8,128)(2,1)S(1)}, bf16[96,768]{1,0:T(8,128)(2,1)S(1)}, u32[]{:S(2)}, u32[]{:S(2)}) collective-permute-start(bf16[96,768]{1,0:T(8,128)(2,1)S(1)} %get-tuple-element.33), channel_id=1, source_target_pairs={{0,24},{8,16},{16,8},{24,0},{1,25},{9,17},{17,9},{25,1},{2,26},{10... | collective-permute-start | bytes 442376 | tf_op jit(solution)/shard_map/ppermute | solution.py:27
  14.5 1.5 %collective-permute-start.4 = (bf16[112,768]{1,0:T(8,128)(2,1)S(1)}, bf16[112,768]{1,0:T(8,128)(2,1)S(1)}, u32[]{:S(2)}, u32[]{:S(2)}) collective-permute-start(bf16[112,768]{1,0:T(8,128)(2,1)S(1)} %get-tuple-element.32.refs_5_), channel_id=1, source_target_pairs={{0,4},{2,6},{4,0},{6,2},{1,5},{3,7},{5,1},{7,3},{8,12},{10,14},{12... | collective-permute-start | bytes 516104 | tf_op jit(solution)/shard_map/ppermute | solution.py:27
  16.0 3.2 %collective-permute-start.7 = (bf16[96,768]{1,0:T(8,128)(2,1)S(1)}, bf16[96,768]{1,0:T(8,128)(2,1)S(1)}, u32[]{:S(2)}, u32[]{:S(2)}) collective-permute-start(bf16[96,768]{1,0:T(8,128)(2,1)S(1)} %get-tuple-element.33), channel_id=1, source_target_pairs={{0,16},{8,24},{16,0},{24,8},{1,17},{9,25},{17,1},{25,9},{2,18},{10... | collective-permute-start | bytes 442376 | tf_op jit(solution)/shard_map/ppermute | solution.py:27
  19.2 1.6 %collective-permute-done.5.refs_9_ = bf16[96,768]{1,0:T(8,128)(2,1)S(1)} collective-permute-done((bf16[96,768]{1,0:T(8,128)(2,1)S(1)}, bf16[96,768]{1,0:T(8,128)(2,1)S(1)}, u32[]{:S(2)}, u32[]{:S(2)}) %collective-permute-start.5) | collective-permute-done | bytes 147488 | tf_op jit(solution)/shard_map/ppermute | solution.py:27
  20.8 1.8 %collective-permute-start.12 = (bf16[96,768]{1,0:T(8,128)(2,1)S(1)}, bf16[96,768]{1,0:T(8,128)(2,1)S(1)}, u32[]{:S(2)}, u32[]{:S(2)}) collective-permute-start(bf16[96,768]{1,0:T(8,128)(2,1)S(1)} %collective-permute-done.5.refs_9_), channel_id=1, source_target_pairs={{0,4},{2,6},{4,0},{6,2},{1,5},{3,7},{5,1},{7,3},{8,12},{10,14},{12... | collective-permute-start | bytes 442376 | tf_op jit(solution)/shard_map/ppermute | solution.py:27
  22.8 4.2 %collective-permute-done.7.refs_9_ = bf16[96,768]{1,0:T(8,128)(2,1)S(1)} collective-permute-done((bf16[96,768]{1,0:T(8,128)(2,1)S(1)}, bf16[96,768]{1,0:T(8,128)(2,1)S(1)}, u32[]{:S(2)}, u32[]{:S(2)}) %collective-permute-start.7) | collective-permute-done | bytes 147488 | tf_op jit(solution)/shard_map/ppermute | solution.py:27
  28.3 1.2 %collective-permute-start.9 = (bf16[96,768]{1,0:T(8,128)(2,1)S(1)}, bf16[96,768]{1,0:T(8,128)(2,1)S(1)}, u32[]{:S(2)}, u32[]{:S(2)}) collective-permute-start(bf16[96,768]{1,0:T(8,128)(2,1)S(1)} %collective-permute-done.7.refs_9_), channel_id=1, source_target_pairs={{0,4},{2,6},{4,0},{6,2},{1,5},{3,7},{5,1},{7,3},{8,12},{10,14},{12... | collective-permute-start | bytes 442376 | tf_op jit(solution)/shard_map/ppermute | solution.py:27
  29.7 3.0 %experts.2 = (bf16[48,3072]{1,0:T(8,128)(2,1)S(1)}, bf16[48,3072]{1,0:T(8,128)(2,1)S(1)}, bf16[48,3072]{1,0:T(8,128)(2,1)S(1)}, bf16[48,3072]{1,0:T(8,128)(2,1)S(1)}) custom-call(s32[1]{0:T(128)} %bitcast.place_ref.refs_0_, f32[4,1,768]{2,1,0:T(1,128)} %bitcast.14, bf16[1,3072,512]{2,1,0:T(8,128)(2,1)} %refs_2_.3, bf16[1,512,3072]{2,1,0:T(8,128)(2,1)} %refs_3_.3, ...), custom_call_target="tpu_custom_call" | custom-call | flops 1207959552 | bytes 8388608 | tf_op jit(solution)/shard_map/experts/pallas_call | solution.py:433
  32.7 1.8 %collective-permute-done.9.refs_11_ = bf16[96,768]{1,0:T(8,128)(2,1)S(1)} collective-permute-done((bf16[96,768]{1,0:T(8,128)(2,1)S(1)}, bf16[96,768]{1,0:T(8,128)(2,1)S(1)}, u32[]{:S(2)}, u32[]{:S(2)}) %collective-permute-start.9) | collective-permute-done | bytes 147488 | tf_op jit(solution)/shard_map/ppermute | solution.py:27
  36.2 1.1 %collective-permute-start.19 = (bf16[24,3072]{1,0:T(8,128)(2,1)S(1)}, bf16[24,3072]{1,0:T(8,128)(2,1)S(1)}, u32[]{:S(2)}, u32[]{:S(2)}) collective-permute-start(bf16[24,3072]{1,0:T(8,128)(2,1)S(1)} %slice.65), channel_id=1, source_target_pairs={{0,4},{2,6},{4,0},{6,2},{1,5},{3,7},{5,1},{7,3},{8,12},{10,14},{12... | collective-permute-start | bytes 442376 | tf_op jit(solution)/shard_map/ppermute | solution.py:27
  37.4 3.0 %experts.3 = (bf16[48,3072]{1,0:T(8,128)(2,1)S(1)}, bf16[48,3072]{1,0:T(8,128)(2,1)S(1)}, bf16[48,3072]{1,0:T(8,128)(2,1)S(1)}, bf16[48,3072]{1,0:T(8,128)(2,1)S(1)}, bf16[4,24,768]{2,1,0:T(8,128)(2,1)S(1)}) custom-call(s32[1]{0:T(128)} %bitcast.place_ref.refs_0_, f32[4,1,768]{2,1,0:T(1,128)} %bitcast.15, bf16[1,3072,512]{2,1,0:T(8,128)(2,1)} %refs_2_.3, ...), custom_call_target="tpu_custom_call" | custom-call | flops 1207959552 | bytes 8388608 | tf_op jit(solution)/shard_map/experts/pallas_call | solution.py:433
  41.1 1.1 %collective-permute-done.19 = bf16[24,3072]{1,0:T(8,128)(2,1)S(1)} collective-permute-done((bf16[24,3072]{1,0:T(8,128)(2,1)S(1)}, bf16[24,3072]{1,0:T(8,128)(2,1)S(1)}, u32[]{:S(2)}, u32[]{:S(2)}) %collective-permute-start.19) | collective-permute-done | bytes 147488 | tf_op jit(solution)/shard_map/ppermute | solution.py:27
  42.2 1.7 %collective-permute-start.20 = (bf16[24,3072]{1,0:T(8,128)(2,1)S(1)}, bf16[24,3072]{1,0:T(8,128)(2,1)S(1)}, u32[]{:S(2)}, u32[]{:S(2)}) collective-permute-start(bf16[24,3072]{1,0:T(8,128)(2,1)S(1)} %fusion.4), channel_id=1, source_target_pairs={{0,24},{8,16},{16,8},{24,0},{1,25},{9,17},{17,9},{25,1},{2,26},{10... | collective-permute-start | bytes 442376 | tf_op jit(solution)/shard_map/ppermute | solution.py:27
  44.0 1.7 %collective-permute-start.22 = (bf16[24,3072]{1,0:T(8,128)(2,1)S(1)}, bf16[24,3072]{1,0:T(8,128)(2,1)S(1)}, u32[]{:S(2)}, u32[]{:S(2)}) collective-permute-start(bf16[24,3072]{1,0:T(8,128)(2,1)S(1)} %slice.64), channel_id=1, source_target_pairs={{0,4},{2,6},{4,0},{6,2},{1,5},{3,7},{5,1},{7,3},{8,12},{10,14},{12... | collective-permute-start | bytes 442376 | tf_op jit(solution)/shard_map/ppermute | solution.py:27
  46.2 4.5 %collective-permute-done.22 = bf16[24,3072]{1,0:T(8,128)(2,1)S(1)} collective-permute-done((bf16[24,3072]{1,0:T(8,128)(2,1)S(1)}, bf16[24,3072]{1,0:T(8,128)(2,1)S(1)}, u32[]{:S(2)}, u32[]{:S(2)}) %collective-permute-start.22) | collective-permute-done | bytes 147488 | tf_op jit(solution)/shard_map/ppermute | solution.py:27
  50.8 1.5 %collective-permute-done.25 = bf16[24,3072]{1,0:T(8,128)(2,1)S(1)} collective-permute-done((bf16[24,3072]{1,0:T(8,128)(2,1)S(1)}, bf16[24,3072]{1,0:T(8,128)(2,1)S(1)}, u32[]{:S(2)}, u32[]{:S(2)}) %collective-permute-start.25) | collective-permute-done | bytes 147488 | tf_op jit(solution)/shard_map/ppermute | solution.py:27
  52.3 1.1 %collective-permute-start.26 = (bf16[24,3072]{1,0:T(8,128)(2,1)S(1)}, bf16[24,3072]{1,0:T(8,128)(2,1)S(1)}, u32[]{:S(2)}, u32[]{:S(2)}) collective-permute-start(bf16[24,3072]{1,0:T(8,128)(2,1)S(1)} %fusion.2), channel_id=1, source_target_pairs={{0,8},{8,0},{16,24},{24,16},{1,9},{9,1},{17,25},{25,17},{2,10},{10... | collective-permute-start | bytes 442376 | tf_op jit(solution)/shard_map/ppermute | solution.py:27
  53.4 1.0 %collective-permute-start.28 = (bf16[24,3072]{1,0:T(8,128)(2,1)S(1)}, bf16[24,3072]{1,0:T(8,128)(2,1)S(1)}, u32[]{:S(2)}, u32[]{:S(2)}) collective-permute-start(bf16[24,3072]{1,0:T(8,128)(2,1)S(1)} %slice.62), channel_id=1, source_target_pairs={{0,4},{2,6},{4,0},{6,2},{1,5},{3,7},{5,1},{7,3},{8,12},{10,14},{12... | collective-permute-start | bytes 442376 | tf_op jit(solution)/shard_map/ppermute | solution.py:27
  54.5 3.6 %collective-permute-done.23 = bf16[24,3072]{1,0:T(8,128)(2,1)S(1)} collective-permute-done((bf16[24,3072]{1,0:T(8,128)(2,1)S(1)}, bf16[24,3072]{1,0:T(8,128)(2,1)S(1)}, u32[]{:S(2)}, u32[]{:S(2)}) %collective-permute-start.23) | collective-permute-done | bytes 147488 | tf_op jit(solution)/shard_map/ppermute | solution.py:27
  (57 shorter events, 8.9 us)
Async XLA Ops:
  0.8 8.0 %collective-permute-start = (bf16[208,128]{1,0:T(8,128)(2,1)S(1)}, bf16[208,128]{1,0:T(8,128)(2,1)S(1)}, u32[]{:S(2)}, u32[]{:S(2)}) collective-permute-start(bf16[208,128]{1,0:T(8,128)(2,1)S(1)} %pack.1.refs_3_), channel_id=1, source_target_pairs={{0,8},{8,0},{16,24},{24,16},{1,9},{9,1},{17,25},{25,17},{2,10},{10... | collective-permute-start | bytes 159752 | tf_op jit(solution)/shard_map/ppermute | solution.py:27
  3.9 6.1 %collective-permute-start.1 = (bf16[208,128]{1,0:T(8,128)(2,1)S(1)}, bf16[208,128]{1,0:T(8,128)(2,1)S(1)}, u32[]{:S(2)}, u32[]{:S(2)}) collective-permute-start(bf16[208,128]{1,0:T(8,128)(2,1)S(1)} %pack.1.refs_3_), channel_id=1, source_target_pairs={{0,16},{8,24},{16,0},{24,8},{1,17},{9,25},{17,1},{25,9},{2,18},{10... | collective-permute-start | bytes 159752 | tf_op jit(solution)/shard_map/ppermute | solution.py:27
  6.5 5.9 %collective-permute-start.2 = (bf16[208,128]{1,0:T(8,128)(2,1)S(1)}, bf16[208,128]{1,0:T(8,128)(2,1)S(1)}, u32[]{:S(2)}, u32[]{:S(2)}) collective-permute-start(bf16[208,128]{1,0:T(8,128)(2,1)S(1)} %pack.1.refs_3_), channel_id=1, source_target_pairs={{0,24},{8,16},{16,8},{24,0},{1,25},{9,17},{17,9},{25,1},{2,26},{10... | collective-permute-start | bytes 159752 | tf_op jit(solution)/shard_map/ppermute | solution.py:27
  13.2 7.6 %collective-permute-start.5 = (bf16[96,768]{1,0:T(8,128)(2,1)S(1)}, bf16[96,768]{1,0:T(8,128)(2,1)S(1)}, u32[]{:S(2)}, u32[]{:S(2)}) collective-permute-start(bf16[96,768]{1,0:T(8,128)(2,1)S(1)} %get-tuple-element.33), channel_id=1, source_target_pairs={{0,24},{8,16},{16,8},{24,0},{1,25},{9,17},{17,9},{25,1},{2,26},{10... | collective-permute-start | bytes 442376 | tf_op jit(solution)/shard_map/ppermute | solution.py:27
  14.3 8.3 %collective-permute-start.14 = (bf16[96,768]{1,0:T(8,128)(2,1)S(1)}, bf16[96,768]{1,0:T(8,128)(2,1)S(1)}, u32[]{:S(2)}, u32[]{:S(2)}) collective-permute-start(bf16[96,768]{1,0:T(8,128)(2,1)S(1)} %get-tuple-element.33), channel_id=1, source_target_pairs={{0,8},{8,0},{16,24},{24,16},{1,9},{9,1},{17,25},{25,17},{2,10},{10... | collective-permute-start | bytes 442376 | tf_op jit(solution)/shard_map/ppermute | solution.py:27
  14.5 8.3 %collective-permute-start.4 = (bf16[112,768]{1,0:T(8,128)(2,1)S(1)}, bf16[112,768]{1,0:T(8,128)(2,1)S(1)}, u32[]{:S(2)}, u32[]{:S(2)}) collective-permute-start(bf16[112,768]{1,0:T(8,128)(2,1)S(1)} %get-tuple-element.32.refs_5_), channel_id=1, source_target_pairs={{0,4},{2,6},{4,0},{6,2},{1,5},{3,7},{5,1},{7,3},{8,12},{10,14},{12... | collective-permute-start | bytes 516104 | tf_op jit(solution)/shard_map/ppermute | solution.py:27
  16.0 11.2 %collective-permute-start.3 = (bf16[112,768]{1,0:T(8,128)(2,1)S(1)}, bf16[112,768]{1,0:T(8,128)(2,1)S(1)}, u32[]{:S(2)}, u32[]{:S(2)}) collective-permute-start(bf16[112,768]{1,0:T(8,128)(2,1)S(1)} %get-tuple-element.32.refs_5_), channel_id=1, source_target_pairs={{0,2},{2,0},{4,6},{6,4},{1,3},{3,1},{5,7},{7,5},{8,10},{10,8},{12,... | collective-permute-start | bytes 516104 | tf_op jit(solution)/shard_map/ppermute | solution.py:27
  16.0 11.0 %collective-permute-start.7 = (bf16[96,768]{1,0:T(8,128)(2,1)S(1)}, bf16[96,768]{1,0:T(8,128)(2,1)S(1)}, u32[]{:S(2)}, u32[]{:S(2)}) collective-permute-start(bf16[96,768]{1,0:T(8,128)(2,1)S(1)} %get-tuple-element.33), channel_id=1, source_target_pairs={{0,16},{8,24},{16,0},{24,8},{1,17},{9,25},{17,1},{25,9},{2,18},{10... | collective-permute-start | bytes 442376 | tf_op jit(solution)/shard_map/ppermute | solution.py:27
  20.8 6.8 %collective-permute-start.12 = (bf16[96,768]{1,0:T(8,128)(2,1)S(1)}, bf16[96,768]{1,0:T(8,128)(2,1)S(1)}, u32[]{:S(2)}, u32[]{:S(2)}) collective-permute-start(bf16[96,768]{1,0:T(8,128)(2,1)S(1)} %collective-permute-done.5.refs_9_), channel_id=1, source_target_pairs={{0,4},{2,6},{4,0},{6,2},{1,5},{3,7},{5,1},{7,3},{8,12},{10,14},{12... | collective-permute-start | bytes 442376 | tf_op jit(solution)/shard_map/ppermute | solution.py:27
  22.6 5.7 %collective-permute-start.16 = (bf16[96,768]{1,0:T(8,128)(2,1)S(1)}, bf16[96,768]{1,0:T(8,128)(2,1)S(1)}, u32[]{:S(2)}, u32[]{:S(2)}) collective-permute-start(bf16[96,768]{1,0:T(8,128)(2,1)S(1)} %collective-permute-done.14.refs_13_), channel_id=1, source_target_pairs={{0,4},{2,6},{4,0},{6,2},{1,5},{3,7},{5,1},{7,3},{8,12},{10,14},{12... | collective-permute-start | bytes 442376 | tf_op jit(solution)/shard_map/ppermute | solution.py:27
  22.8 5.5 %collective-permute-start.11 = (bf16[96,768]{1,0:T(8,128)(2,1)S(1)}, bf16[96,768]{1,0:T(8,128)(2,1)S(1)}, u32[]{:S(2)}, u32[]{:S(2)}) collective-permute-start(bf16[96,768]{1,0:T(8,128)(2,1)S(1)} %collective-permute-done.5.refs_9_), channel_id=1, source_target_pairs={{0,2},{2,0},{4,6},{6,4},{1,3},{3,1},{5,7},{7,5},{8,10},{10,8},{12,... | collective-permute-start | bytes 442376 | tf_op jit(solution)/shard_map/ppermute | solution.py:27
  27.1 2.5 %collective-permute-start.6 = (bf16[112,768]{1,0:T(8,128)(2,1)S(1)}, bf16[112,768]{1,0:T(8,128)(2,1)S(1)}, u32[]{:S(2)}, u32[]{:S(2)}) collective-permute-start(bf16[112,768]{1,0:T(8,128)(2,1)S(1)} %collective-permute-done.4.refs_7_), channel_id=1, source_target_pairs={{0,2},{2,0},{4,6},{6,4},{1,3},{3,1},{5,7},{7,5},{8,10},{10,8},{12,... | collective-permute-start | bytes 516104 | tf_op jit(solution)/shard_map/ppermute | solution.py:27
  28.3 6.3 %collective-permute-start.9 = (bf16[96,768]{1,0:T(8,128)(2,1)S(1)}, bf16[96,768]{1,0:T(8,128)(2,1)S(1)}, u32[]{:S(2)}, u32[]{:S(2)}) collective-permute-start(bf16[96,768]{1,0:T(8,128)(2,1)S(1)} %collective-permute-done.7.refs_9_), channel_id=1, source_target_pairs={{0,4},{2,6},{4,0},{6,2},{1,5},{3,7},{5,1},{7,3},{8,12},{10,14},{12... | collective-permute-start | bytes 442376 | tf_op jit(solution)/shard_map/ppermute | solution.py:27
  34.6 2.8 %collective-permute-start.8 = (bf16[96,768]{1,0:T(8,128)(2,1)S(1)}, bf16[96,768]{1,0:T(8,128)(2,1)S(1)}, u32[]{:S(2)}, u32[]{:S(2)}) collective-permute-start(bf16[96,768]{1,0:T(8,128)(2,1)S(1)} %collective-permute-done.7.refs_9_), channel_id=1, source_target_pairs={{0,2},{2,0},{4,6},{6,4},{1,3},{3,1},{5,7},{7,5},{8,10},{10,8},{12,... | collective-permute-start | bytes 442376 | tf_op jit(solution)/shard_map/ppermute | solution.py:27
  35.1 5.4 %collective-permute-start.24 = (bf16[48,3072]{1,0:T(8,128)(2,1)S(1)}, bf16[48,3072]{1,0:T(8,128)(2,1)S(1)}, u32[]{:S(2)}, u32[]{:S(2)}) collective-permute-start(bf16[48,3072]{1,0:T(8,128)(2,1)S(1)} %get-tuple-element.44), channel_id=1, source_target_pairs={{0,2},{2,0},{4,6},{6,4},{1,3},{3,1},{5,7},{7,5},{8,10},{10,8},{12,... | collective-permute-start | bytes 884744 | tf_op jit(solution)/shard_map/ppermute | solution.py:27
  36.2 6.0 %collective-permute-start.19 = (bf16[24,3072]{1,0:T(8,128)(2,1)S(1)}, bf16[24,3072]{1,0:T(8,128)(2,1)S(1)}, u32[]{:S(2)}, u32[]{:S(2)}) collective-permute-start(bf16[24,3072]{1,0:T(8,128)(2,1)S(1)} %slice.65), channel_id=1, source_target_pairs={{0,4},{2,6},{4,0},{6,2},{1,5},{3,7},{5,1},{7,3},{8,12},{10,14},{12... | collective-permute-start | bytes 442376 | tf_op jit(solution)/shard_map/ppermute | solution.py:27
  40.4 3.5 %collective-permute-start.21 = (bf16[48,3072]{1,0:T(8,128)(2,1)S(1)}, bf16[48,3072]{1,0:T(8,128)(2,1)S(1)}, u32[]{:S(2)}, u32[]{:S(2)}) collective-permute-start(bf16[48,3072]{1,0:T(8,128)(2,1)S(1)} %get-tuple-element.41), channel_id=1, source_target_pairs={{0,2},{2,0},{4,6},{6,4},{1,3},{3,1},{5,7},{7,5},{8,10},{10,8},{12,... | collective-permute-start | bytes 884744 | tf_op jit(solution)/shard_map/ppermute | solution.py:27
  40.6 5.5 %collective-permute-start.27 = (bf16[48,3072]{1,0:T(8,128)(2,1)S(1)}, bf16[48,3072]{1,0:T(8,128)(2,1)S(1)}, u32[]{:S(2)}, u32[]{:S(2)}) collective-permute-start(bf16[48,3072]{1,0:T(8,128)(2,1)S(1)} %get-tuple-element.47), channel_id=1, source_target_pairs={{0,2},{2,0},{4,6},{6,4},{1,3},{3,1},{5,7},{7,5},{8,10},{10,8},{12,... | collective-permute-start | bytes 884744 | tf_op jit(solution)/shard_map/ppermute | solution.py:27
  42.2 12.3 %collective-permute-start.20 = (bf16[24,3072]{1,0:T(8,128)(2,1)S(1)}, bf16[24,3072]{1,0:T(8,128)(2,1)S(1)}, u32[]{:S(2)}, u32[]{:S(2)}) collective-permute-start(bf16[24,3072]{1,0:T(8,128)(2,1)S(1)} %fusion.4), channel_id=1, source_target_pairs={{0,24},{8,16},{16,8},{24,0},{1,25},{9,17},{17,9},{25,1},{2,26},{10... | collective-permute-start | bytes 442376 | tf_op jit(solution)/shard_map/ppermute | solution.py:27
  44.0 6.7 %collective-permute-start.22 = (bf16[24,3072]{1,0:T(8,128)(2,1)S(1)}, bf16[24,3072]{1,0:T(8,128)(2,1)S(1)}, u32[]{:S(2)}, u32[]{:S(2)}) collective-permute-start(bf16[24,3072]{1,0:T(8,128)(2,1)S(1)} %slice.64), channel_id=1, source_target_pairs={{0,4},{2,6},{4,0},{6,2},{1,5},{3,7},{5,1},{7,3},{8,12},{10,14},{12... | collective-permute-start | bytes 442376 | tf_op jit(solution)/shard_map/ppermute | solution.py:27
  45.7 6.6 %collective-permute-start.25 = (bf16[24,3072]{1,0:T(8,128)(2,1)S(1)}, bf16[24,3072]{1,0:T(8,128)(2,1)S(1)}, u32[]{:S(2)}, u32[]{:S(2)}) collective-permute-start(bf16[24,3072]{1,0:T(8,128)(2,1)S(1)} %slice.63), channel_id=1, source_target_pairs={{0,4},{2,6},{4,0},{6,2},{1,5},{3,7},{5,1},{7,3},{8,12},{10,14},{12... | collective-permute-start | bytes 442376 | tf_op jit(solution)/shard_map/ppermute | solution.py:27
  50.7 7.5 %collective-permute-start.23 = (bf16[24,3072]{1,0:T(8,128)(2,1)S(1)}, bf16[24,3072]{1,0:T(8,128)(2,1)S(1)}, u32[]{:S(2)}, u32[]{:S(2)}) collective-permute-start(bf16[24,3072]{1,0:T(8,128)(2,1)S(1)} %fusion.3), channel_id=1, source_target_pairs={{0,16},{8,24},{16,0},{24,8},{1,17},{9,25},{17,1},{25,9},{2,18},{10... | collective-permute-start | bytes 442376 | tf_op jit(solution)/shard_map/ppermute | solution.py:27
  52.3 6.5 %collective-permute-start.26 = (bf16[24,3072]{1,0:T(8,128)(2,1)S(1)}, bf16[24,3072]{1,0:T(8,128)(2,1)S(1)}, u32[]{:S(2)}, u32[]{:S(2)}) collective-permute-start(bf16[24,3072]{1,0:T(8,128)(2,1)S(1)} %fusion.2), channel_id=1, source_target_pairs={{0,8},{8,0},{16,24},{24,16},{1,9},{9,1},{17,25},{25,17},{2,10},{10... | collective-permute-start | bytes 442376 | tf_op jit(solution)/shard_map/ppermute | solution.py:27
  53.4 5.3 %collective-permute-start.28 = (bf16[24,3072]{1,0:T(8,128)(2,1)S(1)}, bf16[24,3072]{1,0:T(8,128)(2,1)S(1)}, u32[]{:S(2)}, u32[]{:S(2)}) collective-permute-start(bf16[24,3072]{1,0:T(8,128)(2,1)S(1)} %slice.62), channel_id=1, source_target_pairs={{0,4},{2,6},{4,0},{6,2},{1,5},{3,7},{5,1},{7,3},{8,12},{10,14},{12... | collective-permute-start | bytes 442376 | tf_op jit(solution)/shard_map/ppermute | solution.py:27
  (6 other events, 18.4 us)

commit v6 on v5

--- a/solution.py
+++ b/solution.py
@@ -13,8 +13,8 @@
 epsilon = 1e-05
 
 GROUPS = [[3, 1], [2, 0]]
-SEQUENCE = ['z3', 'z1', 'z2', 'd0', 'x3', 'd3', 'x1', 'd1', 'x2', 'd2', 'e1', 'e2', 'x0', 'e0', 'e3', 'g0', 'r1', 'r3', 'g1', 'r2', 'y1', 'r0', 'y3', 'w3', 'y2', 'w2', 'w1', 'y0']
-WAITS = {'e0': ('z3',), 'g1': ('r3',), 'r1': ('x1', 'x2'), 'r3': ('x2',), 'y0': ('y2',), 'y1': ('r2',)}
+SEQUENCE = ['z3', 'z1', 'z2', 'd0', 'x3', 'd3', 'x1', 'd1', 'x2', 'd2', 'e1', 'e2', 'x0', 'e0', 'e3', 'g0', 'r3', 'r1', 'g1', 'r2', 'y1', 'r0', 'y3', 'w3', 'y2', 'w2', 'w1', 'y0']
+WAITS = {'d3': ('z1',), 'e0': ('z3',), 'e2': ('x3',), 'g1': ('r3',), 'r1': ('x2',), 'r3': ('x2',), 'y0': ('y2',), 'y1': ('r2',)}
 
 
 def shifted(x, axis, by):
@@ -375,10 +375,10 @@
     w_in_here, _ = lax.optimization_barrier((w_in, pack))
     w_near = pl.pallas_call(
         near_kernel,
-        out_shape=pltpu.VMEM((2, part_width, hidden_width), w_in.dtype),
+        out_shape=pltpu.VMEM((3, part_width, hidden_width), w_in.dtype),
         in_specs=[pl.BlockSpec(memory_space=pltpu.SMEM), anywhere()],
         out_specs=vmem(),
-        scratch_shapes=[pltpu.SemaphoreType.DMA((2,))],
+        scratch_shapes=[pltpu.SemaphoreType.DMA((3,))],
         compiler_params=pltpu.CompilerParams(vmem_limit_bytes=4 << 20),
         name="near",
     )(exp_index.reshape(1), pltpu.with_memory_space_constraint(w_in_here, pltpu.HBM))

time: 59.8 us -> 59.8 us (level)
  starting transfers between devices: 24.3 us -> 24.9 us
    ppermute x29, starting transfers between devices: 24.3 us -> 24.9 us  [flipped(): lax.ppermute(x, axis, [(i, i ^ by) for i in range(lax.axis_size(axis))])]
  transfers between devices with their start and end apart: 29 -> 29, of which waited for: 13 -> 14; matrix products, arithmetic and copies ran while one was open for 2% -> 2% of each run, Pallas kernels for 13% -> 12%
where the time goes in v6:
time: 59.8 us; the launch traced here: 59.5 us
  starting transfers between devices  24.9 us (42%)
  waiting for transfers between devices  23.5 us (39%)
  Pallas kernels  8.81 us (15%)
  other arithmetic  2.05 us (3%)
    ppermute x29, starting transfers between devices, flipped(): lax.ppermute(x, axis, [(i, i ^ by) for i in range(lax.axis_size(axis))])  24.9 us
    ppermute x29, waiting for transfers between devices, flipped(): lax.ppermute(x, axis, [(i, i ^ by) for i in range(lax.axis_size(axis))])  23.5 us
    pallas_call x2, Pallas kernels, experts(): pl.pallas_call(functools.partial(experts_kernel, seq_count, group, order)...  5.59 us
    pallas_call x1, Pallas kernels, gathered_shards(): pl.pallas_call(near_kernel, out_shape=pltpu.VMEM((3, part_width, hidden_w...  1.64 us
  transfers between devices with their start and end apart: 29, of which 14 were waited for; matrix products, arithmetic and copies ran while one was open for 2% of the time, Pallas kernels for 12%

profile of v6, /device:TPU:0, one launch (start us, length us, event | category | flops | bytes accessed | tf_op | source)
XLA Modules:
  0.0 59.5 jit_solution(2387080818901722208)
XLA Ops:
  0.8 3.1 %collective-permute-start = (bf16[208,128]{1,0:T(8,128)(2,1)S(1)}, bf16[208,128]{1,0:T(8,128)(2,1)S(1)}, u32[]{:S(2)}, u32[]{:S(2)}) collective-permute-start(bf16[208,128]{1,0:T(8,128)(2,1)S(1)} %pack.1.refs_3_), channel_id=1, source_target_pairs={{0,8},{8,0},{16,24},{24,16},{1,9},{9,1},{17,25},{25,17},{2,10},{10... | collective-permute-start | bytes 159752 | tf_op jit(solution)/shard_map/ppermute | solution.py:27
  3.9 2.6 %collective-permute-start.1 = (bf16[208,128]{1,0:T(8,128)(2,1)S(1)}, bf16[208,128]{1,0:T(8,128)(2,1)S(1)}, u32[]{:S(2)}, u32[]{:S(2)}) collective-permute-start(bf16[208,128]{1,0:T(8,128)(2,1)S(1)} %pack.1.refs_3_), channel_id=1, source_target_pairs={{0,16},{8,24},{16,0},{24,8},{1,17},{9,25},{17,1},{25,9},{2,18},{10... | collective-permute-start | bytes 159752 | tf_op jit(solution)/shard_map/ppermute | solution.py:27
  6.5 0.9 %broadcast_multiply_fusion.refs_1_ = bf16[6,96,128]{2,1,0:T(8,128)(2,1)S(1)} fusion(bf16[6,96,128]{2,1,0:T(8,128)(2,1)} %bitcast.13), kind=kLoop, calls=%fused_computation.18 | loop fusion | flops 73728 | bytes 294912 | tf_op jit(solution)/shard_map/mul | solution.py:374
  7.5 1.6 %near.1.refs_4_ = bf16[3,768,512]{2,1,0:T(8,128)(2,1)S(1)} custom-call(s32[1]{0:T(128)} %bitcast.place_ref.refs_0_, bf16[1,3072,512]{2,1,0:T(8,128)(2,1)} %refs_2_.3), custom_call_target="tpu_custom_call" | custom-call | tf_op jit(solution)/shard_map/near/pallas_call | solution.py:376
  10.0 2.5 %collective-permute-done.2.refs_6_ = bf16[208,128]{1,0:T(8,128)(2,1)S(1)} collective-permute-done((bf16[208,128]{1,0:T(8,128)(2,1)S(1)}, bf16[208,128]{1,0:T(8,128)(2,1)S(1)}, u32[]{:S(2)}, u32[]{:S(2)}) %collective-permute-start.2) | collective-permute-done | bytes 53280 | tf_op jit(solution)/shard_map/ppermute | solution.py:27
  13.2 1.1 %collective-permute-start.5 = (bf16[96,768]{1,0:T(8,128)(2,1)S(1)}, bf16[96,768]{1,0:T(8,128)(2,1)S(1)}, u32[]{:S(2)}, u32[]{:S(2)}) collective-permute-start(bf16[96,768]{1,0:T(8,128)(2,1)S(1)} %get-tuple-element.35), channel_id=1, source_target_pairs={{0,24},{8,16},{16,8},{24,0},{1,25},{9,17},{17,9},{25,1},{2,26},{10... | collective-permute-start | bytes 442376 | tf_op jit(solution)/shard_map/ppermute | solution.py:27
  14.5 1.5 %collective-permute-start.4 = (bf16[112,768]{1,0:T(8,128)(2,1)S(1)}, bf16[112,768]{1,0:T(8,128)(2,1)S(1)}, u32[]{:S(2)}, u32[]{:S(2)}) collective-permute-start(bf16[112,768]{1,0:T(8,128)(2,1)S(1)} %get-tuple-element.34.refs_5_), channel_id=1, source_target_pairs={{0,4},{2,6},{4,0},{6,2},{1,5},{3,7},{5,1},{7,3},{8,12},{10,14},{12... | collective-permute-start | bytes 516104 | tf_op jit(solution)/shard_map/ppermute | solution.py:27
  16.0 3.2 %collective-permute-start.7 = (bf16[96,768]{1,0:T(8,128)(2,1)S(1)}, bf16[96,768]{1,0:T(8,128)(2,1)S(1)}, u32[]{:S(2)}, u32[]{:S(2)}) collective-permute-start(bf16[96,768]{1,0:T(8,128)(2,1)S(1)} %get-tuple-element.35), channel_id=1, source_target_pairs={{0,16},{8,24},{16,0},{24,8},{1,17},{9,25},{17,1},{25,9},{2,18},{10... | collective-permute-start | bytes 442376 | tf_op jit(solution)/shard_map/ppermute | solution.py:27
  19.2 1.6 %collective-permute-done.5.refs_9_ = bf16[96,768]{1,0:T(8,128)(2,1)S(1)} collective-permute-done((bf16[96,768]{1,0:T(8,128)(2,1)S(1)}, bf16[96,768]{1,0:T(8,128)(2,1)S(1)}, u32[]{:S(2)}, u32[]{:S(2)}) %collective-permute-start.5) | collective-permute-done | bytes 147488 | tf_op jit(solution)/shard_map/ppermute | solution.py:27
  20.8 1.8 %collective-permute-start.10 = (bf16[96,768]{1,0:T(8,128)(2,1)S(1)}, bf16[96,768]{1,0:T(8,128)(2,1)S(1)}, u32[]{:S(2)}, u32[]{:S(2)}) collective-permute-start(bf16[96,768]{1,0:T(8,128)(2,1)S(1)} %collective-permute-done.5.refs_9_), channel_id=1, source_target_pairs={{0,4},{2,6},{4,0},{6,2},{1,5},{3,7},{5,1},{7,3},{8,12},{10,14},{12... | collective-permute-start | bytes 442376 | tf_op jit(solution)/shard_map/ppermute | solution.py:27
  23.3 3.7 %collective-permute-done.7.refs_9_ = bf16[96,768]{1,0:T(8,128)(2,1)S(1)} collective-permute-done((bf16[96,768]{1,0:T(8,128)(2,1)S(1)}, bf16[96,768]{1,0:T(8,128)(2,1)S(1)}, u32[]{:S(2)}, u32[]{:S(2)}) %collective-permute-start.7) | collective-permute-done | bytes 147488 | tf_op jit(solution)/shard_map/ppermute | solution.py:27
  28.3 1.2 %collective-permute-start.9 = (bf16[96,768]{1,0:T(8,128)(2,1)S(1)}, bf16[96,768]{1,0:T(8,128)(2,1)S(1)}, u32[]{:S(2)}, u32[]{:S(2)}) collective-permute-start(bf16[96,768]{1,0:T(8,128)(2,1)S(1)} %collective-permute-done.7.refs_9_), channel_id=1, source_target_pairs={{0,4},{2,6},{4,0},{6,2},{1,5},{3,7},{5,1},{7,3},{8,12},{10,14},{12... | collective-permute-start | bytes 442376 | tf_op jit(solution)/shard_map/ppermute | solution.py:27
  29.7 2.8 %experts.2 = (bf16[48,3072]{1,0:T(8,128)(2,1)S(1)}, bf16[48,3072]{1,0:T(8,128)(2,1)S(1)}, bf16[48,3072]{1,0:T(8,128)(2,1)S(1)}, bf16[48,3072]{1,0:T(8,128)(2,1)S(1)}) custom-call(s32[1]{0:T(128)} %bitcast.place_ref.refs_0_, f32[4,1,768]{2,1,0:T(1,128)} %bitcast.14, bf16[1,3072,512]{2,1,0:T(8,128)(2,1)} %refs_2_.3, bf16[1,512,3072]{2,1,0:T(8,128)(2,1)} %refs_3_.3, ...), custom_call_target="tpu_custom_call" | custom-call | flops 1207959552 | bytes 8388608 | tf_op jit(solution)/shard_map/experts/pallas_call | solution.py:433
  32.5 2.1 %collective-permute-done.9.refs_11_ = bf16[96,768]{1,0:T(8,128)(2,1)S(1)} collective-permute-done((bf16[96,768]{1,0:T(8,128)(2,1)S(1)}, bf16[96,768]{1,0:T(8,128)(2,1)S(1)}, u32[]{:S(2)}, u32[]{:S(2)}) %collective-permute-start.9) | collective-permute-done | bytes 147488 | tf_op jit(solution)/shard_map/ppermute | solution.py:27
  36.2 1.1 %collective-permute-start.19 = (bf16[24,3072]{1,0:T(8,128)(2,1)S(1)}, bf16[24,3072]{1,0:T(8,128)(2,1)S(1)}, u32[]{:S(2)}, u32[]{:S(2)}) collective-permute-start(bf16[24,3072]{1,0:T(8,128)(2,1)S(1)} %slice.65), channel_id=1, source_target_pairs={{0,4},{2,6},{4,0},{6,2},{1,5},{3,7},{5,1},{7,3},{8,12},{10,14},{12... | collective-permute-start | bytes 442376 | tf_op jit(solution)/shard_map/ppermute | solution.py:27
  37.4 2.8 %experts.3 = (bf16[48,3072]{1,0:T(8,128)(2,1)S(1)}, bf16[48,3072]{1,0:T(8,128)(2,1)S(1)}, bf16[48,3072]{1,0:T(8,128)(2,1)S(1)}, bf16[48,3072]{1,0:T(8,128)(2,1)S(1)}, bf16[4,24,768]{2,1,0:T(8,128)(2,1)S(1)}) custom-call(s32[1]{0:T(128)} %bitcast.place_ref.refs_0_, f32[4,1,768]{2,1,0:T(1,128)} %bitcast.15, bf16[1,3072,512]{2,1,0:T(8,128)(2,1)} %refs_2_.3, ...), custom_call_target="tpu_custom_call" | custom-call | flops 1207959552 | bytes 8388608 | tf_op jit(solution)/shard_map/experts/pallas_call | solution.py:433
  40.9 1.3 %collective-permute-done.19 = bf16[24,3072]{1,0:T(8,128)(2,1)S(1)} collective-permute-done((bf16[24,3072]{1,0:T(8,128)(2,1)S(1)}, bf16[24,3072]{1,0:T(8,128)(2,1)S(1)}, u32[]{:S(2)}, u32[]{:S(2)}) %collective-permute-start.19) | collective-permute-done | bytes 147488 | tf_op jit(solution)/shard_map/ppermute | solution.py:27
  42.2 1.9 %collective-permute-start.20 = (bf16[24,3072]{1,0:T(8,128)(2,1)S(1)}, bf16[24,3072]{1,0:T(8,128)(2,1)S(1)}, u32[]{:S(2)}, u32[]{:S(2)}) collective-permute-start(bf16[24,3072]{1,0:T(8,128)(2,1)S(1)} %fusion.4), channel_id=1, source_target_pairs={{0,24},{8,16},{16,8},{24,0},{1,25},{9,17},{17,9},{25,1},{2,26},{10... | collective-permute-start | bytes 442376 | tf_op jit(solution)/shard_map/ppermute | solution.py:27
  44.3 1.7 %collective-permute-start.22 = (bf16[24,3072]{1,0:T(8,128)(2,1)S(1)}, bf16[24,3072]{1,0:T(8,128)(2,1)S(1)}, u32[]{:S(2)}, u32[]{:S(2)}) collective-permute-start(bf16[24,3072]{1,0:T(8,128)(2,1)S(1)} %slice.64), channel_id=1, source_target_pairs={{0,4},{2,6},{4,0},{6,2},{1,5},{3,7},{5,1},{7,3},{8,12},{10,14},{12... | collective-permute-start | bytes 442376 | tf_op jit(solution)/shard_map/ppermute | solution.py:27
  46.5 4.2 %collective-permute-done.22 = bf16[24,3072]{1,0:T(8,128)(2,1)S(1)} collective-permute-done((bf16[24,3072]{1,0:T(8,128)(2,1)S(1)}, bf16[24,3072]{1,0:T(8,128)(2,1)S(1)}, u32[]{:S(2)}, u32[]{:S(2)}) %collective-permute-start.22) | collective-permute-done | bytes 147488 | tf_op jit(solution)/shard_map/ppermute | solution.py:27
  50.8 1.5 %collective-permute-done.25 = bf16[24,3072]{1,0:T(8,128)(2,1)S(1)} collective-permute-done((bf16[24,3072]{1,0:T(8,128)(2,1)S(1)}, bf16[24,3072]{1,0:T(8,128)(2,1)S(1)}, u32[]{:S(2)}, u32[]{:S(2)}) %collective-permute-start.25) | collective-permute-done | bytes 147488 | tf_op jit(solution)/shard_map/ppermute | solution.py:27
  52.3 1.1 %collective-permute-start.26 = (bf16[24,3072]{1,0:T(8,128)(2,1)S(1)}, bf16[24,3072]{1,0:T(8,128)(2,1)S(1)}, u32[]{:S(2)}, u32[]{:S(2)}) collective-permute-start(bf16[24,3072]{1,0:T(8,128)(2,1)S(1)} %fusion.2), channel_id=1, source_target_pairs={{0,8},{8,0},{16,24},{24,16},{1,9},{9,1},{17,25},{25,17},{2,10},{10... | collective-permute-start | bytes 442376 | tf_op jit(solution)/shard_map/ppermute | solution.py:27
  53.4 1.0 %collective-permute-start.28 = (bf16[24,3072]{1,0:T(8,128)(2,1)S(1)}, bf16[24,3072]{1,0:T(8,128)(2,1)S(1)}, u32[]{:S(2)}, u32[]{:S(2)}) collective-permute-start(bf16[24,3072]{1,0:T(8,128)(2,1)S(1)} %slice.62), channel_id=1, source_target_pairs={{0,4},{2,6},{4,0},{6,2},{1,5},{3,7},{5,1},{7,3},{8,12},{10,14},{12... | collective-permute-start | bytes 442376 | tf_op jit(solution)/shard_map/ppermute | solution.py:27
  54.5 3.6 %collective-permute-done.23 = bf16[24,3072]{1,0:T(8,128)(2,1)S(1)} collective-permute-done((bf16[24,3072]{1,0:T(8,128)(2,1)S(1)}, bf16[24,3072]{1,0:T(8,128)(2,1)S(1)}, u32[]{:S(2)}, u32[]{:S(2)}) %collective-permute-start.23) | collective-permute-done | bytes 147488 | tf_op jit(solution)/shard_map/ppermute | solution.py:27
  (57 shorter events, 9.3 us)
Async XLA Ops:
  0.8 8.3 %collective-permute-start = (bf16[208,128]{1,0:T(8,128)(2,1)S(1)}, bf16[208,128]{1,0:T(8,128)(2,1)S(1)}, u32[]{:S(2)}, u32[]{:S(2)}) collective-permute-start(bf16[208,128]{1,0:T(8,128)(2,1)S(1)} %pack.1.refs_3_), channel_id=1, source_target_pairs={{0,8},{8,0},{16,24},{24,16},{1,9},{9,1},{17,25},{25,17},{2,10},{10... | collective-permute-start | bytes 159752 | tf_op jit(solution)/shard_map/ppermute | solution.py:27
  3.9 6.1 %collective-permute-start.1 = (bf16[208,128]{1,0:T(8,128)(2,1)S(1)}, bf16[208,128]{1,0:T(8,128)(2,1)S(1)}, u32[]{:S(2)}, u32[]{:S(2)}) collective-permute-start(bf16[208,128]{1,0:T(8,128)(2,1)S(1)} %pack.1.refs_3_), channel_id=1, source_target_pairs={{0,16},{8,24},{16,0},{24,8},{1,17},{9,25},{17,1},{25,9},{2,18},{10... | collective-permute-start | bytes 159752 | tf_op jit(solution)/shard_map/ppermute | solution.py:27
  6.5 5.9 %collective-permute-start.2 = (bf16[208,128]{1,0:T(8,128)(2,1)S(1)}, bf16[208,128]{1,0:T(8,128)(2,1)S(1)}, u32[]{:S(2)}, u32[]{:S(2)}) collective-permute-start(bf16[208,128]{1,0:T(8,128)(2,1)S(1)} %pack.1.refs_3_), channel_id=1, source_target_pairs={{0,24},{8,16},{16,8},{24,0},{1,25},{9,17},{17,9},{25,1},{2,26},{10... | collective-permute-start | bytes 159752 | tf_op jit(solution)/shard_map/ppermute | solution.py:27
  13.2 7.6 %collective-permute-start.5 = (bf16[96,768]{1,0:T(8,128)(2,1)S(1)}, bf16[96,768]{1,0:T(8,128)(2,1)S(1)}, u32[]{:S(2)}, u32[]{:S(2)}) collective-permute-start(bf16[96,768]{1,0:T(8,128)(2,1)S(1)} %get-tuple-element.35), channel_id=1, source_target_pairs={{0,24},{8,16},{16,8},{24,0},{1,25},{9,17},{17,9},{25,1},{2,26},{10... | collective-permute-start | bytes 442376 | tf_op jit(solution)/shard_map/ppermute | solution.py:27
  14.3 8.4 %collective-permute-start.12 = (bf16[96,768]{1,0:T(8,128)(2,1)S(1)}, bf16[96,768]{1,0:T(8,128)(2,1)S(1)}, u32[]{:S(2)}, u32[]{:S(2)}) collective-permute-start(bf16[96,768]{1,0:T(8,128)(2,1)S(1)} %get-tuple-element.35), channel_id=1, source_target_pairs={{0,8},{8,0},{16,24},{24,16},{1,9},{9,1},{17,25},{25,17},{2,10},{10... | collective-permute-start | bytes 442376 | tf_op jit(solution)/shard_map/ppermute | solution.py:27
  14.5 8.8 %collective-permute-start.4 = (bf16[112,768]{1,0:T(8,128)(2,1)S(1)}, bf16[112,768]{1,0:T(8,128)(2,1)S(1)}, u32[]{:S(2)}, u32[]{:S(2)}) collective-permute-start(bf16[112,768]{1,0:T(8,128)(2,1)S(1)} %get-tuple-element.34.refs_5_), channel_id=1, source_target_pairs={{0,4},{2,6},{4,0},{6,2},{1,5},{3,7},{5,1},{7,3},{8,12},{10,14},{12... | collective-permute-start | bytes 516104 | tf_op jit(solution)/shard_map/ppermute | solution.py:27
  16.0 11.2 %collective-permute-start.3 = (bf16[112,768]{1,0:T(8,128)(2,1)S(1)}, bf16[112,768]{1,0:T(8,128)(2,1)S(1)}, u32[]{:S(2)}, u32[]{:S(2)}) collective-permute-start(bf16[112,768]{1,0:T(8,128)(2,1)S(1)} %get-tuple-element.34.refs_5_), channel_id=1, source_target_pairs={{0,2},{2,0},{4,6},{6,4},{1,3},{3,1},{5,7},{7,5},{8,10},{10,8},{12,... | collective-permute-start | bytes 516104 | tf_op jit(solution)/shard_map/ppermute | solution.py:27
  16.0 11.0 %collective-permute-start.7 = (bf16[96,768]{1,0:T(8,128)(2,1)S(1)}, bf16[96,768]{1,0:T(8,128)(2,1)S(1)}, u32[]{:S(2)}, u32[]{:S(2)}) collective-permute-start(bf16[96,768]{1,0:T(8,128)(2,1)S(1)} %get-tuple-element.35), channel_id=1, source_target_pairs={{0,16},{8,24},{16,0},{24,8},{1,17},{9,25},{17,1},{25,9},{2,18},{10... | collective-permute-start | bytes 442376 | tf_op jit(solution)/shard_map/ppermute | solution.py:27
  20.8 6.8 %collective-permute-start.10 = (bf16[96,768]{1,0:T(8,128)(2,1)S(1)}, bf16[96,768]{1,0:T(8,128)(2,1)S(1)}, u32[]{:S(2)}, u32[]{:S(2)}) collective-permute-start(bf16[96,768]{1,0:T(8,128)(2,1)S(1)} %collective-permute-done.5.refs_9_), channel_id=1, source_target_pairs={{0,4},{2,6},{4,0},{6,2},{1,5},{3,7},{5,1},{7,3},{8,12},{10,14},{12... | collective-permute-start | bytes 442376 | tf_op jit(solution)/shard_map/ppermute | solution.py:27
  22.7 5.6 %collective-permute-start.16 = (bf16[96,768]{1,0:T(8,128)(2,1)S(1)}, bf16[96,768]{1,0:T(8,128)(2,1)S(1)}, u32[]{:S(2)}, u32[]{:S(2)}) collective-permute-start(bf16[96,768]{1,0:T(8,128)(2,1)S(1)} %collective-permute-done.12.refs_13_), channel_id=1, source_target_pairs={{0,4},{2,6},{4,0},{6,2},{1,5},{3,7},{5,1},{7,3},{8,12},{10,14},{12... | collective-permute-start | bytes 442376 | tf_op jit(solution)/shard_map/ppermute | solution.py:27
  23.3 5.0 %collective-permute-start.13 = (bf16[96,768]{1,0:T(8,128)(2,1)S(1)}, bf16[96,768]{1,0:T(8,128)(2,1)S(1)}, u32[]{:S(2)}, u32[]{:S(2)}) collective-permute-start(bf16[96,768]{1,0:T(8,128)(2,1)S(1)} %collective-permute-done.5.refs_9_), channel_id=1, source_target_pairs={{0,2},{2,0},{4,6},{6,4},{1,3},{3,1},{5,7},{7,5},{8,10},{10,8},{12,... | collective-permute-start | bytes 442376 | tf_op jit(solution)/shard_map/ppermute | solution.py:27
  27.1 2.5 %collective-permute-start.6 = (bf16[112,768]{1,0:T(8,128)(2,1)S(1)}, bf16[112,768]{1,0:T(8,128)(2,1)S(1)}, u32[]{:S(2)}, u32[]{:S(2)}) collective-permute-start(bf16[112,768]{1,0:T(8,128)(2,1)S(1)} %collective-permute-done.4.refs_7_), channel_id=1, source_target_pairs={{0,2},{2,0},{4,6},{6,4},{1,3},{3,1},{5,7},{7,5},{8,10},{10,8},{12,... | collective-permute-start | bytes 516104 | tf_op jit(solution)/shard_map/ppermute | solution.py:27
  28.3 6.3 %collective-permute-start.9 = (bf16[96,768]{1,0:T(8,128)(2,1)S(1)}, bf16[96,768]{1,0:T(8,128)(2,1)S(1)}, u32[]{:S(2)}, u32[]{:S(2)}) collective-permute-start(bf16[96,768]{1,0:T(8,128)(2,1)S(1)} %collective-permute-done.7.refs_9_), channel_id=1, source_target_pairs={{0,4},{2,6},{4,0},{6,2},{1,5},{3,7},{5,1},{7,3},{8,12},{10,14},{12... | collective-permute-start | bytes 442376 | tf_op jit(solution)/shard_map/ppermute | solution.py:27
  34.6 2.8 %collective-permute-start.8 = (bf16[96,768]{1,0:T(8,128)(2,1)S(1)}, bf16[96,768]{1,0:T(8,128)(2,1)S(1)}, u32[]{:S(2)}, u32[]{:S(2)}) collective-permute-start(bf16[96,768]{1,0:T(8,128)(2,1)S(1)} %collective-permute-done.7.refs_9_), channel_id=1, source_target_pairs={{0,2},{2,0},{4,6},{6,4},{1,3},{3,1},{5,7},{7,5},{8,10},{10,8},{12,... | collective-permute-start | bytes 442376 | tf_op jit(solution)/shard_map/ppermute | solution.py:27
  35.1 5.2 %collective-permute-start.24 = (bf16[48,3072]{1,0:T(8,128)(2,1)S(1)}, bf16[48,3072]{1,0:T(8,128)(2,1)S(1)}, u32[]{:S(2)}, u32[]{:S(2)}) collective-permute-start(bf16[48,3072]{1,0:T(8,128)(2,1)S(1)} %get-tuple-element.48), channel_id=1, source_target_pairs={{0,2},{2,0},{4,6},{6,4},{1,3},{3,1},{5,7},{7,5},{8,10},{10,8},{12,... | collective-permute-start | bytes 884744 | tf_op jit(solution)/shard_map/ppermute | solution.py:27
  36.2 6.0 %collective-permute-start.19 = (bf16[24,3072]{1,0:T(8,128)(2,1)S(1)}, bf16[24,3072]{1,0:T(8,128)(2,1)S(1)}, u32[]{:S(2)}, u32[]{:S(2)}) collective-permute-start(bf16[24,3072]{1,0:T(8,128)(2,1)S(1)} %slice.65), channel_id=1, source_target_pairs={{0,4},{2,6},{4,0},{6,2},{1,5},{3,7},{5,1},{7,3},{8,12},{10,14},{12... | collective-permute-start | bytes 442376 | tf_op jit(solution)/shard_map/ppermute | solution.py:27
  40.2 4.0 %collective-permute-start.21 = (bf16[48,3072]{1,0:T(8,128)(2,1)S(1)}, bf16[48,3072]{1,0:T(8,128)(2,1)S(1)}, u32[]{:S(2)}, u32[]{:S(2)}) collective-permute-start(bf16[48,3072]{1,0:T(8,128)(2,1)S(1)} %get-tuple-element.45), channel_id=1, source_target_pairs={{0,2},{2,0},{4,6},{6,4},{1,3},{3,1},{5,7},{7,5},{8,10},{10,8},{12,... | collective-permute-start | bytes 884744 | tf_op jit(solution)/shard_map/ppermute | solution.py:27
  40.3 6.0 %collective-permute-start.27 = (bf16[48,3072]{1,0:T(8,128)(2,1)S(1)}, bf16[48,3072]{1,0:T(8,128)(2,1)S(1)}, u32[]{:S(2)}, u32[]{:S(2)}) collective-permute-start(bf16[48,3072]{1,0:T(8,128)(2,1)S(1)} %get-tuple-element.51), channel_id=1, source_target_pairs={{0,2},{2,0},{4,6},{6,4},{1,3},{3,1},{5,7},{7,5},{8,10},{10,8},{12,... | collective-permute-start | bytes 884744 | tf_op jit(solution)/shard_map/ppermute | solution.py:27
  42.2 12.3 %collective-permute-start.20 = (bf16[24,3072]{1,0:T(8,128)(2,1)S(1)}, bf16[24,3072]{1,0:T(8,128)(2,1)S(1)}, u32[]{:S(2)}, u32[]{:S(2)}) collective-permute-start(bf16[24,3072]{1,0:T(8,128)(2,1)S(1)} %fusion.4), channel_id=1, source_target_pairs={{0,24},{8,16},{16,8},{24,0},{1,25},{9,17},{17,9},{25,1},{2,26},{10... | collective-permute-start | bytes 442376 | tf_op jit(solution)/shard_map/ppermute | solution.py:27
  44.3 6.4 %collective-permute-start.22 = (bf16[24,3072]{1,0:T(8,128)(2,1)S(1)}, bf16[24,3072]{1,0:T(8,128)(2,1)S(1)}, u32[]{:S(2)}, u32[]{:S(2)}) collective-permute-start(bf16[24,3072]{1,0:T(8,128)(2,1)S(1)} %slice.64), channel_id=1, source_target_pairs={{0,4},{2,6},{4,0},{6,2},{1,5},{3,7},{5,1},{7,3},{8,12},{10,14},{12... | collective-permute-start | bytes 442376 | tf_op jit(solution)/shard_map/ppermute | solution.py:27
  45.9 6.3 %collective-permute-start.25 = (bf16[24,3072]{1,0:T(8,128)(2,1)S(1)}, bf16[24,3072]{1,0:T(8,128)(2,1)S(1)}, u32[]{:S(2)}, u32[]{:S(2)}) collective-permute-start(bf16[24,3072]{1,0:T(8,128)(2,1)S(1)} %slice.63), channel_id=1, source_target_pairs={{0,4},{2,6},{4,0},{6,2},{1,5},{3,7},{5,1},{7,3},{8,12},{10,14},{12... | collective-permute-start | bytes 442376 | tf_op jit(solution)/shard_map/ppermute | solution.py:27
  50.7 7.4 %collective-permute-start.23 = (bf16[24,3072]{1,0:T(8,128)(2,1)S(1)}, bf16[24,3072]{1,0:T(8,128)(2,1)S(1)}, u32[]{:S(2)}, u32[]{:S(2)}) collective-permute-start(bf16[24,3072]{1,0:T(8,128)(2,1)S(1)} %fusion.3), channel_id=1, source_target_pairs={{0,16},{8,24},{16,0},{24,8},{1,17},{9,25},{17,1},{25,9},{2,18},{10... | collective-permute-start | bytes 442376 | tf_op jit(solution)/shard_map/ppermute | solution.py:27
  52.3 6.4 %collective-permute-start.26 = (bf16[24,3072]{1,0:T(8,128)(2,1)S(1)}, bf16[24,3072]{1,0:T(8,128)(2,1)S(1)}, u32[]{:S(2)}, u32[]{:S(2)}) collective-permute-start(bf16[24,3072]{1,0:T(8,128)(2,1)S(1)} %fusion.2), channel_id=1, source_target_pairs={{0,8},{8,0},{16,24},{24,16},{1,9},{9,1},{17,25},{25,17},{2,10},{10... | collective-permute-start | bytes 442376 | tf_op jit(solution)/shard_map/ppermute | solution.py:27
  53.4 5.3 %collective-permute-start.28 = (bf16[24,3072]{1,0:T(8,128)(2,1)S(1)}, bf16[24,3072]{1,0:T(8,128)(2,1)S(1)}, u32[]{:S(2)}, u32[]{:S(2)}) collective-permute-start(bf16[24,3072]{1,0:T(8,128)(2,1)S(1)} %slice.62), channel_id=1, source_target_pairs={{0,4},{2,6},{4,0},{6,2},{1,5},{3,7},{5,1},{7,3},{8,12},{10,14},{12... | collective-permute-start | bytes 442376 | tf_op jit(solution)/shard_map/ppermute | solution.py:27
  (6 other events, 18.7 us)

commit v7 on v6

--- a/solution.py
+++ b/solution.py
@@ -14,7 +14,7 @@
 
 GROUPS = [[3, 1], [2, 0]]
 SEQUENCE = ['z3', 'z1', 'z2', 'd0', 'x3', 'd3', 'x1', 'd1', 'x2', 'd2', 'e1', 'e2', 'x0', 'e0', 'e3', 'g0', 'r3', 'r1', 'g1', 'r2', 'y1', 'r0', 'y3', 'w3', 'y2', 'w2', 'w1', 'y0']
-WAITS = {'d3': ('z1',), 'e0': ('z3',), 'e2': ('x3',), 'g1': ('r3',), 'r1': ('x2',), 'r3': ('x2',), 'y0': ('y2',), 'y1': ('r2',)}
+WAITS = {'d3': ('z1',), 'e0': ('z3',), 'e2': ('x3',), 'g1': ('r3',), 'r3': ('x2',), 'y0': ('y2',), 'y1': ('r2',)}
 
 
 def shifted(x, axis, by):

time: 59.8 us -> 59.8 us (level)
  no operation moved by 1% of the time
where the time goes in v7:
time: 59.8 us; the launch traced here: 59.5 us
  starting transfers between devices  24.9 us (42%)
  waiting for transfers between devices  23.5 us (39%)
  Pallas kernels  8.81 us (15%)
  other arithmetic  2.05 us (3%)
    ppermute x29, starting transfers between devices, flipped(): lax.ppermute(x, axis, [(i, i ^ by) for i in range(lax.axis_size(axis))])  24.9 us
    ppermute x29, waiting for transfers between devices, flipped(): lax.ppermute(x, axis, [(i, i ^ by) for i in range(lax.axis_size(axis))])  23.5 us
    pallas_call x2, Pallas kernels, experts(): pl.pallas_call(functools.partial(experts_kernel, seq_count, group, order)...  5.59 us
    pallas_call x1, Pallas kernels, gathered_shards(): pl.pallas_call(near_kernel, out_shape=pltpu.VMEM((3, part_width, hidden_w...  1.64 us
  transfers between devices with their start and end apart: 29, of which 14 were waited for; matrix products, arithmetic and copies ran while one was open for 2% of the time, Pallas kernels for 12%

profile of v7, /device:TPU:0, one launch (start us, length us, event | category | flops | bytes accessed | tf_op | source)
XLA Modules:
  0.0 59.5 jit_solution(2387080818901722208)
XLA Ops:
  0.8 3.1 %collective-permute-start = (bf16[208,128]{1,0:T(8,128)(2,1)S(1)}, bf16[208,128]{1,0:T(8,128)(2,1)S(1)}, u32[]{:S(2)}, u32[]{:S(2)}) collective-permute-start(bf16[208,128]{1,0:T(8,128)(2,1)S(1)} %pack.1.refs_3_), channel_id=1, source_target_pairs={{0,8},{8,0},{16,24},{24,16},{1,9},{9,1},{17,25},{25,17},{2,10},{10... | collective-permute-start | bytes 159752 | tf_op jit(solution)/shard_map/ppermute | solution.py:27
  3.9 2.6 %collective-permute-start.1 = (bf16[208,128]{1,0:T(8,128)(2,1)S(1)}, bf16[208,128]{1,0:T(8,128)(2,1)S(1)}, u32[]{:S(2)}, u32[]{:S(2)}) collective-permute-start(bf16[208,128]{1,0:T(8,128)(2,1)S(1)} %pack.1.refs_3_), channel_id=1, source_target_pairs={{0,16},{8,24},{16,0},{24,8},{1,17},{9,25},{17,1},{25,9},{2,18},{10... | collective-permute-start | bytes 159752 | tf_op jit(solution)/shard_map/ppermute | solution.py:27
  6.5 0.9 %broadcast_multiply_fusion.refs_1_ = bf16[6,96,128]{2,1,0:T(8,128)(2,1)S(1)} fusion(bf16[6,96,128]{2,1,0:T(8,128)(2,1)} %bitcast.13), kind=kLoop, calls=%fused_computation.18 | loop fusion | flops 73728 | bytes 294912 | tf_op jit(solution)/shard_map/mul | solution.py:374
  7.5 1.6 %near.1.refs_4_ = bf16[3,768,512]{2,1,0:T(8,128)(2,1)S(1)} custom-call(s32[1]{0:T(128)} %bitcast.place_ref.refs_0_, bf16[1,3072,512]{2,1,0:T(8,128)(2,1)} %refs_2_.3), custom_call_target="tpu_custom_call" | custom-call | tf_op jit(solution)/shard_map/near/pallas_call | solution.py:376
  10.0 2.5 %collective-permute-done.2.refs_6_ = bf16[208,128]{1,0:T(8,128)(2,1)S(1)} collective-permute-done((bf16[208,128]{1,0:T(8,128)(2,1)S(1)}, bf16[208,128]{1,0:T(8,128)(2,1)S(1)}, u32[]{:S(2)}, u32[]{:S(2)}) %collective-permute-start.2) | collective-permute-done | bytes 53280 | tf_op jit(solution)/shard_map/ppermute | solution.py:27
  13.2 1.1 %collective-permute-start.5 = (bf16[96,768]{1,0:T(8,128)(2,1)S(1)}, bf16[96,768]{1,0:T(8,128)(2,1)S(1)}, u32[]{:S(2)}, u32[]{:S(2)}) collective-permute-start(bf16[96,768]{1,0:T(8,128)(2,1)S(1)} %get-tuple-element.34), channel_id=1, source_target_pairs={{0,24},{8,16},{16,8},{24,0},{1,25},{9,17},{17,9},{25,1},{2,26},{10... | collective-permute-start | bytes 442376 | tf_op jit(solution)/shard_map/ppermute | solution.py:27
  14.5 1.5 %collective-permute-start.4 = (bf16[112,768]{1,0:T(8,128)(2,1)S(1)}, bf16[112,768]{1,0:T(8,128)(2,1)S(1)}, u32[]{:S(2)}, u32[]{:S(2)}) collective-permute-start(bf16[112,768]{1,0:T(8,128)(2,1)S(1)} %get-tuple-element.33.refs_5_), channel_id=1, source_target_pairs={{0,4},{2,6},{4,0},{6,2},{1,5},{3,7},{5,1},{7,3},{8,12},{10,14},{12... | collective-permute-start | bytes 516104 | tf_op jit(solution)/shard_map/ppermute | solution.py:27
  16.0 3.2 %collective-permute-start.7 = (bf16[96,768]{1,0:T(8,128)(2,1)S(1)}, bf16[96,768]{1,0:T(8,128)(2,1)S(1)}, u32[]{:S(2)}, u32[]{:S(2)}) collective-permute-start(bf16[96,768]{1,0:T(8,128)(2,1)S(1)} %get-tuple-element.34), channel_id=1, source_target_pairs={{0,16},{8,24},{16,0},{24,8},{1,17},{9,25},{17,1},{25,9},{2,18},{10... | collective-permute-start | bytes 442376 | tf_op jit(solution)/shard_map/ppermute | solution.py:27
  19.2 1.6 %collective-permute-done.5.refs_9_ = bf16[96,768]{1,0:T(8,128)(2,1)S(1)} collective-permute-done((bf16[96,768]{1,0:T(8,128)(2,1)S(1)}, bf16[96,768]{1,0:T(8,128)(2,1)S(1)}, u32[]{:S(2)}, u32[]{:S(2)}) %collective-permute-start.5) | collective-permute-done | bytes 147488 | tf_op jit(solution)/shard_map/ppermute | solution.py:27
  20.8 1.8 %collective-permute-start.10 = (bf16[96,768]{1,0:T(8,128)(2,1)S(1)}, bf16[96,768]{1,0:T(8,128)(2,1)S(1)}, u32[]{:S(2)}, u32[]{:S(2)}) collective-permute-start(bf16[96,768]{1,0:T(8,128)(2,1)S(1)} %collective-permute-done.5.refs_9_), channel_id=1, source_target_pairs={{0,4},{2,6},{4,0},{6,2},{1,5},{3,7},{5,1},{7,3},{8,12},{10,14},{12... | collective-permute-start | bytes 442376 | tf_op jit(solution)/shard_map/ppermute | solution.py:27
  23.3 3.7 %collective-permute-done.7.refs_9_ = bf16[96,768]{1,0:T(8,128)(2,1)S(1)} collective-permute-done((bf16[96,768]{1,0:T(8,128)(2,1)S(1)}, bf16[96,768]{1,0:T(8,128)(2,1)S(1)}, u32[]{:S(2)}, u32[]{:S(2)}) %collective-permute-start.7) | collective-permute-done | bytes 147488 | tf_op jit(solution)/shard_map/ppermute | solution.py:27
  28.3 1.2 %collective-permute-start.9 = (bf16[96,768]{1,0:T(8,128)(2,1)S(1)}, bf16[96,768]{1,0:T(8,128)(2,1)S(1)}, u32[]{:S(2)}, u32[]{:S(2)}) collective-permute-start(bf16[96,768]{1,0:T(8,128)(2,1)S(1)} %collective-permute-done.7.refs_9_), channel_id=1, source_target_pairs={{0,4},{2,6},{4,0},{6,2},{1,5},{3,7},{5,1},{7,3},{8,12},{10,14},{12... | collective-permute-start | bytes 442376 | tf_op jit(solution)/shard_map/ppermute | solution.py:27
  29.7 2.8 %experts.2 = (bf16[48,3072]{1,0:T(8,128)(2,1)S(1)}, bf16[48,3072]{1,0:T(8,128)(2,1)S(1)}, bf16[48,3072]{1,0:T(8,128)(2,1)S(1)}, bf16[48,3072]{1,0:T(8,128)(2,1)S(1)}) custom-call(s32[1]{0:T(128)} %bitcast.place_ref.refs_0_, f32[4,1,768]{2,1,0:T(1,128)} %bitcast.14, bf16[1,3072,512]{2,1,0:T(8,128)(2,1)} %refs_2_.3, bf16[1,512,3072]{2,1,0:T(8,128)(2,1)} %refs_3_.3, ...), custom_call_target="tpu_custom_call" | custom-call | flops 1207959552 | bytes 8388608 | tf_op jit(solution)/shard_map/experts/pallas_call | solution.py:433
  32.5 2.1 %collective-permute-done.9.refs_11_ = bf16[96,768]{1,0:T(8,128)(2,1)S(1)} collective-permute-done((bf16[96,768]{1,0:T(8,128)(2,1)S(1)}, bf16[96,768]{1,0:T(8,128)(2,1)S(1)}, u32[]{:S(2)}, u32[]{:S(2)}) %collective-permute-start.9) | collective-permute-done | bytes 147488 | tf_op jit(solution)/shard_map/ppermute | solution.py:27
  36.2 1.1 %collective-permute-start.19 = (bf16[24,3072]{1,0:T(8,128)(2,1)S(1)}, bf16[24,3072]{1,0:T(8,128)(2,1)S(1)}, u32[]{:S(2)}, u32[]{:S(2)}) collective-permute-start(bf16[24,3072]{1,0:T(8,128)(2,1)S(1)} %slice.65), channel_id=1, source_target_pairs={{0,4},{2,6},{4,0},{6,2},{1,5},{3,7},{5,1},{7,3},{8,12},{10,14},{12... | collective-permute-start | bytes 442376 | tf_op jit(solution)/shard_map/ppermute | solution.py:27
  37.4 2.8 %experts.3 = (bf16[48,3072]{1,0:T(8,128)(2,1)S(1)}, bf16[48,3072]{1,0:T(8,128)(2,1)S(1)}, bf16[48,3072]{1,0:T(8,128)(2,1)S(1)}, bf16[48,3072]{1,0:T(8,128)(2,1)S(1)}, bf16[4,24,768]{2,1,0:T(8,128)(2,1)S(1)}) custom-call(s32[1]{0:T(128)} %bitcast.place_ref.refs_0_, f32[4,1,768]{2,1,0:T(1,128)} %bitcast.15, bf16[1,3072,512]{2,1,0:T(8,128)(2,1)} %refs_2_.3, ...), custom_call_target="tpu_custom_call" | custom-call | flops 1207959552 | bytes 8388608 | tf_op jit(solution)/shard_map/experts/pallas_call | solution.py:433
  40.9 1.3 %collective-permute-done.19 = bf16[24,3072]{1,0:T(8,128)(2,1)S(1)} collective-permute-done((bf16[24,3072]{1,0:T(8,128)(2,1)S(1)}, bf16[24,3072]{1,0:T(8,128)(2,1)S(1)}, u32[]{:S(2)}, u32[]{:S(2)}) %collective-permute-start.19) | collective-permute-done | bytes 147488 | tf_op jit(solution)/shard_map/ppermute | solution.py:27
  42.2 1.9 %collective-permute-start.20 = (bf16[24,3072]{1,0:T(8,128)(2,1)S(1)}, bf16[24,3072]{1,0:T(8,128)(2,1)S(1)}, u32[]{:S(2)}, u32[]{:S(2)}) collective-permute-start(bf16[24,3072]{1,0:T(8,128)(2,1)S(1)} %fusion.4), channel_id=1, source_target_pairs={{0,24},{8,16},{16,8},{24,0},{1,25},{9,17},{17,9},{25,1},{2,26},{10... | collective-permute-start | bytes 442376 | tf_op jit(solution)/shard_map/ppermute | solution.py:27
  44.3 1.7 %collective-permute-start.22 = (bf16[24,3072]{1,0:T(8,128)(2,1)S(1)}, bf16[24,3072]{1,0:T(8,128)(2,1)S(1)}, u32[]{:S(2)}, u32[]{:S(2)}) collective-permute-start(bf16[24,3072]{1,0:T(8,128)(2,1)S(1)} %slice.64), channel_id=1, source_target_pairs={{0,4},{2,6},{4,0},{6,2},{1,5},{3,7},{5,1},{7,3},{8,12},{10,14},{12... | collective-permute-start | bytes 442376 | tf_op jit(solution)/shard_map/ppermute | solution.py:27
  46.5 4.2 %collective-permute-done.22 = bf16[24,3072]{1,0:T(8,128)(2,1)S(1)} collective-permute-done((bf16[24,3072]{1,0:T(8,128)(2,1)S(1)}, bf16[24,3072]{1,0:T(8,128)(2,1)S(1)}, u32[]{:S(2)}, u32[]{:S(2)}) %collective-permute-start.22) | collective-permute-done | bytes 147488 | tf_op jit(solution)/shard_map/ppermute | solution.py:27
  50.8 1.5 %collective-permute-done.25 = bf16[24,3072]{1,0:T(8,128)(2,1)S(1)} collective-permute-done((bf16[24,3072]{1,0:T(8,128)(2,1)S(1)}, bf16[24,3072]{1,0:T(8,128)(2,1)S(1)}, u32[]{:S(2)}, u32[]{:S(2)}) %collective-permute-start.25) | collective-permute-done | bytes 147488 | tf_op jit(solution)/shard_map/ppermute | solution.py:27
  52.3 1.1 %collective-permute-start.26 = (bf16[24,3072]{1,0:T(8,128)(2,1)S(1)}, bf16[24,3072]{1,0:T(8,128)(2,1)S(1)}, u32[]{:S(2)}, u32[]{:S(2)}) collective-permute-start(bf16[24,3072]{1,0:T(8,128)(2,1)S(1)} %fusion.2), channel_id=1, source_target_pairs={{0,8},{8,0},{16,24},{24,16},{1,9},{9,1},{17,25},{25,17},{2,10},{10... | collective-permute-start | bytes 442376 | tf_op jit(solution)/shard_map/ppermute | solution.py:27
  53.4 1.0 %collective-permute-start.28 = (bf16[24,3072]{1,0:T(8,128)(2,1)S(1)}, bf16[24,3072]{1,0:T(8,128)(2,1)S(1)}, u32[]{:S(2)}, u32[]{:S(2)}) collective-permute-start(bf16[24,3072]{1,0:T(8,128)(2,1)S(1)} %slice.62), channel_id=1, source_target_pairs={{0,4},{2,6},{4,0},{6,2},{1,5},{3,7},{5,1},{7,3},{8,12},{10,14},{12... | collective-permute-start | bytes 442376 | tf_op jit(solution)/shard_map/ppermute | solution.py:27
  54.5 3.6 %collective-permute-done.23 = bf16[24,3072]{1,0:T(8,128)(2,1)S(1)} collective-permute-done((bf16[24,3072]{1,0:T(8,128)(2,1)S(1)}, bf16[24,3072]{1,0:T(8,128)(2,1)S(1)}, u32[]{:S(2)}, u32[]{:S(2)}) %collective-permute-start.23) | collective-permute-done | bytes 147488 | tf_op jit(solution)/shard_map/ppermute | solution.py:27
  (57 shorter events, 9.3 us)
Async XLA Ops:
  0.8 8.3 %collective-permute-start = (bf16[208,128]{1,0:T(8,128)(2,1)S(1)}, bf16[208,128]{1,0:T(8,128)(2,1)S(1)}, u32[]{:S(2)}, u32[]{:S(2)}) collective-permute-start(bf16[208,128]{1,0:T(8,128)(2,1)S(1)} %pack.1.refs_3_), channel_id=1, source_target_pairs={{0,8},{8,0},{16,24},{24,16},{1,9},{9,1},{17,25},{25,17},{2,10},{10... | collective-permute-start | bytes 159752 | tf_op jit(solution)/shard_map/ppermute | solution.py:27
  3.9 6.1 %collective-permute-start.1 = (bf16[208,128]{1,0:T(8,128)(2,1)S(1)}, bf16[208,128]{1,0:T(8,128)(2,1)S(1)}, u32[]{:S(2)}, u32[]{:S(2)}) collective-permute-start(bf16[208,128]{1,0:T(8,128)(2,1)S(1)} %pack.1.refs_3_), channel_id=1, source_target_pairs={{0,16},{8,24},{16,0},{24,8},{1,17},{9,25},{17,1},{25,9},{2,18},{10... | collective-permute-start | bytes 159752 | tf_op jit(solution)/shard_map/ppermute | solution.py:27
  6.5 5.9 %collective-permute-start.2 = (bf16[208,128]{1,0:T(8,128)(2,1)S(1)}, bf16[208,128]{1,0:T(8,128)(2,1)S(1)}, u32[]{:S(2)}, u32[]{:S(2)}) collective-permute-start(bf16[208,128]{1,0:T(8,128)(2,1)S(1)} %pack.1.refs_3_), channel_id=1, source_target_pairs={{0,24},{8,16},{16,8},{24,0},{1,25},{9,17},{17,9},{25,1},{2,26},{10... | collective-permute-start | bytes 159752 | tf_op jit(solution)/shard_map/ppermute | solution.py:27
  13.2 7.6 %collective-permute-start.5 = (bf16[96,768]{1,0:T(8,128)(2,1)S(1)}, bf16[96,768]{1,0:T(8,128)(2,1)S(1)}, u32[]{:S(2)}, u32[]{:S(2)}) collective-permute-start(bf16[96,768]{1,0:T(8,128)(2,1)S(1)} %get-tuple-element.34), channel_id=1, source_target_pairs={{0,24},{8,16},{16,8},{24,0},{1,25},{9,17},{17,9},{25,1},{2,26},{10... | collective-permute-start | bytes 442376 | tf_op jit(solution)/shard_map/ppermute | solution.py:27
  14.3 8.4 %collective-permute-start.12 = (bf16[96,768]{1,0:T(8,128)(2,1)S(1)}, bf16[96,768]{1,0:T(8,128)(2,1)S(1)}, u32[]{:S(2)}, u32[]{:S(2)}) collective-permute-start(bf16[96,768]{1,0:T(8,128)(2,1)S(1)} %get-tuple-element.34), channel_id=1, source_target_pairs={{0,8},{8,0},{16,24},{24,16},{1,9},{9,1},{17,25},{25,17},{2,10},{10... | collective-permute-start | bytes 442376 | tf_op jit(solution)/shard_map/ppermute | solution.py:27
  14.5 8.8 %collective-permute-start.4 = (bf16[112,768]{1,0:T(8,128)(2,1)S(1)}, bf16[112,768]{1,0:T(8,128)(2,1)S(1)}, u32[]{:S(2)}, u32[]{:S(2)}) collective-permute-start(bf16[112,768]{1,0:T(8,128)(2,1)S(1)} %get-tuple-element.33.refs_5_), channel_id=1, source_target_pairs={{0,4},{2,6},{4,0},{6,2},{1,5},{3,7},{5,1},{7,3},{8,12},{10,14},{12... | collective-permute-start | bytes 516104 | tf_op jit(solution)/shard_map/ppermute | solution.py:27
  16.0 11.2 %collective-permute-start.3 = (bf16[112,768]{1,0:T(8,128)(2,1)S(1)}, bf16[112,768]{1,0:T(8,128)(2,1)S(1)}, u32[]{:S(2)}, u32[]{:S(2)}) collective-permute-start(bf16[112,768]{1,0:T(8,128)(2,1)S(1)} %get-tuple-element.33.refs_5_), channel_id=1, source_target_pairs={{0,2},{2,0},{4,6},{6,4},{1,3},{3,1},{5,7},{7,5},{8,10},{10,8},{12,... | collective-permute-start | bytes 516104 | tf_op jit(solution)/shard_map/ppermute | solution.py:27
  16.0 11.0 %collective-permute-start.7 = (bf16[96,768]{1,0:T(8,128)(2,1)S(1)}, bf16[96,768]{1,0:T(8,128)(2,1)S(1)}, u32[]{:S(2)}, u32[]{:S(2)}) collective-permute-start(bf16[96,768]{1,0:T(8,128)(2,1)S(1)} %get-tuple-element.34), channel_id=1, source_target_pairs={{0,16},{8,24},{16,0},{24,8},{1,17},{9,25},{17,1},{25,9},{2,18},{10... | collective-permute-start | bytes 442376 | tf_op jit(solution)/shard_map/ppermute | solution.py:27
  20.8 6.8 %collective-permute-start.10 = (bf16[96,768]{1,0:T(8,128)(2,1)S(1)}, bf16[96,768]{1,0:T(8,128)(2,1)S(1)}, u32[]{:S(2)}, u32[]{:S(2)}) collective-permute-start(bf16[96,768]{1,0:T(8,128)(2,1)S(1)} %collective-permute-done.5.refs_9_), channel_id=1, source_target_pairs={{0,4},{2,6},{4,0},{6,2},{1,5},{3,7},{5,1},{7,3},{8,12},{10,14},{12... | collective-permute-start | bytes 442376 | tf_op jit(solution)/shard_map/ppermute | solution.py:27
  22.7 5.6 %collective-permute-start.16 = (bf16[96,768]{1,0:T(8,128)(2,1)S(1)}, bf16[96,768]{1,0:T(8,128)(2,1)S(1)}, u32[]{:S(2)}, u32[]{:S(2)}) collective-permute-start(bf16[96,768]{1,0:T(8,128)(2,1)S(1)} %collective-permute-done.12.refs_13_), channel_id=1, source_target_pairs={{0,4},{2,6},{4,0},{6,2},{1,5},{3,7},{5,1},{7,3},{8,12},{10,14},{12... | collective-permute-start | bytes 442376 | tf_op jit(solution)/shard_map/ppermute | solution.py:27
  23.3 5.0 %collective-permute-start.13 = (bf16[96,768]{1,0:T(8,128)(2,1)S(1)}, bf16[96,768]{1,0:T(8,128)(2,1)S(1)}, u32[]{:S(2)}, u32[]{:S(2)}) collective-permute-start(bf16[96,768]{1,0:T(8,128)(2,1)S(1)} %collective-permute-done.5.refs_9_), channel_id=1, source_target_pairs={{0,2},{2,0},{4,6},{6,4},{1,3},{3,1},{5,7},{7,5},{8,10},{10,8},{12,... | collective-permute-start | bytes 442376 | tf_op jit(solution)/shard_map/ppermute | solution.py:27
  27.1 2.5 %collective-permute-start.6 = (bf16[112,768]{1,0:T(8,128)(2,1)S(1)}, bf16[112,768]{1,0:T(8,128)(2,1)S(1)}, u32[]{:S(2)}, u32[]{:S(2)}) collective-permute-start(bf16[112,768]{1,0:T(8,128)(2,1)S(1)} %collective-permute-done.4.refs_7_), channel_id=1, source_target_pairs={{0,2},{2,0},{4,6},{6,4},{1,3},{3,1},{5,7},{7,5},{8,10},{10,8},{12,... | collective-permute-start | bytes 516104 | tf_op jit(solution)/shard_map/ppermute | solution.py:27
  28.3 6.3 %collective-permute-start.9 = (bf16[96,768]{1,0:T(8,128)(2,1)S(1)}, bf16[96,768]{1,0:T(8,128)(2,1)S(1)}, u32[]{:S(2)}, u32[]{:S(2)}) collective-permute-start(bf16[96,768]{1,0:T(8,128)(2,1)S(1)} %collective-permute-done.7.refs_9_), channel_id=1, source_target_pairs={{0,4},{2,6},{4,0},{6,2},{1,5},{3,7},{5,1},{7,3},{8,12},{10,14},{12... | collective-permute-start | bytes 442376 | tf_op jit(solution)/shard_map/ppermute | solution.py:27
  34.6 2.8 %collective-permute-start.8 = (bf16[96,768]{1,0:T(8,128)(2,1)S(1)}, bf16[96,768]{1,0:T(8,128)(2,1)S(1)}, u32[]{:S(2)}, u32[]{:S(2)}) collective-permute-start(bf16[96,768]{1,0:T(8,128)(2,1)S(1)} %collective-permute-done.7.refs_9_), channel_id=1, source_target_pairs={{0,2},{2,0},{4,6},{6,4},{1,3},{3,1},{5,7},{7,5},{8,10},{10,8},{12,... | collective-permute-start | bytes 442376 | tf_op jit(solution)/shard_map/ppermute | solution.py:27
  35.1 5.2 %collective-permute-start.24 = (bf16[48,3072]{1,0:T(8,128)(2,1)S(1)}, bf16[48,3072]{1,0:T(8,128)(2,1)S(1)}, u32[]{:S(2)}, u32[]{:S(2)}) collective-permute-start(bf16[48,3072]{1,0:T(8,128)(2,1)S(1)} %get-tuple-element.46), channel_id=1, source_target_pairs={{0,2},{2,0},{4,6},{6,4},{1,3},{3,1},{5,7},{7,5},{8,10},{10,8},{12,... | collective-permute-start | bytes 884744 | tf_op jit(solution)/shard_map/ppermute | solution.py:27
  36.2 6.0 %collective-permute-start.19 = (bf16[24,3072]{1,0:T(8,128)(2,1)S(1)}, bf16[24,3072]{1,0:T(8,128)(2,1)S(1)}, u32[]{:S(2)}, u32[]{:S(2)}) collective-permute-start(bf16[24,3072]{1,0:T(8,128)(2,1)S(1)} %slice.65), channel_id=1, source_target_pairs={{0,4},{2,6},{4,0},{6,2},{1,5},{3,7},{5,1},{7,3},{8,12},{10,14},{12... | collective-permute-start | bytes 442376 | tf_op jit(solution)/shard_map/ppermute | solution.py:27
  40.2 4.0 %collective-permute-start.21 = (bf16[48,3072]{1,0:T(8,128)(2,1)S(1)}, bf16[48,3072]{1,0:T(8,128)(2,1)S(1)}, u32[]{:S(2)}, u32[]{:S(2)}) collective-permute-start(bf16[48,3072]{1,0:T(8,128)(2,1)S(1)} %get-tuple-element.44), channel_id=1, source_target_pairs={{0,2},{2,0},{4,6},{6,4},{1,3},{3,1},{5,7},{7,5},{8,10},{10,8},{12,... | collective-permute-start | bytes 884744 | tf_op jit(solution)/shard_map/ppermute | solution.py:27
  40.3 6.0 %collective-permute-start.27 = (bf16[48,3072]{1,0:T(8,128)(2,1)S(1)}, bf16[48,3072]{1,0:T(8,128)(2,1)S(1)}, u32[]{:S(2)}, u32[]{:S(2)}) collective-permute-start(bf16[48,3072]{1,0:T(8,128)(2,1)S(1)} %get-tuple-element.49), channel_id=1, source_target_pairs={{0,2},{2,0},{4,6},{6,4},{1,3},{3,1},{5,7},{7,5},{8,10},{10,8},{12,... | collective-permute-start | bytes 884744 | tf_op jit(solution)/shard_map/ppermute | solution.py:27
  42.2 12.3 %collective-permute-start.20 = (bf16[24,3072]{1,0:T(8,128)(2,1)S(1)}, bf16[24,3072]{1,0:T(8,128)(2,1)S(1)}, u32[]{:S(2)}, u32[]{:S(2)}) collective-permute-start(bf16[24,3072]{1,0:T(8,128)(2,1)S(1)} %fusion.4), channel_id=1, source_target_pairs={{0,24},{8,16},{16,8},{24,0},{1,25},{9,17},{17,9},{25,1},{2,26},{10... | collective-permute-start | bytes 442376 | tf_op jit(solution)/shard_map/ppermute | solution.py:27
  44.3 6.4 %collective-permute-start.22 = (bf16[24,3072]{1,0:T(8,128)(2,1)S(1)}, bf16[24,3072]{1,0:T(8,128)(2,1)S(1)}, u32[]{:S(2)}, u32[]{:S(2)}) collective-permute-start(bf16[24,3072]{1,0:T(8,128)(2,1)S(1)} %slice.64), channel_id=1, source_target_pairs={{0,4},{2,6},{4,0},{6,2},{1,5},{3,7},{5,1},{7,3},{8,12},{10,14},{12... | collective-permute-start | bytes 442376 | tf_op jit(solution)/shard_map/ppermute | solution.py:27
  45.9 6.3 %collective-permute-start.25 = (bf16[24,3072]{1,0:T(8,128)(2,1)S(1)}, bf16[24,3072]{1,0:T(8,128)(2,1)S(1)}, u32[]{:S(2)}, u32[]{:S(2)}) collective-permute-start(bf16[24,3072]{1,0:T(8,128)(2,1)S(1)} %slice.63), channel_id=1, source_target_pairs={{0,4},{2,6},{4,0},{6,2},{1,5},{3,7},{5,1},{7,3},{8,12},{10,14},{12... | collective-permute-start | bytes 442376 | tf_op jit(solution)/shard_map/ppermute | solution.py:27
  50.7 7.4 %collective-permute-start.23 = (bf16[24,3072]{1,0:T(8,128)(2,1)S(1)}, bf16[24,3072]{1,0:T(8,128)(2,1)S(1)}, u32[]{:S(2)}, u32[]{:S(2)}) collective-permute-start(bf16[24,3072]{1,0:T(8,128)(2,1)S(1)} %fusion.3), channel_id=1, source_target_pairs={{0,16},{8,24},{16,0},{24,8},{1,17},{9,25},{17,1},{25,9},{2,18},{10... | collective-permute-start | bytes 442376 | tf_op jit(solution)/shard_map/ppermute | solution.py:27
  52.3 6.4 %collective-permute-start.26 = (bf16[24,3072]{1,0:T(8,128)(2,1)S(1)}, bf16[24,3072]{1,0:T(8,128)(2,1)S(1)}, u32[]{:S(2)}, u32[]{:S(2)}) collective-permute-start(bf16[24,3072]{1,0:T(8,128)(2,1)S(1)} %fusion.2), channel_id=1, source_target_pairs={{0,8},{8,0},{16,24},{24,16},{1,9},{9,1},{17,25},{25,17},{2,10},{10... | collective-permute-start | bytes 442376 | tf_op jit(solution)/shard_map/ppermute | solution.py:27
  53.4 5.3 %collective-permute-start.28 = (bf16[24,3072]{1,0:T(8,128)(2,1)S(1)}, bf16[24,3072]{1,0:T(8,128)(2,1)S(1)}, u32[]{:S(2)}, u32[]{:S(2)}) collective-permute-start(bf16[24,3072]{1,0:T(8,128)(2,1)S(1)} %slice.62), channel_id=1, source_target_pairs={{0,4},{2,6},{4,0},{6,2},{1,5},{3,7},{5,1},{7,3},{8,12},{10,14},{12... | collective-permute-start | bytes 442376 | tf_op jit(solution)/shard_map/ppermute | solution.py:27
  (6 other events, 18.7 us)
